TPU v7x, 256 devices: a whole 4x4x8 slice. The times are simulated.
256 devices in a mesh: rows: 16 (over x, z_hi, core), cols: 16 (over y, z_lo).
Axes of the slice: x: 4, y: 4, z: 8 (z_hi: 2, z_lo: 4; z = z_hi * 4 + z_lo), core: 2. Of those that a mesh axis runs over, the one named last changes fastest.
Arguments:
- elevation: float32 [2048, 16384], P('rows', 'cols'), may hold values from -6 to 6
- data_mask: int32 [2048, 16384], P('rows', 'cols'), may hold values 0 or 1
- tie_order: int32 [8], replicated, may hold values from 0 to 7, each once
Outputs:
- inflow: float32 [2048, 16384], P('rows', 'cols')
Inputs may be any that keep to these rules, and one draw needn't show every extreme that they name: tie_order holds each of 0 to 7 once.
All inputs are finite; a program needn't handle non-finite values. No bound on the sum of `data_mask` on one device may be relied on, other than what follows from the above.
Results may differ from a plain program's by a relative error of at most 0.0003.
Values sent between devices are 32-bit elements; how exact they have to be, the bound alone decides.
No kernel may reach another device: no remote copies, remote signals or barrier semaphores. Data moves between devices by JAX's collectives and lax.ppermute only.
A program may use at most 64 MiB of HBM per device.

v0:
```python
import jax
import jax.numpy as jnp
from jax import lax
from jax.sharding import PartitionSpec as P

ITERS = 8


OFFSETS = ((0, 1), (1, 1), (1, 0), (1, -1), (0, -1), (-1, -1), (-1, 0), (-1, 1))
RECIPROCAL = (
    1.0,
    0.7071067811865476,
    1.0,
    0.7071067811865476,
    1.0,
    0.7071067811865476,
    1.0,
    0.7071067811865476,
)
RETENTION = 0.1


def with_halo(cells, sides, width):
    for axis, dim in sides:
        count = lax.axis_size(axis)
        ends = count - 1
        head = lax.slice_in_dim(cells, 0, width, axis=dim)
        tail = lax.slice_in_dim(cells, cells.shape[dim] - width, cells.shape[dim], axis=dim)
        cells = jnp.concatenate(
            [
                lax.ppermute(tail, axis, [(i, (i + 1) % count) for i in range(ends)]),
                cells,
                lax.ppermute(head, axis, [((i + 1) % count, i) for i in range(ends)]),
            ],
            axis=dim,
        )
    return cells


def priorities(tie_order):
    places = jnp.arange(8, dtype=jnp.float32)
    values = 1.0 + 0.5 * (7.0 - places) / 7.0
    matches = (tie_order[:, None] == jnp.arange(8, dtype=jnp.int32)[None, :]).astype(jnp.float32)
    return jnp.sum(matches * values[:, None], axis=0)


def outflow_weight_matrix(height_pad, valid_pad, ranking_order):
    height = height_pad.shape[0] - 2
    breadth = height_pad.shape[1] - 2
    centre = height_pad[1:-1, 1:-1]
    slopes = []
    for number, (step_row, step_col) in enumerate(OFFSETS):
        beside = height_pad[
            1 + step_row : 1 + step_row + height, 1 + step_col : 1 + step_col + breadth
        ]
        beside_ok = valid_pad[
            1 + step_row : 1 + step_row + height, 1 + step_col : 1 + step_col + breadth
        ]
        slopes.append(
            beside_ok
            * ranking_order[number]
            * jnp.maximum(centre - beside, 0.0)
            * RECIPROCAL[number]
        )
    slopes = jnp.stack(slopes)
    totals = jnp.sum(slopes, axis=0) + RETENTION
    return slopes / totals


def gather_inflow(weights, field_pad):
    height = field_pad.shape[0] - 2
    breadth = field_pad.shape[1] - 2
    summed_in = jnp.zeros((height, breadth), jnp.float32)
    for number, (step_row, step_col) in enumerate(OFFSETS):
        term = weights[number] * field_pad
        summed_in = (
            summed_in
            + term[1 - step_row : 1 - step_row + height, 1 - step_col : 1 - step_col + breadth]
        )
    return summed_in


def edge_valid(position, length, devices, margin):
    places = position * length + jnp.arange(length + 2 * margin, dtype=jnp.int32) - margin
    return ((places >= 0) & (places < length * devices)).astype(jnp.float32)


def trimmed(field, cut):
    return field[..., cut : field.shape[-2] - cut, cut : field.shape[-1] - cut]


def on_device(elevation, data_mask, tie_order):
    ranking_order = priorities(tie_order)
    row_index = lax.axis_index("rows")
    col_index = lax.axis_index("cols")
    row_devices = lax.axis_size("rows")
    col_devices = lax.axis_size("cols")
    tile_rows, tile_cols = elevation.shape
    coarse_rows, coarse_cols = (tile_rows // 8, tile_cols // 8)
    valid_flag = data_mask.astype(jnp.float32)
    summed = (valid_flag * elevation).reshape(coarse_rows, 8, coarse_cols, 8).sum(axis=(1, 3))
    counts = valid_flag.reshape(coarse_rows, 8, coarse_cols, 8).sum(axis=(1, 3))
    overview = summed / (counts + 1.0)
    runoff = counts / 64.0
    elevation_window = with_halo(elevation, (("rows", 0), ("cols", 1)), 2)
    depth = ITERS + 2
    over_win, runoff_win = (
        with_halo(overview, (("rows", 0), ("cols", 1)), depth),
        with_halo(runoff, (("rows", 0), ("cols", 1)), depth),
    )
    window_valid = (
        edge_valid(row_index, coarse_rows, row_devices, depth)[:, None]
        * edge_valid(col_index, coarse_cols, col_devices, depth)[None, :]
    )
    coarse_w = outflow_weight_matrix(over_win, window_valid, ranking_order)
    flow_now = trimmed(runoff_win, 1)
    for sweep in range(ITERS):
        flow_now = trimmed(runoff_win, sweep + 2) + gather_inflow(
            trimmed(coarse_w, sweep), flow_now
        )
        flow_now = flow_now * trimmed(window_valid, sweep + 2)
    upsampled = jnp.repeat(jnp.repeat(flow_now, 8, axis=0), 8, axis=1)
    up_window = upsampled[7 : 7 + tile_rows + 2, 7 : 7 + tile_cols + 2]
    detailed_valid = (
        edge_valid(row_index, tile_rows, row_devices, 2)[:, None]
        * edge_valid(col_index, tile_cols, col_devices, 2)[None, :]
    )
    detailed_weight = outflow_weight_matrix(elevation_window, detailed_valid, ranking_order)
    return valid_flag + gather_inflow(detailed_weight, up_window)


def solution(mesh):
    in_specs = (P("rows", "cols"), P("rows", "cols"), P())
    out_specs = P("rows", "cols")
    return jax.shard_map(
        on_device, mesh=mesh, in_specs=in_specs, out_specs=out_specs, check_vma=False
    )
```

profile of v0, /device:TPU:30, one launch (start us, length us, event | category | flops | bytes accessed | tf_op | source)
XLA Modules:
  0.0 121.7 jit_solution(10839938555065517978)
XLA Ops:
  0.8 1.0 copy.22
  1.9 1.9 %collective-permute-start = (f32[2,1024]{0,1:T(8,128)}, f32[2,1024]{0,1:T(8,128)S(1)}, u32[]{:S(2)}, u32[]{:S(2)}) collective-permute-start(f32[2,1024]{0,1:T(8,128)} %copy.22), channel_id=1, source_target_pairs={{0,16},{16,32},{32,48},{48,64},{64,80},{80,96},{96,112},{112,128},... | collective-permute-start | bytes 24584 | tf_op jit(solution)/shard_map/ppermute | solution.py:31
  4.8 8.8 %collective-permute-start.1 = (f32[2,1024]{0,1:T(8,128)}, f32[2,1024]{0,1:T(8,128)S(1)}, u32[]{:S(2)}, u32[]{:S(2)}) collective-permute-start(f32[2,1024]{0,1:T(8,128)} %copy.23), channel_id=1, source_target_pairs={{16,0},{32,16},{48,32},{64,48},{80,64},{96,80},{112,96},{128,112},... | collective-permute-start | bytes 24584 | tf_op jit(solution)/shard_map/ppermute | solution.py:33
  15.3 6.2 %reshape.122 = f32[16,8,128,8]{3,2,1,0:T(8,128)} reshape(f32[128,1024]{1,0:T(8,128)S(1)} %copy.27) | data formatting | bytes 1048576 | tf_op jit(solution)/shard_map/reshape | solution.py:101
  21.7 6.1 %reshape.121 = f32[16,8,128,8]{3,2,1,0:T(8,128)} reshape(f32[128,1024]{1,0:T(8,128)S(1)} %copy.25) | data formatting | bytes 1048576 | tf_op jit(solution)/shard_map/reshape | solution.py:102
  27.8 4.0 %reduce_sum.100 = f32[16,128]{1,0:T(8,128)S(1)} reduce(f32[16,8,128,8]{3,2,1,0:T(8,128)} %reshape.122, f32[]{:T(128)} %constant.11.clone.1), dimensions={1,3}, to_apply=%region_2.0 | reduce | flops 129024 | bytes 532484 | tf_op jit(solution)/shard_map/reduce_sum | solution.py:101
  31.8 4.0 %reduce_sum.99 = f32[16,128]{1,0:T(8,128)S(1)} reduce(f32[16,8,128,8]{3,2,1,0:T(8,128)} %reshape.121, f32[]{:T(128)} %constant.11.clone.1), dimensions={1,3}, to_apply=%region_1.0 | reduce | flops 129024 | bytes 532484 | tf_op jit(solution)/shard_map/reduce_sum | solution.py:102
  35.9 2.3 %collective-permute-start.8 = (f32[10,128]{1,0:T(8,128)S(1)}, f32[10,128]{1,0:T(8,128)S(1)}, u32[]{:S(2)}, u32[]{:S(2)}) collective-permute-start(f32[10,128]{1,0:T(8,128)S(1)} %get-tuple-element.105), channel_id=1, source_target_pairs={{0,16},{16,32},{32,48},{48,64},{64,80},{80,96},{96,112},{112,128},... | collective-permute-start | bytes 15368 | tf_op jit(solution)/shard_map/ppermute | solution.py:31
  38.2 8.1 %collective-permute-start.9 = (f32[10,128]{1,0:T(8,128)S(1)}, f32[10,128]{1,0:T(8,128)S(1)}, u32[]{:S(2)}, u32[]{:S(2)}) collective-permute-start(f32[10,128]{1,0:T(8,128)S(1)} %get-tuple-element.106), channel_id=1, source_target_pairs={{16,0},{32,16},{48,32},{64,48},{80,64},{96,80},{112,96},{128,112},... | collective-permute-start | bytes 15368 | tf_op jit(solution)/shard_map/ppermute | solution.py:33
  46.3 1.9 %collective-permute-start.4 = (f32[10,128]{1,0:T(8,128)S(1)}, f32[10,128]{1,0:T(8,128)S(1)}, u32[]{:S(2)}, u32[]{:S(2)}) collective-permute-start(f32[10,128]{1,0:T(8,128)S(1)} %get-tuple-element.109), channel_id=1, source_target_pairs={{0,16},{16,32},{32,48},{48,64},{64,80},{80,96},{96,112},{112,128},... | collective-permute-start | bytes 15368 | tf_op jit(solution)/shard_map/ppermute | solution.py:31
  49.4 8.4 %collective-permute-start.5 = (f32[10,128]{1,0:T(8,128)S(1)}, f32[10,128]{1,0:T(8,128)S(1)}, u32[]{:S(2)}, u32[]{:S(2)}) collective-permute-start(f32[10,128]{1,0:T(8,128)S(1)} %get-tuple-element.110), channel_id=1, source_target_pairs={{16,0},{32,16},{48,32},{64,48},{80,64},{96,80},{112,96},{128,112},... | collective-permute-start | bytes 15368 | tf_op jit(solution)/shard_map/ppermute | solution.py:33
  57.9 3.5 %collective-permute-start.10 = (f32[36,10]{1,0:T(8,128)S(1)}, f32[36,10]{1,0:T(8,128)S(1)}, u32[]{:S(2)}, u32[]{:S(2)}) collective-permute-start(f32[36,10]{1,0:T(8,128)S(1)} %get-tuple-element.101), channel_id=1, source_target_pairs={{0,1},{1,2},{2,3},{3,4},{4,5},{5,6},{6,7},{7,8},{8,9},{9,10},{10,1... | collective-permute-start | bytes 4328 | tf_op jit(solution)/shard_map/ppermute | solution.py:31
  61.4 5.1 %collective-permute-start.11 = (f32[36,10]{1,0:T(8,128)S(1)}, f32[36,10]{1,0:T(8,128)S(1)}, u32[]{:S(2)}, u32[]{:S(2)}) collective-permute-start(f32[36,10]{1,0:T(8,128)S(1)} %get-tuple-element.102), channel_id=1, source_target_pairs={{1,0},{2,1},{3,2},{4,3},{5,4},{6,5},{7,6},{8,7},{9,8},{10,9},{11,1... | collective-permute-start | bytes 4328 | tf_op jit(solution)/shard_map/ppermute | solution.py:33
  66.6 1.9 %collective-permute-start.6 = (f32[36,10]{1,0:T(8,128)S(1)}, f32[36,10]{1,0:T(8,128)S(1)}, u32[]{:S(2)}, u32[]{:S(2)}) collective-permute-start(f32[36,10]{1,0:T(8,128)S(1)} %get-tuple-element.103), channel_id=1, source_target_pairs={{0,1},{1,2},{2,3},{3,4},{4,5},{5,6},{6,7},{7,8},{8,9},{9,10},{10,1... | collective-permute-start | bytes 4328 | tf_op jit(solution)/shard_map/ppermute | solution.py:31
  68.5 6.6 %collective-permute-start.7 = (f32[36,10]{1,0:T(8,128)S(1)}, f32[36,10]{1,0:T(8,128)S(1)}, u32[]{:S(2)}, u32[]{:S(2)}) collective-permute-start(f32[36,10]{1,0:T(8,128)S(1)} %get-tuple-element.104), channel_id=1, source_target_pairs={{1,0},{2,1},{3,2},{4,3},{5,4},{6,5},{7,6},{8,7},{9,8},{10,9},{11,1... | collective-permute-start | bytes 4328 | tf_op jit(solution)/shard_map/ppermute | solution.py:33
  75.2 5.1 %add_add_fusion.1 = (f32[34,146]{1,0:T(8,128)S(1)}, f32[34,146]{1,0:T(8,128)S(1)}, f32[34,146]{1,0:T(8,128)S(1)}, f32[34,146]{1,0:T(8,128)S(1)}, f32[34,146]{1,0...) fusion(f32[36,148]{1,0:T(8,128)S(1)} %pad_maximum_fusion.3, ...), kind=kLoop, calls=%fused_computation.131 | loop fusion | flops 218416 | bytes 516288 | tf_op jit(solution)/shard_map/add | solution.py:66
  83.9 1.9 %collective-permute-start.2 = (f32[132,2]{0,1:T(2,128)S(1)}, f32[132,2]{0,1:T(2,128)S(1)}, u32[]{:S(2)}, u32[]{:S(2)}) collective-permute-start(f32[132,2]{0,1:T(2,128)S(1)} %get-tuple-element.33), channel_id=1, source_target_pairs={{0,1},{1,2},{2,3},{3,4},{4,5},{5,6},{6,7},{7,8},{8,9},{9,10},{10,1... | collective-permute-start | bytes 3176 | tf_op jit(solution)/shard_map/ppermute | solution.py:31
  85.8 6.8 %collective-permute-start.3 = (f32[132,2]{0,1:T(2,128)S(1)}, f32[132,2]{0,1:T(2,128)S(1)}, u32[]{:S(2)}, u32[]{:S(2)}) collective-permute-start(f32[132,2]{0,1:T(2,128)S(1)} %get-tuple-element.34), channel_id=1, source_target_pairs={{1,0},{2,1},{3,2},{4,3},{5,4},{6,5},{7,6},{8,7},{9,8},{10,9},{11,1... | collective-permute-start | bytes 3176 | tf_op jit(solution)/shard_map/ppermute | solution.py:33
  93.8 2.2 %maximum_maximum_fusion = (f32[132,1026]{0,1:T(8,128)}, f32[132,1026]{0,1:T(8,128)}) fusion(f32[2,1024]{0,1:T(8,128)S(1)} %copy-done.5, f32[128,1024]{0,1:T(8,128)S(1)} %copy.24, f32[2,1024]{0,1:T(8,128)S(1)} %collective-permute-done, f32[132,2]{0,1:T(2,128)S(1)} %collective-permute-done.2, f32[132,2]{0,1:T(2,128)S(1)} %collective-permute-done.3), kind=kLoop, calls=%fused_computation.46 | loop fusion | flops 812592 | bytes 1626240 | tf_op jit(solution)/shard_map/concatenate | solution.py:29
  96.0 3.2 %concatenate.29 = f32[132,1028]{0,1:T(8,128)S(1)} concatenate(f32[132,2]{0,1:T(2,128)S(1)} %collective-permute-done.2, f32[132,1024]{0,1:T(8,128)} %copy-done.3, f32[132,2]{0,1:T(2,128)S(1)} %collective-permute-done.3), dimensions={1} | concatenate | bytes 1085568 | tf_op jit(solution)/shard_map/concatenate | solution.py:29
  99.2 10.9 %add_add_fusion = (f32[130,1026]{0,1:T(8,128)S(1)}, f32[130,1026]{0,1:T(8,128)S(1)}, f32[130,1026]{0,1:T(8,128)S(1)}, f32[130,1026]{0,1:T(8,128)S(1)}, f32[130,1...) fusion(f32[132,1026]{0,1:T(8,128)} %get-tuple-element.32, ...), kind=kLoop, calls=%fused_computation.55 | loop fusion | flops 5868720 | bytes 13871552 | tf_op jit(solution)/shard_map/add | solution.py:66
  110.8 3.3 %copy-done = f32[8,130,1026]{1,2,0:T(8,128)} copy-done((f32[8,130,1026]{1,2,0:T(8,128)}, f32[8,130,1026]{1,2,0:T(8,128)S(1)}, u32[]{:S(2)}) %copy-start) | copy-done | bytes 4268184
  114.1 4.1 %broadcast_divide_fusion = f32[8,130,1026]{1,2,0:T(8,128)S(1)} fusion(f32[8,130,1026]{1,2,0:T(8,128)} %copy-done, f32[130,1026]{0,1:T(8,128)S(1)} %get-tuple-element.5), kind=kLoop, calls=%fused_computation | loop fusion | flops 1067040 | bytes 9069840 | tf_op jit(solution)/shard_map/div | solution.py:67
  119.2 1.5 %fusion.21 = f32[128,1024]{0,1:T(8,128)S(1)} fusion(f32[130,1026]{0,1:T(8,128)S(1)} %slice.1195, f32[130,1026]{0,1:T(8,128)S(1)} %get-tuple-element.24, f32[130,1026]{0,1:T(8,128)S(1)} %get-tuple-element.25, f32[130,1026]{0,1:T(8,128)S(1)} %get-tuple-element.26, f32[130,1026]{0,1:T(8,128)S(1)} %get-tuple-element.27, f32[130,1026]{0,1:T(8,128)S(1)} %get-tuple-element.28, ...), kind=kLoop, calls=%fused_computation.61 | loop fusion | flops 2228224 | bytes 9437184 | tf_op jit(solution)/shard_map/add | solution.py:129
  (99 shorter events, 12.0 us)
Async XLA Ops:
  0.0 13.6 %copy-start.7 = (f32[128,1024]{1,0:T(8,128)S(1)}, f32[128,1024]{1,0:T(8,128)}, u32[]{:S(2)}) copy-start(f32[128,1024]{1,0:T(8,128)} %param.3) | copy-start | bytes 1572868
  0.8 13.0 %copy-start.8 = (s32[128,1024]{1,0:T(8,128)S(1)}, s32[128,1024]{1,0:T(8,128)}, u32[]{:S(2)}) copy-start(s32[128,1024]{1,0:T(8,128)} %param.4) | copy-start | bytes 1572868
  1.9 81.2 %collective-permute-start = (f32[2,1024]{0,1:T(8,128)}, f32[2,1024]{0,1:T(8,128)S(1)}, u32[]{:S(2)}, u32[]{:S(2)}) collective-permute-start(f32[2,1024]{0,1:T(8,128)} %copy.22), channel_id=1, source_target_pairs={{0,16},{16,32},{32,48},{48,64},{64,80},{80,96},{96,112},{112,128},... | collective-permute-start | bytes 24584 | tf_op jit(solution)/shard_map/ppermute | solution.py:31
  4.8 78.3 %collective-permute-start.1 = (f32[2,1024]{0,1:T(8,128)}, f32[2,1024]{0,1:T(8,128)S(1)}, u32[]{:S(2)}, u32[]{:S(2)}) collective-permute-start(f32[2,1024]{0,1:T(8,128)} %copy.23), channel_id=1, source_target_pairs={{16,0},{32,16},{48,32},{64,48},{80,64},{96,80},{112,96},{128,112},... | collective-permute-start | bytes 24584 | tf_op jit(solution)/shard_map/ppermute | solution.py:33
  14.1 1.0 copy-start.1
  15.2 6.2 %copy-start.6 = (f32[128,1024]{0,1:T(8,128)S(1)}, f32[128,1024]{0,1:T(8,128)}, u32[]{:S(2)}) copy-start(f32[128,1024]{0,1:T(8,128)} %convert_element_type.32) | copy-start | bytes 1572868
  31.8 16.5 %copy-start.9 = (s32[8]{0:T(128)S(1)}, s32[8]{0:T(128)}, u32[]{:S(2)}) copy-start(s32[8]{0:T(128)} %param.5) | copy-start | bytes 100
  35.9 13.5 %collective-permute-start.8 = (f32[10,128]{1,0:T(8,128)S(1)}, f32[10,128]{1,0:T(8,128)S(1)}, u32[]{:S(2)}, u32[]{:S(2)}) collective-permute-start(f32[10,128]{1,0:T(8,128)S(1)} %get-tuple-element.105), channel_id=1, source_target_pairs={{0,16},{16,32},{32,48},{48,64},{64,80},{80,96},{96,112},{112,128},... | collective-permute-start | bytes 15368 | tf_op jit(solution)/shard_map/ppermute | solution.py:31
  38.2 19.6 %collective-permute-start.9 = (f32[10,128]{1,0:T(8,128)S(1)}, f32[10,128]{1,0:T(8,128)S(1)}, u32[]{:S(2)}, u32[]{:S(2)}) collective-permute-start(f32[10,128]{1,0:T(8,128)S(1)} %get-tuple-element.106), channel_id=1, source_target_pairs={{16,0},{32,16},{48,32},{64,48},{80,64},{96,80},{112,96},{128,112},... | collective-permute-start | bytes 15368 | tf_op jit(solution)/shard_map/ppermute | solution.py:33
  46.3 15.1 %collective-permute-start.4 = (f32[10,128]{1,0:T(8,128)S(1)}, f32[10,128]{1,0:T(8,128)S(1)}, u32[]{:S(2)}, u32[]{:S(2)}) collective-permute-start(f32[10,128]{1,0:T(8,128)S(1)} %get-tuple-element.109), channel_id=1, source_target_pairs={{0,16},{16,32},{32,48},{48,64},{64,80},{80,96},{96,112},{112,128},... | collective-permute-start | bytes 15368 | tf_op jit(solution)/shard_map/ppermute | solution.py:31
  49.4 17.1 %collective-permute-start.5 = (f32[10,128]{1,0:T(8,128)S(1)}, f32[10,128]{1,0:T(8,128)S(1)}, u32[]{:S(2)}, u32[]{:S(2)}) collective-permute-start(f32[10,128]{1,0:T(8,128)S(1)} %get-tuple-element.110), channel_id=1, source_target_pairs={{16,0},{32,16},{48,32},{64,48},{80,64},{96,80},{112,96},{128,112},... | collective-permute-start | bytes 15368 | tf_op jit(solution)/shard_map/ppermute | solution.py:33
  57.9 10.6 %collective-permute-start.10 = (f32[36,10]{1,0:T(8,128)S(1)}, f32[36,10]{1,0:T(8,128)S(1)}, u32[]{:S(2)}, u32[]{:S(2)}) collective-permute-start(f32[36,10]{1,0:T(8,128)S(1)} %get-tuple-element.101), channel_id=1, source_target_pairs={{0,1},{1,2},{2,3},{3,4},{4,5},{5,6},{6,7},{7,8},{8,9},{9,10},{10,1... | collective-permute-start | bytes 4328 | tf_op jit(solution)/shard_map/ppermute | solution.py:31
  61.4 13.7 %collective-permute-start.11 = (f32[36,10]{1,0:T(8,128)S(1)}, f32[36,10]{1,0:T(8,128)S(1)}, u32[]{:S(2)}, u32[]{:S(2)}) collective-permute-start(f32[36,10]{1,0:T(8,128)S(1)} %get-tuple-element.102), channel_id=1, source_target_pairs={{1,0},{2,1},{3,2},{4,3},{5,4},{6,5},{7,6},{8,7},{9,8},{10,9},{11,1... | collective-permute-start | bytes 4328 | tf_op jit(solution)/shard_map/ppermute | solution.py:33
  66.6 14.9 %collective-permute-start.6 = (f32[36,10]{1,0:T(8,128)S(1)}, f32[36,10]{1,0:T(8,128)S(1)}, u32[]{:S(2)}, u32[]{:S(2)}) collective-permute-start(f32[36,10]{1,0:T(8,128)S(1)} %get-tuple-element.103), channel_id=1, source_target_pairs={{0,1},{1,2},{2,3},{3,4},{4,5},{5,6},{6,7},{7,8},{8,9},{9,10},{10,1... | collective-permute-start | bytes 4328 | tf_op jit(solution)/shard_map/ppermute | solution.py:31
  68.5 13.0 %collective-permute-start.7 = (f32[36,10]{1,0:T(8,128)S(1)}, f32[36,10]{1,0:T(8,128)S(1)}, u32[]{:S(2)}, u32[]{:S(2)}) collective-permute-start(f32[36,10]{1,0:T(8,128)S(1)} %get-tuple-element.104), channel_id=1, source_target_pairs={{1,0},{2,1},{3,2},{4,3},{5,4},{6,5},{7,6},{8,7},{9,8},{10,9},{11,1... | collective-permute-start | bytes 4328 | tf_op jit(solution)/shard_map/ppermute | solution.py:33
  83.1 0.8 copy-start.4
  83.9 9.2 %copy-start.3 = (f32[132,1024]{0,1:T(8,128)}, f32[132,1024]{0,1:T(8,128)S(1)}, u32[]{:S(2)}) copy-start(f32[132,1024]{0,1:T(8,128)S(1)} %pad_maximum_fusion.1) | copy-start | bytes 1622020
  83.9 9.2 %collective-permute-start.2 = (f32[132,2]{0,1:T(2,128)S(1)}, f32[132,2]{0,1:T(2,128)S(1)}, u32[]{:S(2)}, u32[]{:S(2)}) collective-permute-start(f32[132,2]{0,1:T(2,128)S(1)} %get-tuple-element.33), channel_id=1, source_target_pairs={{0,1},{1,2},{2,3},{3,4},{4,5},{5,6},{6,7},{7,8},{8,9},{9,10},{10,1... | collective-permute-start | bytes 3176 | tf_op jit(solution)/shard_map/ppermute | solution.py:31
  85.8 7.9 %collective-permute-start.3 = (f32[132,2]{0,1:T(2,128)S(1)}, f32[132,2]{0,1:T(2,128)S(1)}, u32[]{:S(2)}, u32[]{:S(2)}) collective-permute-start(f32[132,2]{0,1:T(2,128)S(1)} %get-tuple-element.34), channel_id=1, source_target_pairs={{1,0},{2,1},{3,2},{4,3},{5,4},{6,5},{7,6},{8,7},{9,8},{10,9},{11,1... | collective-permute-start | bytes 3176 | tf_op jit(solution)/shard_map/ppermute | solution.py:33
  92.7 1.0 copy-start.5
  110.8 3.3 %copy-start = (f32[8,130,1026]{1,2,0:T(8,128)}, f32[8,130,1026]{1,2,0:T(8,128)S(1)}, u32[]{:S(2)}) copy-start(f32[8,130,1026]{1,2,0:T(8,128)S(1)} %bitcast_dynamic-update-slice_fusion) | copy-start | bytes 12804484
  118.2 1.0 copy-start.2
where the time goes:
time: 123 us; the launch traced here: 122 us
  starting transfers between devices  57.2 us (47%)
  other arithmetic  35.2 us (29%)
  local copies, waits for them, and re-layouts  27.9 us (23%)
    ppermute x6, starting transfers between devices, with_halo(): lax.ppermute(head, axis, [((i + 1) % count, i) for i in range(ends)])  43.8 us
    add x2, other arithmetic, outflow_weight_matrix(): totals = jnp.sum(slopes, axis=0) + RETENTION  16 us
    ppermute x6, starting transfers between devices, with_halo(): lax.ppermute(tail, axis, [(i, (i + 1) % count) for i in range(ends)])  13.4 us
    reshape x1, local copies, waits for them, and re-layouts, on_device(): (valid_flag * elevation).reshape(coarse_rows, 8, coarse_cols, 8)  6.22 us
    reshape x1, local copies, waits for them, and re-layouts, on_device(): counts = valid_flag.reshape(coarse_rows, 8, coarse_cols, 8).sum(axis=(1, 3))  6.14 us
    unnamed x36, local copies, waits for them, and re-layouts  5.03 us
    div x2, other arithmetic, outflow_weight_matrix(): return slopes / totals  4.13 us
    reduce_sum x1, other arithmetic, on_device(): counts = valid_flag.reshape(coarse_rows, 8, coarse_cols, 8).sum(axis=(1, 3))  4.02 us
  transfers between devices with their start and end apart: 12, of which 1 were waited for; matrix products, arithmetic and copies ran while one was open for 27% of the time, Pallas kernels for 0%

commit v1 on v0

v1 whole, which is shorter than its diff:
```python
import functools

import jax
import jax.numpy as jnp
from jax import lax
from jax.experimental import pallas as pl
from jax.experimental.pallas import tpu as pltpu
from jax.sharding import PartitionSpec as P

ITERS = 8
OFFSETS = ((0, 1), (1, 1), (1, 0), (1, -1), (0, -1), (-1, -1), (-1, 0), (-1, 1))
DIAGONAL = 0.7071067811865476
RETENTION = 0.1
OUTSIDE = 1e30
LANES = 128
VMEM = pltpu.VMEM
LIMIT = 48 * 1024 * 1024


def iota(shape, dim):
    return lax.broadcasted_iota(jnp.int32, shape, dim)


def coefficients(tie_ref, coef_ref):
    for place in range(8):
        k = tie_ref[place]
        value = 1.0 + 0.5 * (7.0 - place) / 7.0
        coef_ref[k] = jnp.where(k % 2 == 0, value, value * DIAGONAL).astype(jnp.float32)
    return [coef_ref[k] for k in range(8)]


def beside(left, mid, right):
    lane = iota(mid.shape, 1)
    west = jnp.where(lane == 0, pltpu.roll(left, 1, 1), pltpu.roll(mid, 1, 1))
    east = jnp.where(lane == LANES - 1, pltpu.roll(right, LANES - 1, 1), pltpu.roll(mid, LANES - 1, 1))
    return west, east


def neighbour(planes, j, row, k):
    step_row, step_col = OFFSETS[k]
    ref = planes[{0: 0, -1: 1, 1: 2}[step_col]]
    return ref[j, pl.ds(row + step_row, 8), :]


def spread(planes, chunks, first, count):
    centre, west, east = planes
    for j in range(chunks):
        w, e = beside(
            centre[(j - 1) % chunks, pl.ds(first, count), :],
            centre[j, pl.ds(first, count), :],
            centre[(j + 1) % chunks, pl.ds(first, count), :],
        )
        west[j, pl.ds(first, count), :] = w
        east[j, pl.ds(first, count), :] = e


def reciprocal_total(planes, j, row, coef):
    z = planes[0][j, pl.ds(row, 8), :]
    parts = [coef[k] * jnp.maximum(z - neighbour(planes, j, row, k), 0.0) for k in range(8)]
    total = ((parts[0] + parts[1]) + (parts[2] + parts[3])) + ((parts[4] + parts[5]) + (parts[6] + parts[7]))
    return 1.0 / (total + RETENTION)


def inward(planes, j, row, k, coef):
    z = planes[0][j, pl.ds(row, 8), :]
    return coef[(k + 4) % 8] * jnp.maximum(neighbour(planes, j, row, k) - z, 0.0)


def fields(z_planes, r_planes, j, row, coef):
    lane = iota((8, LANES), 1) % 8
    sub = iota((8, LANES), 0)
    at_east, at_west = lane == 7, lane == 0
    first, last = sub == 0, sub == 7
    t = [inward(z_planes, j, row, k, coef) * neighbour(r_planes, j, row, k) for k in range(8)]

    def split(east, west):
        own = jnp.where(at_east, west, jnp.where(at_west, east, east + west))
        other = jnp.where(at_east, east, jnp.where(at_west, west, 0.0))
        return own, other

    own0, other0 = split(t[0], t[4])
    own_down, other_down = split(t[1], t[3])
    own_down = own_down + t[2]
    own_up, other_up = split(t[7], t[5])
    own_up = own_up + t[6]
    a00 = own0 + jnp.where(first, 0.0, own_up) + jnp.where(last, 0.0, own_down)
    a01 = other0 + jnp.where(first, 0.0, other_up) + jnp.where(last, 0.0, other_down)
    a10 = jnp.where(first, own_up, jnp.where(last, own_down, 0.0))
    a11 = jnp.where(first, other_up, jnp.where(last, other_down, 0.0))
    return a00, a01, a10, a11


def block_rows(tiles):
    sub = iota(tiles[0].shape, 0)
    level = [tiles[t] for t in (0, 4, 2, 6, 1, 5, 3, 7)]
    for shift in (4, 2, 1):
        low = (sub & shift) == 0
        level = [
            jnp.where(low, a + pltpu.roll(a, 8 - shift, 0), b + pltpu.roll(b, shift, 0))
            for a, b in zip(level[0::2], level[1::2])
        ]
    return level[0]


def overview_kernel(el, mk, msg, edge):
    rows, cols = el.shape
    chunks = cols // LANES
    col = iota((cols, LANES), 0) // 8
    pick = jnp.where(col == iota((cols, LANES), 1), 1.0, 0.0).astype(jnp.bfloat16)
    sums, counts = [], []
    for g in range(rows // 64):
        s_parts, n_parts = [], []
        for j in range(chunks):
            s_tiles, n_tiles = [], []
            for t in range(8):
                at = (slice(64 * g + 8 * t, 64 * g + 8 * t + 8), slice(LANES * j, LANES * j + LANES))
                m = mk[at].astype(jnp.float32)
                n_tiles.append(m)
                s_tiles.append(m * el[at])
            s_parts.append(block_rows(s_tiles))
            n_parts.append(block_rows(n_tiles))
        sums.append(jnp.concatenate(s_parts, axis=1))
        counts.append(jnp.concatenate(n_parts, axis=1))
    s = jnp.concatenate(sums, axis=0)
    n = jnp.concatenate(counts, axis=0)
    hi = s.astype(jnp.bfloat16)
    rest = s - hi.astype(jnp.float32)
    mid = rest.astype(jnp.bfloat16)
    low = (rest - mid.astype(jnp.float32)).astype(jnp.bfloat16)
    left = jnp.concatenate([hi, mid, low, n.astype(jnp.bfloat16)], axis=0)
    out = lax.dot_general(left, pick, (((1,), (0,)), ((), ())), preferred_element_type=jnp.float32)
    k = rows // 8
    summed = out[0:k] + (out[k : 2 * k] + out[2 * k : 3 * k])
    count = out[3 * k : 4 * k]
    msg[0:k, :] = summed / (count + 1.0)
    msg[k : 2 * k, :] = count * (1.0 / 64.0)
    first = jnp.transpose(el[:, 0:LANES])
    last = jnp.transpose(el[:, cols - LANES : cols])
    msg[2 * k : 2 * k + 4, :] = first[0:4]
    msg[2 * k + 4 : 2 * k + 8, :] = last[LANES - 4 : LANES]
    edge[0:4, :] = el[0:4, :]
    edge[4:8, :] = el[rows - 4 : rows, :]


def row_message_kernel(own, from_a, from_b, edge, coarse, side, to_n, to_f):
    k = (own.shape[0] - 8) // 2
    cols = edge.shape[1]
    chunks = cols // LANES
    r, c = lax.axis_index("rows"), lax.axis_index("cols")
    count = lax.axis_size("cols")
    even = c % 2 == 0
    shape = own.shape
    a, b = from_a[...], from_b[...]
    line = iota(shape, 0)
    missing = jnp.where((line >= k) & (line < 2 * k), 0.0, OUTSIDE)
    right = jnp.where(jnp.full(shape, c == count - 1), missing, jnp.where(jnp.full(shape, even), a, b))
    left = jnp.where(jnp.full(shape, c == 0), missing, jnp.where(jnp.full(shape, even), b, a))
    lane = iota((2 * k, LANES), 1)
    near = jnp.where(lane < LANES // 2, right[0 : 2 * k], left[0 : 2 * k])
    mine = own[...]
    c4 = (mine[0:k], near[0:k], mine[k : 2 * k], near[k : 2 * k])
    for i, part in enumerate(c4):
        coarse[i * k : (i + 1) * k, :] = part
        to_n[i * k : (i + 1) * k, :] = part
        to_f[i * k : (i + 1) * k, :] = part
    cols_t = jnp.concatenate(
        [right[2 * k : 2 * k + 4], jnp.zeros((LANES - 8, LANES), jnp.float32), left[2 * k + 4 : 2 * k + 8]], axis=0
    )
    beyond = jnp.transpose(cols_t)
    side[...] = beyond
    rows = beyond.shape[0]
    upper = r % 2 == 0
    for j in range(chunks + 1):
        if j < chunks:
            top, bottom = edge[0:2, LANES * j : LANES * j + LANES], edge[6:8, LANES * j : LANES * j + LANES]
        else:
            top, bottom = beyond[0:2], beyond[rows - 2 : rows]
        cond = jnp.full((2, LANES), upper)
        to_n[4 * k + 2 * j : 4 * k + 2 * j + 2, :] = jnp.where(cond, bottom, top)
        to_f[4 * k + 2 * j : 4 * k + 2 * j + 2, :] = jnp.where(cond, top, bottom)


def coefficient_kernel(tie, el, side, out, coef_ref, zc, zw, ze, rc, rw, re):
    rows, cols = el.shape
    chunks = cols // LANES
    coef = coefficients(tie, coef_ref)
    z_planes, r_planes = (zc, zw, ze), (rc, rw, re)
    for j in range(chunks + 1):
        for at in (0, rows + 8):
            zc[j, at : at + 8, :] = jnp.zeros((8, LANES), jnp.float32)
            rc[j, at : at + 8, :] = jnp.zeros((8, LANES), jnp.float32)
        zc[j, 8 : 8 + rows, :] = el[:, LANES * j : LANES * j + LANES] if j < chunks else side[...]
    spread(z_planes, chunks + 1, 0, rows + 16)

    def totals(t, carry):
        row = pl.multiple_of(8 + 8 * t, 8)
        for j in range(chunks + 1):
            rc[j, pl.ds(row, 8), :] = reciprocal_total(z_planes, j, row, coef)
        return carry

    lax.fori_loop(0, rows // 8, totals, 0)
    spread(r_planes, chunks + 1, 0, rows + 16)

    def combine(t, carry):
        row = pl.multiple_of(8 + 8 * t, 8)
        for j in range(chunks):
            for i, field in enumerate(fields(z_planes, r_planes, j, row, coef)):
                out[i, pl.ds(pl.multiple_of(8 * t, 8), 8), LANES * j : LANES * j + LANES] = field
        return carry

    lax.fori_loop(0, rows // 8, combine, 0)


def inflow_kernel(
    tie, coarse, from_n, from_f, ends, side, given, mk, out,
    coef_ref, kc, kw, ke, sc, sw, se, run, gain, flow, zc, zw, ze, rc, rw, re, edge_fields, up_ref, vv_ref,
):
    k = coarse.shape[0] // 4
    rows, cols = mk.shape
    chunks = cols // LANES
    r, count = lax.axis_index("rows"), lax.axis_size("rows")
    upper = r % 2 == 0
    coef = coefficients(tie, coef_ref)
    n, f = from_n[...], from_f[...]
    shape = n.shape
    line = iota(shape, 0)
    missing = jnp.where((line >= 2 * k) & (line < 4 * k), 0.0, OUTSIDE)
    cond = jnp.full(shape, upper)
    above = jnp.where(jnp.full(shape, r == 0), missing, jnp.where(cond, f, n))
    below = jnp.where(jnp.full(shape, r == count - 1), missing, jnp.where(cond, n, f))

    k_planes, s_planes = (kc, kw, ke), (sc, sw, se)
    for j in range(2):
        kc[j, 0:8, :] = jnp.zeros((8, LANES), jnp.float32)
        kc[j, 8 + 3 * k : 16 + 3 * k, :] = jnp.zeros((8, LANES), jnp.float32)
        for ref, base, first in ((kc, 0, 8), (run, 2 * k, 0)):
            lo = base + j * k
            ref[j, first : first + k, :] = above[lo : lo + k]
            ref[j, first + k : first + 2 * k, :] = coarse[lo : lo + k, :]
            ref[j, first + 2 * k : first + 3 * k, :] = below[lo : lo + k]
    spread(k_planes, 2, 0, 3 * k + 16)
    recip = {}
    for j in range(2):
        for t in range(3 * k // 8):
            recip[j, t] = reciprocal_total(k_planes, j, 8 + 8 * t, coef)
    inner = range(1, 3 * k // 8 - 1)
    for j in range(2):
        for t in inner:
            for d in range(8):
                gain[d, j, 8 * t : 8 * t + 8, :] = inward(k_planes, j, 8 + 8 * t, d, coef)

    z_planes, r_planes = (zc, zw, ze), (rc, rw, re)
    for top in (True, False):
        halo = above if top else below
        for j in range(chunks + 1):
            lines = halo[4 * k + 2 * j : 4 * k + 2 * j + 2]
            pad = jnp.zeros((6, LANES), jnp.float32)
            if j < chunks:
                known = ends[0:16, LANES * j : LANES * j + LANES] if top else ends[16:32, LANES * j : LANES * j + LANES]
            else:
                known = side[0:16, :] if top else side[rows - 16 : rows, :]
            blank = jnp.zeros((8, LANES), jnp.float32)
            zc[j, 0:8, :] = blank
            zc[j, 32:40, :] = blank
            if top:
                zc[j, 8:16, :] = jnp.concatenate([pad, lines], axis=0)
                zc[j, 16:32, :] = known
            else:
                zc[j, 8:24, :] = known
                zc[j, 24:32, :] = jnp.concatenate([lines, pad], axis=0)
        spread(z_planes, chunks + 1, 0, 40)
        for j in range(chunks + 1):
            for t in range(3):
                rc[j, 8 + 8 * t : 16 + 8 * t, :] = reciprocal_total(z_planes, j, 8 + 8 * t, coef)
        spread(r_planes, chunks + 1, 8, 24)
        for j in range(chunks):
            for i, field in enumerate(fields(z_planes, r_planes, j, 16, coef)):
                edge_fields[0 if top else 1, i, :, LANES * j : LANES * j + LANES] = field

    for j in range(2):
        for t in range(3 * k // 8):
            sc[j, 8 * t : 8 * t + 8, :] = recip[j, t] * run[j, 8 * t : 8 * t + 8, :]
    spread(s_planes, 2, 0, 3 * k)
    for sweep in range(ITERS):
        for j in range(2):
            for t in inner:
                parts = [gain[d, j, 8 * t : 8 * t + 8, :] * neighbour(s_planes, j, 8 * t, d) for d in range(8)]
                total = ((parts[0] + parts[1]) + (parts[2] + parts[3])) + (
                    (parts[4] + parts[5]) + (parts[6] + parts[7])
                )
                flow[j, 8 * t : 8 * t + 8, :] = run[j, 8 * t : 8 * t + 8, :] + total
        if sweep < ITERS - 1:
            for j in range(2):
                for t in inner:
                    sc[j, 8 * t : 8 * t + 8, :] = recip[j, t] * flow[j, 8 * t : 8 * t + 8, :]
            spread(s_planes, 2, 8, 3 * k - 16)

    lane = iota((8, LANES), 1)
    block = lane // 8
    step = jnp.where(lane % 8 == 7, 1, jnp.where(lane % 8 == 0, -1, 0))
    per = LANES // 8
    for t in inner:
        main = flow[0, 8 * t : 8 * t + 8, :]
        apart = flow[1, 8 * t : 8 * t + 8, :]
        for j in range(chunks):
            here = block + per * j
            over = here + step
            up_ref[j, 8 * t : 8 * t + 8, :] = jnp.take_along_axis(main, here, axis=1, mode="promise_in_bounds")
            v = jnp.take_along_axis(main, over & (LANES - 1), axis=1, mode="promise_in_bounds")
            if j == 0:
                far = jnp.take_along_axis(apart, over & (LANES - 1), axis=1, mode="promise_in_bounds")
                v = jnp.where(lane == 0, far, v)
            if j == chunks - 1:
                far = jnp.take_along_axis(apart, over & (LANES - 1), axis=1, mode="promise_in_bounds")
                v = jnp.where(lane == LANES - 1, far, v)
            vv_ref[j, 8 * t : 8 * t + 8, :] = v

    high = iota((8, LANES), 0) < 4
    for j in range(chunks):
        for b in range(rows // 8):
            at = (slice(8 * b, 8 * b + 8), slice(LANES * j, LANES * j + LANES))
            row = k + b
            wide = [jnp.broadcast_to(up_ref[j, row + i : row + i + 1, :], (8, LANES)) for i in (-1, 0, 1)]
            apart = [jnp.broadcast_to(vv_ref[j, row + i : row + i + 1, :], (8, LANES)) for i in (-1, 0, 1)]
            if b == 0 or b == rows // 8 - 1:
                which = 0 if b == 0 else 1
                a = [edge_fields[which, i, :, at[1]] for i in range(4)]
            else:
                a = [given[i, at[0], at[1]] for i in range(4)]
            out[at] = mk[at].astype(jnp.float32) + (
                (a[0] * wide[1] + a[1] * apart[1])
                + (a[2] * jnp.where(high, wide[0], wide[2]) + a[3] * jnp.where(high, apart[0], apart[2]))
            )


def swap(x, axis, far):
    count = lax.axis_size(axis)
    if far:
        pairs = [(i, (i + 1) % count if i % 2 else (i - 1) % count) for i in range(count)]
    else:
        pairs = [(i, i ^ 1) for i in range(count)]
    return lax.ppermute(x, axis, pairs)


def f32(*shape):
    return jax.ShapeDtypeStruct(shape, jnp.float32)


def whole(count):
    return [pl.BlockSpec(memory_space=VMEM)] * count


def on_device(elevation, data_mask, tie_order):
    rows, cols = elevation.shape
    k, chunks = rows // 8, cols // LANES
    params = pltpu.CompilerParams(vmem_limit_bytes=LIMIT)
    msg, edge = pl.pallas_call(
        overview_kernel,
        out_shape=[f32(2 * k + 8, LANES), f32(8, cols)],
        in_specs=whole(2),
        out_specs=whole(2),
        compiler_params=params,
        name="overview",
    )(elevation, data_mask)
    from_b = swap(msg, "cols", True)
    from_a = swap(msg, "cols", False)
    size = 4 * k + 24
    coarse, side, to_n, to_f = pl.pallas_call(
        row_message_kernel,
        out_shape=[f32(4 * k, LANES), f32(rows, LANES), f32(size, LANES), f32(size, LANES)],
        in_specs=whole(4),
        out_specs=whole(4),
        compiler_params=params,
        name="row_message",
    )(msg, from_a, from_b, edge)
    from_n = swap(to_n, "rows", False)
    from_f = swap(to_f, "rows", True)
    smem = pl.BlockSpec(memory_space=pltpu.SMEM)
    fine = lambda height: [VMEM((chunks + 1, height, LANES), jnp.float32)] * 6
    given = pl.pallas_call(
        coefficient_kernel,
        out_shape=f32(4, rows, cols),
        in_specs=[smem] + whole(2),
        out_specs=pl.BlockSpec(memory_space=VMEM),
        scratch_shapes=[pltpu.SMEM((8,), jnp.float32)] + fine(rows + 16),
        compiler_params=params,
        cost_estimate=pl.CostEstimate(flops=20_000_000, bytes_accessed=4_000_000, transcendentals=0),
        name="coefficient_fields",
    )(tie_order, elevation, side)
    ends = jnp.concatenate([elevation[0:16], elevation[rows - 16 : rows]], axis=0)
    coarse_plane = lambda height: VMEM((2, height, LANES), jnp.float32)
    return pl.pallas_call(
        inflow_kernel,
        out_shape=f32(rows, cols),
        in_specs=[smem] + whole(7),
        out_specs=pl.BlockSpec(memory_space=VMEM),
        scratch_shapes=[pltpu.SMEM((8,), jnp.float32)]
        + [coarse_plane(3 * k + 16)] * 3
        + [coarse_plane(3 * k)] * 3
        + [coarse_plane(3 * k), VMEM((8, 2, 3 * k, LANES), jnp.float32), coarse_plane(3 * k)]
        + fine(40)
        + [VMEM((2, 4, 8, cols), jnp.float32)]
        + [VMEM((chunks, 3 * k, LANES), jnp.float32)] * 2,
        compiler_params=params,
        name="inflow",
    )(tie_order, coarse, from_n, from_f, ends, side, given, data_mask)


def solution(mesh):
    in_specs = (P("rows", "cols"), P("rows", "cols"), P())
    out_specs = P("rows", "cols")
    return jax.shard_map(
        on_device, mesh=mesh, in_specs=in_specs, out_specs=out_specs, check_vma=False
    )
```

time: 123 us -> 29 us (0.24)
  the two profiles are of different devices: /device:TPU:30 before, /device:TPU:1 now
where the time goes in v1:
time: 29 us; the launch traced here: 28.8 us
  starting transfers between devices  13.8 us (48%)
  Pallas kernels  8.23 us (28%)
  local copies, waits for them, and re-layouts  3.79 us (13%)
  waiting for transfers between devices  2.9 us (10%)
    ppermute x4, starting transfers between devices, swap(): return lax.ppermute(x, axis, pairs)  13.8 us
    pallas_call x1, Pallas kernels, on_device(): pl.pallas_call(coefficient_kernel, out_shape=f32(4, rows, cols), in_specs...  4.15 us
    unnamed x10, local copies, waits for them, and re-layouts  3.78 us
    pallas_call x1, Pallas kernels, on_device(): pl.pallas_call(inflow_kernel, out_shape=f32(rows, cols), in_specs=[smem]...  3.59 us
    ppermute x4, waiting for transfers between devices, swap(): return lax.ppermute(x, axis, pairs)  2.9 us
  transfers between devices with their start and end apart: 4, of which 2 were waited for; matrix products, arithmetic and copies ran while one was open for 0% of the time, Pallas kernels for 14%

profile of v1, /device:TPU:1, one launch (start us, length us, event | category | flops | bytes accessed | tf_op | source)
XLA Modules:
  0.0 28.8 jit_solution(17197146675776887599)
XLA Ops:
  0.0 0.0 copy-start
  0.0 1.0 %copy-done = f32[128,1024]{1,0:T(8,128)S(1)} copy-done((f32[128,1024]{1,0:T(8,128)S(1)}, f32[128,1024]{1,0:T(8,128)}, u32[]{:S(2)}) %copy-start) | copy-done | bytes 524312
  1.0 0.0 copy-start.2
  1.0 1.0 %copy-done.2 = s32[128,1024]{1,0:T(8,128)S(1)} copy-done((s32[128,1024]{1,0:T(8,128)S(1)}, s32[128,1024]{1,0:T(8,128)}, u32[]{:S(2)}) %copy-start.2) | copy-done | bytes 524312
  2.1 0.0 copy-start.3
  2.1 0.4 %overview.1 = (f32[40,128]{1,0:T(8,128)S(1)}, f32[8,1024]{1,0:T(8,128)S(1)}) custom-call(f32[128,1024]{1,0:T(8,128)S(1)} %copy-done, s32[128,1024]{1,0:T(8,128)S(1)} %copy-done.2), custom_call_target="tpu_custom_call" | custom-call | tf_op jit(solution)/shard_map/overview/pallas_call | solution.py:357
  2.5 7.7 %collective-permute-start.1 = (f32[40,128]{1,0:T(8,128)S(1)}, f32[40,128]{1,0:T(8,128)S(1)}, u32[]{:S(2)}, u32[]{:S(2)}) collective-permute-start(f32[40,128]{1,0:T(8,128)S(1)} %get-tuple-element.11.own), channel_id=1, source_target_pairs={{0,15},{1,2},{2,1},{3,4},{4,3},{5,6},{6,5},{7,8},{8,7},{9,10},{10,... | collective-permute-start | bytes 61448 | tf_op jit(solution)/shard_map/ppermute | solution.py:342
  10.2 0.0 collective-permute-start
  10.2 1.2 %collective-permute-done.1.from_b = f32[40,128]{1,0:T(8,128)S(1)} collective-permute-done((f32[40,128]{1,0:T(8,128)S(1)}, f32[40,128]{1,0:T(8,128)S(1)}, u32[]{:S(2)}, u32[]{:S(2)}) %collective-permute-start.1) | collective-permute-done | bytes 20512 | tf_op jit(solution)/shard_map/ppermute | solution.py:342
  11.4 1.7 %collective-permute-done.from_a = f32[40,128]{1,0:T(8,128)S(1)} collective-permute-done((f32[40,128]{1,0:T(8,128)S(1)}, f32[40,128]{1,0:T(8,128)S(1)}, u32[]{:S(2)}, u32[]{:S(2)}) %collective-permute-start) | collective-permute-done | bytes 20512 | tf_op jit(solution)/shard_map/ppermute | solution.py:342
  13.1 0.1 row_message.1
  13.2 1.9 %collective-permute-start.2 = (f32[88,128]{1,0:T(8,128)S(1)}, f32[88,128]{1,0:T(8,128)S(1)}, u32[]{:S(2)}, u32[]{:S(2)}) collective-permute-start(f32[88,128]{1,0:T(8,128)S(1)} %get-tuple-element.14), channel_id=1, source_target_pairs={{0,16},{16,0},{32,48},{48,32},{64,80},{80,64},{96,112},{112,96},{1... | collective-permute-start | bytes 135176 | tf_op jit(solution)/shard_map/ppermute | solution.py:342
  15.1 4.2 %collective-permute-start.3 = (f32[88,128]{1,0:T(8,128)S(1)}, f32[88,128]{1,0:T(8,128)S(1)}, u32[]{:S(2)}, u32[]{:S(2)}) collective-permute-start(f32[88,128]{1,0:T(8,128)S(1)} %get-tuple-element.15), channel_id=1, source_target_pairs={{0,240},{16,32},{32,16},{48,64},{64,48},{80,96},{96,80},{112,128},... | collective-permute-start | bytes 135176 | tf_op jit(solution)/shard_map/ppermute | solution.py:342
  19.3 0.0 copy-start.1
  19.3 1.0 %copy-done.1 = f32[128,1024]{1,0:T(8,128)S(1)} copy-done((f32[128,1024]{1,0:T(8,128)S(1)}, f32[128,1024]{1,0:T(8,128)}, u32[]{:S(2)}) %copy-start.1) | copy-done | bytes 524312
  20.4 0.0 copy-start.4
  20.4 0.7 %copy-done.4 = s32[8]{0:T(128)S(1)} copy-done((s32[8]{0:T(128)S(1)}, s32[8]{0:T(128)}, u32[]{:S(2)}) %copy-start.4) | copy-done | bytes 56
  21.0 4.2 %coefficient_fields.1.given = f32[4,128,1024]{2,1,0:T(8,128)S(1)} custom-call(s32[8]{0:T(128)S(1)} %copy-done.4, f32[128,1024]{1,0:T(8,128)S(1)} %copy-done.1, f32[128,128]{1,0:T(8,128)S(1)} %get-tuple-element.16.side), custom_call_target="tpu_custom_call" | custom-call | flops 20000000 | bytes 4000000 | tf_op jit(solution)/shard_map/coefficient_fields/pallas_call | solution.py:380
  25.2 0.0 collective-permute-done.2.from_n
  25.2 0.0 collective-permute-done.3.from_f
  25.2 0.0 copy-done.3
  25.2 3.6 %inflow.1 = f32[128,1024]{1,0:T(8,128)} custom-call(s32[8]{0:T(128)S(1)} %copy-done.4, f32[64,128]{1,0:T(8,128)S(1)} %get-tuple-element.13.coarse, f32[88,128]{1,0:T(8,128)S(1)} %collective-permute-done.2.from_n, f32[88,128]{1,0:T(8,128)S(1)} %collective-permute-done.3.from_f, f32[32,1024]{1,0:T(8,128)S(1)} %pad_maximum_fusion.ends, ...), custom_call_target="tpu_custom_call" | custom-call | tf_op jit(solution)/shard_map/inflow/pallas_call | solution.py:392
  (2 shorter events, 0.0 us)
Async XLA Ops:
  0.0 1.0 %copy-start = (f32[128,1024]{1,0:T(8,128)S(1)}, f32[128,1024]{1,0:T(8,128)}, u32[]{:S(2)}) copy-start(f32[128,1024]{1,0:T(8,128)} %el.3) | copy-start | bytes 1572868
  1.0 1.0 %copy-start.2 = (s32[128,1024]{1,0:T(8,128)S(1)}, s32[128,1024]{1,0:T(8,128)}, u32[]{:S(2)}) copy-start(s32[128,1024]{1,0:T(8,128)} %mk.3) | copy-start | bytes 1572868
  2.1 23.1 %copy-start.3 = (s32[128,1024]{1,0:T(8,128)S(1)}, s32[128,1024]{1,0:T(8,128)}, u32[]{:S(2)}) copy-start(s32[128,1024]{1,0:T(8,128)} %mk.3) | copy-start | bytes 1572868
  2.5 8.9 %collective-permute-start.1 = (f32[40,128]{1,0:T(8,128)S(1)}, f32[40,128]{1,0:T(8,128)S(1)}, u32[]{:S(2)}, u32[]{:S(2)}) collective-permute-start(f32[40,128]{1,0:T(8,128)S(1)} %get-tuple-element.11.own), channel_id=1, source_target_pairs={{0,15},{1,2},{2,1},{3,4},{4,3},{5,6},{6,5},{7,8},{8,7},{9,10},{10,... | collective-permute-start | bytes 61448 | tf_op jit(solution)/shard_map/ppermute | solution.py:342
  10.2 2.9 %collective-permute-start = (f32[40,128]{1,0:T(8,128)S(1)}, f32[40,128]{1,0:T(8,128)S(1)}, u32[]{:S(2)}, u32[]{:S(2)}) collective-permute-start(f32[40,128]{1,0:T(8,128)S(1)} %get-tuple-element.11.own), channel_id=1, source_target_pairs={{0,1},{1,0},{2,3},{3,2},{4,5},{5,4},{6,7},{7,6},{8,9},{9,8},{10,11... | collective-permute-start | bytes 61448 | tf_op jit(solution)/shard_map/ppermute | solution.py:342
  13.2 12.0 %collective-permute-start.2 = (f32[88,128]{1,0:T(8,128)S(1)}, f32[88,128]{1,0:T(8,128)S(1)}, u32[]{:S(2)}, u32[]{:S(2)}) collective-permute-start(f32[88,128]{1,0:T(8,128)S(1)} %get-tuple-element.14), channel_id=1, source_target_pairs={{0,16},{16,0},{32,48},{48,32},{64,80},{80,64},{96,112},{112,96},{1... | collective-permute-start | bytes 135176 | tf_op jit(solution)/shard_map/ppermute | solution.py:342
  15.1 10.1 %collective-permute-start.3 = (f32[88,128]{1,0:T(8,128)S(1)}, f32[88,128]{1,0:T(8,128)S(1)}, u32[]{:S(2)}, u32[]{:S(2)}) collective-permute-start(f32[88,128]{1,0:T(8,128)S(1)} %get-tuple-element.15), channel_id=1, source_target_pairs={{0,240},{16,32},{32,16},{48,64},{64,48},{80,96},{96,80},{112,128},... | collective-permute-start | bytes 135176 | tf_op jit(solution)/shard_map/ppermute | solution.py:342
  19.3 1.0 %copy-start.1 = (f32[128,1024]{1,0:T(8,128)S(1)}, f32[128,1024]{1,0:T(8,128)}, u32[]{:S(2)}) copy-start(f32[128,1024]{1,0:T(8,128)} %el.3) | copy-start | bytes 1572868
  20.4 0.7 %copy-start.4 = (s32[8]{0:T(128)S(1)}, s32[8]{0:T(128)}, u32[]{:S(2)}) copy-start(s32[8]{0:T(128)} %tie.3) | copy-start | bytes 100

commit v2 on v1

v2 whole, which is shorter than its diff:
```python
import jax
import jax.numpy as jnp
from jax import lax
from jax.experimental import pallas as pl
from jax.experimental.pallas import tpu as pltpu
from jax.sharding import PartitionSpec as P

ITERS = 8
OFFSETS = ((0, 1), (1, 1), (1, 0), (1, -1), (0, -1), (-1, -1), (-1, 0), (-1, 1))
DIAGONAL = 0.7071067811865476
RETENTION = 0.1
OUTSIDE = 1e30
LANES = 128
VMEM = pltpu.VMEM
LIMIT = 40 * 1024 * 1024


def iota(shape, dim):
    return lax.broadcasted_iota(jnp.int32, shape, dim)


def coefficients(tie_ref, coef_ref):
    for place in range(8):
        k = tie_ref[place]
        value = 1.0 + 0.5 * (7.0 - place) / 7.0
        scaled = jnp.where(k % 2 == 0, value, value * DIAGONAL).astype(jnp.float32)
        coef_ref[pl.ds(k, 1), :] = jnp.full((1, LANES), scaled)


def coefficient_tiles(coef_ref):
    return [jnp.broadcast_to(coef_ref[k : k + 1, :], (8, LANES)) for k in range(8)]


def neighbour(planes, j, row, k):
    step_row, step_col = OFFSETS[k]
    ref = planes[{0: 0, -1: 1, 1: 2}[step_col]]
    return ref[j, pl.ds(row + step_row, 8), :]


def spread(planes, wanted, row, ring=None):
    centre, west, east = planes
    lane = iota((8, LANES), 1)
    at = pl.ds(row, 8)
    ring = ring or (lambda j: j)
    to_east, to_west = {}, {}
    for j in wanted:
        for i in (ring(j - 1), j):
            if i not in to_east:
                to_east[i] = pltpu.roll(centre[i, at, :], 1, 1)
        for i in (j, ring(j + 1)):
            if i not in to_west:
                to_west[i] = pltpu.roll(centre[i, at, :], LANES - 1, 1)
        west[j, at, :] = jnp.where(lane == 0, to_east[ring(j - 1)], to_east[j])
        east[j, at, :] = jnp.where(lane == LANES - 1, to_west[ring(j + 1)], to_west[j])


def reciprocal_total(planes, j, row, coef):
    z = planes[0][j, pl.ds(row, 8), :]
    parts = [coef[k] * jnp.maximum(z - neighbour(planes, j, row, k), 0.0) for k in range(8)]
    total = ((parts[0] + parts[1]) + (parts[2] + parts[3])) + ((parts[4] + parts[5]) + (parts[6] + parts[7]))
    return 1.0 / (total + RETENTION)


def inward(planes, j, row, k, coef):
    z = planes[0][j, pl.ds(row, 8), :]
    return coef[(k + 4) % 8] * jnp.maximum(neighbour(planes, j, row, k) - z, 0.0)


def fields(z_planes, r_planes, j, row, coef, top=0, bottom=7):
    lane = iota((8, LANES), 1) % 8
    sub = iota((8, LANES), 0)
    at_east, at_west = lane == 7, lane == 0
    first, last = sub == top, sub == bottom
    t = [inward(z_planes, j, row, k, coef) * neighbour(r_planes, j, row, k) for k in range(8)]

    def split(east, west):
        own = jnp.where(at_east, west, jnp.where(at_west, east, east + west))
        other = jnp.where(at_east, east, jnp.where(at_west, west, 0.0))
        return own, other

    own0, other0 = split(t[0], t[4])
    own_down, other_down = split(t[1], t[3])
    own_down = own_down + t[2]
    own_up, other_up = split(t[7], t[5])
    own_up = own_up + t[6]
    a00 = own0 + jnp.where(first, 0.0, own_up) + jnp.where(last, 0.0, own_down)
    a01 = other0 + jnp.where(first, 0.0, other_up) + jnp.where(last, 0.0, other_down)
    a10 = jnp.where(first, own_up, jnp.where(last, own_down, 0.0))
    a11 = jnp.where(first, other_up, jnp.where(last, other_down, 0.0))
    return a00, a01, a10, a11


def block_rows(tiles):
    sub = iota(tiles[0].shape, 0)
    level = [tiles[t] for t in (0, 4, 2, 6, 1, 5, 3, 7)]
    for shift in (4, 2, 1):
        low = (sub & shift) == 0
        level = [
            jnp.where(low, a + pltpu.roll(a, 8 - shift, 0), b + pltpu.roll(b, shift, 0))
            for a, b in zip(level[0::2], level[1::2])
        ]
    return level[0]


PIECES = 4
PARTS = 4


def overview_kernel(tie_hbm, el_hbm, mk_hbm, msg, el, mk, coef, tie, tie_sem, el_sem, mk_sem):
    rows, cols = el.shape
    chunks = cols // LANES
    size = rows // PIECES
    fetch = []
    for p in range(PIECES):
        at = pl.ds(p * size, size)
        fetch.append(
            (
                pltpu.make_async_copy(el_hbm.at[at, :], el.at[at, :], el_sem.at[p]),
                pltpu.make_async_copy(mk_hbm.at[at, :], mk.at[at, :], mk_sem.at[p]),
            )
        )
    for pair in fetch:
        for copy in pair:
            copy.start()
    tie_copy = pltpu.make_async_copy(tie_hbm, tie, tie_sem)
    tie_copy.start()
    col = iota((cols, LANES), 0) // 8
    pick = jnp.where(col == iota((cols, LANES), 1), 1.0, 0.0).astype(jnp.bfloat16)
    tie_copy.wait()
    coefficients(tie, coef)
    sums, counts = [], []
    waited = 0
    for g in range(rows // 64):
        while waited * size < 64 * (g + 1):
            for copy in fetch[waited]:
                copy.wait()
            waited += 1
        s_parts, n_parts = [], []
        for j in range(chunks):
            s_tiles, n_tiles = [], []
            for t in range(8):
                at = (slice(64 * g + 8 * t, 64 * g + 8 * t + 8), slice(LANES * j, LANES * j + LANES))
                m = mk[at].astype(jnp.float32)
                n_tiles.append(m)
                s_tiles.append(m * el[at])
            s_parts.append(block_rows(s_tiles))
            n_parts.append(block_rows(n_tiles))
        sums.append(jnp.concatenate(s_parts, axis=1))
        counts.append(jnp.concatenate(n_parts, axis=1))
    s = jnp.concatenate(sums, axis=0)
    n = jnp.concatenate(counts, axis=0)
    hi = s.astype(jnp.bfloat16)
    rest = s - hi.astype(jnp.float32)
    mid = rest.astype(jnp.bfloat16)
    low = (rest - mid.astype(jnp.float32)).astype(jnp.bfloat16)
    left = jnp.concatenate([hi, mid, low, n.astype(jnp.bfloat16)], axis=0)
    out = lax.dot_general(left, pick, (((1,), (0,)), ((), ())), preferred_element_type=jnp.float32)
    k = rows // 8
    summed = out[0:k] + (out[k : 2 * k] + out[2 * k : 3 * k])
    count = out[3 * k : 4 * k]
    msg[0:k, :] = summed / (count + 1.0)
    msg[k : 2 * k, :] = count * (1.0 / 64.0)
    first = jnp.transpose(el[:, 0:LANES])
    last = jnp.transpose(el[:, cols - LANES : cols])
    msg[2 * k : 2 * k + 4, :] = first[0:4]
    msg[2 * k + 4 : 2 * k + 8, :] = last[LANES - 4 : LANES]


def row_message_kernel(own, from_a, from_b, el, coarse, side, to_n, to_f):
    k = (own.shape[0] - 8) // 2
    rows, cols = el.shape
    chunks = cols // LANES
    r, c = lax.axis_index("rows"), lax.axis_index("cols")
    count = lax.axis_size("cols")
    even = c % 2 == 0
    shape = own.shape
    a, b = from_a[...], from_b[...]
    line = iota(shape, 0)
    missing = jnp.where((line >= k) & (line < 2 * k), 0.0, OUTSIDE)
    right = jnp.where(jnp.full(shape, c == count - 1), missing, jnp.where(jnp.full(shape, even), a, b))
    left = jnp.where(jnp.full(shape, c == 0), missing, jnp.where(jnp.full(shape, even), b, a))
    lane = iota((2 * k, LANES), 1)
    near = jnp.where(lane < LANES // 2, right[0 : 2 * k], left[0 : 2 * k])
    mine = own[...]
    c4 = (mine[0:k], near[0:k], mine[k : 2 * k], near[k : 2 * k])
    for i, part in enumerate(c4):
        coarse[i * k : (i + 1) * k, :] = part
        to_n[i * k : (i + 1) * k, :] = part
        to_f[i * k : (i + 1) * k, :] = part
    cols_t = jnp.concatenate(
        [right[2 * k : 2 * k + 4], jnp.zeros((LANES - 8, LANES), jnp.float32), left[2 * k + 4 : 2 * k + 8]], axis=0
    )
    beyond = jnp.transpose(cols_t)
    side[...] = beyond
    upper = r % 2 == 0
    for j in range(chunks + 1):
        if j < chunks:
            lanes = slice(LANES * j, LANES * j + LANES)
            top, bottom = el[0:2, lanes], el[rows - 2 : rows, lanes]
        else:
            top, bottom = beyond[0:2], beyond[rows - 2 : rows]
        cond = jnp.full((2, LANES), upper)
        to_n[4 * k + 2 * j : 4 * k + 2 * j + 2, :] = jnp.where(cond, bottom, top)
        to_f[4 * k + 2 * j : 4 * k + 2 * j + 2, :] = jnp.where(cond, top, bottom)


def middle_kernel(coefs, el, out, recip, zc, zw, ze, rc, rw, re):
    rows, cols = el.shape
    chunks = cols // LANES
    coef = coefficient_tiles(coefs)
    z_planes, r_planes = (zc, zw, ze), (rc, rw, re)
    inner, core = range(1, chunks - 1), range(2, chunks - 2)
    blank = jnp.zeros((8, LANES), jnp.float32)
    for at in (0, rows + 8):
        for j in inner:
            for ref in z_planes + r_planes:
                ref[j, at : at + 8, :] = blank

    def lift(t, carry):
        row = pl.multiple_of(8 + 8 * t, 8)
        for j in range(chunks):
            zc[j, pl.ds(row, 8), :] = el[pl.ds(pl.multiple_of(8 * t, 8), 8), LANES * j : LANES * j + LANES]
        spread(z_planes, inner, row)
        return carry

    lax.fori_loop(0, rows // 8, lift, 0)

    def totals(t, carry):
        row = pl.multiple_of(8 + 8 * t, 8)
        for j in inner:
            total = reciprocal_total(z_planes, j, row, coef)
            rc[j, pl.ds(row, 8), :] = total
            recip[j - 1, pl.ds(pl.multiple_of(8 * t, 8), 8), :] = total
        spread(r_planes, core, row)
        return carry

    lax.fori_loop(0, rows // 8, totals, 0)

    def combine(t, carry):
        row = pl.multiple_of(8 + 8 * t, 8)
        for j in core:
            for i, field in enumerate(fields(z_planes, r_planes, j, row, coef)):
                out[i, j - 2, pl.ds(pl.multiple_of(8 * t, 8), 8), :] = field
        return carry

    lax.fori_loop(0, rows // 8, combine, 0)


def outer_kernel(coefs, el, side, known, out, recip, zc, zw, ze, rc, rw, re):
    rows, cols = el.shape
    chunks = cols // LANES
    coef = coefficient_tiles(coefs)
    z_planes, r_planes = (zc, zw, ze), (rc, rw, re)
    order = (chunks - 3, chunks - 2, chunks - 1, chunks, 0, 1, 2)
    blank = jnp.zeros((8, LANES), jnp.float32)
    for at in (0, rows + 8):
        for i in range(1, 6):
            for ref in z_planes + r_planes:
                ref[i, at : at + 8, :] = blank

    def lift(t, carry):
        row = pl.multiple_of(8 + 8 * t, 8)
        at = pl.ds(pl.multiple_of(8 * t, 8), 8)
        for i, j in enumerate(order):
            zc[i, pl.ds(row, 8), :] = el[at, LANES * j : LANES * j + LANES] if j < chunks else side[at, :]
        spread(z_planes, range(1, 6), row)
        return carry

    lax.fori_loop(0, rows // 8, lift, 0)

    def totals(t, carry):
        row = pl.multiple_of(8 + 8 * t, 8)
        at = pl.ds(pl.multiple_of(8 * t, 8), 8)
        for i, j in enumerate(order):
            if i in (2, 3, 4):
                total = reciprocal_total(z_planes, i, row, coef)
                recip[i - 2, at, :] = total
            else:
                total = known[j - 1, at, :]
            rc[i, pl.ds(row, 8), :] = total
        spread(r_planes, (1, 2, 4, 5), row)
        return carry

    lax.fori_loop(0, rows // 8, totals, 0)

    def combine(t, carry):
        row = pl.multiple_of(8 + 8 * t, 8)
        for n, i in enumerate((4, 5, 1, 2)):
            for which, field in enumerate(fields(z_planes, r_planes, i, row, coef)):
                out[which, n, pl.ds(pl.multiple_of(8 * t, 8), 8), :] = field
        return carry

    lax.fori_loop(0, rows // 8, combine, 0)


def inflow_kernel(
    coefs, coarse, from_n, from_f, el, side, middle, outer, middle_recip, outer_recip, mk, out_hbm,
    kc, kw, ke, sc, sw, se, run, gain, flow, zc, zw, ze, rc, rw, re, up_ref, vv_ref, out, out_sem,
):
    k = coarse.shape[0] // 4
    rows, cols = mk.shape
    chunks = cols // LANES
    r, count = lax.axis_index("rows"), lax.axis_size("rows")
    upper = r % 2 == 0
    coef = coefficient_tiles(coefs)
    n, f = from_n[...], from_f[...]
    shape = n.shape
    line = iota(shape, 0)
    missing = jnp.where((line >= 2 * k) & (line < 4 * k), 0.0, OUTSIDE)
    cond = jnp.full(shape, upper)
    above = jnp.where(jnp.full(shape, r == 0), missing, jnp.where(cond, f, n))
    below = jnp.where(jnp.full(shape, r == count - 1), missing, jnp.where(cond, n, f))

    k_planes, s_planes = (kc, kw, ke), (sc, sw, se)
    around = lambda size: (lambda j: j % size)
    for j in range(2):
        kc[j, 0:8, :] = jnp.zeros((8, LANES), jnp.float32)
        kc[j, 8 + 3 * k : 16 + 3 * k, :] = jnp.zeros((8, LANES), jnp.float32)
        for ref, base, first in ((kc, 0, 8), (run, 2 * k, 0)):
            lo = base + j * k
            ref[j, first : first + k, :] = above[lo : lo + k]
            ref[j, first + k : first + 2 * k, :] = coarse[lo : lo + k, :]
            ref[j, first + 2 * k : first + 3 * k, :] = below[lo : lo + k]
    for t in range(3 * k // 8 + 2):
        spread(k_planes, range(2), 8 * t, around(2))
    recip = {}
    for j in range(2):
        for t in range(3 * k // 8):
            recip[j, t] = reciprocal_total(k_planes, j, 8 + 8 * t, coef)
    inner = range(1, 3 * k // 8 - 1)
    for j in range(2):
        for t in inner:
            for d in range(8):
                gain[d, j, 8 * t : 8 * t + 8, :] = inward(k_planes, j, 8 + 8 * t, d, coef)

    z_planes, r_planes = (zc, zw, ze), (rc, rw, re)
    ring = around(chunks + 1)
    every = range(chunks + 1)
    for j in every:
        up2, down2 = above[4 * k + 2 * j : 4 * k + 2 * j + 2], below[4 * k + 2 * j : 4 * k + 2 * j + 2]
        if j < chunks:
            first, last = el[0:8, LANES * j : LANES * j + LANES], el[rows - 8 : rows, LANES * j : LANES * j + LANES]
        else:
            first, last = side[0:8, :], side[rows - 8 : rows, :]
        blank = jnp.zeros((8, LANES), jnp.float32)
        for at in (0, 16, 32):
            zc[j, at : at + 8, :] = blank
        zc[j, 8:16, :] = jnp.concatenate([up2, first[0:2], last[6:8], down2], axis=0)
        zc[j, 24:32, :] = jnp.concatenate([up2[1:2], first[0:3], last[5:8], down2[0:1]], axis=0)
    for row in (0, 8, 16, 24, 32):
        spread(z_planes, every, row, ring)
    for j in every:
        total = reciprocal_total(z_planes, j, 8, coef)
        if 1 <= j < chunks - 1:
            near = middle_recip.at[j - 1]
        else:
            near = outer_recip.at[{chunks - 1: 0, chunks: 1, 0: 2}[j]]
        first, last = near[0:8, :], near[rows - 8 : rows, :]
        for at in (0, 16):
            rc[j, at : at + 8, :] = jnp.zeros((8, LANES), jnp.float32)
        rc[j, 8:16, :] = jnp.concatenate([total[1:3], first[1:3], last[5:7], total[5:7]], axis=0)
    for row in (0, 8, 16):
        spread(r_planes, every, row, ring)
    border = {}
    for j in range(chunks):
        border[j] = fields((zc.at[:, 16:40, :], zw.at[:, 16:40, :], ze.at[:, 16:40, :]), r_planes, j, 8, coef, 1, 6)

    for j in range(2):
        for t in range(3 * k // 8):
            sc[j, 8 * t : 8 * t + 8, :] = recip[j, t] * run[j, 8 * t : 8 * t + 8, :]
    for t in range(3 * k // 8):
        spread(s_planes, range(2), 8 * t, around(2))
    for sweep in range(ITERS):
        for j in range(2):
            for t in inner:
                parts = [gain[d, j, 8 * t : 8 * t + 8, :] * neighbour(s_planes, j, 8 * t, d) for d in range(8)]
                total = ((parts[0] + parts[1]) + (parts[2] + parts[3])) + (
                    (parts[4] + parts[5]) + (parts[6] + parts[7])
                )
                flow[j, 8 * t : 8 * t + 8, :] = run[j, 8 * t : 8 * t + 8, :] + total
        if sweep < ITERS - 1:
            for j in range(2):
                for t in inner:
                    sc[j, 8 * t : 8 * t + 8, :] = recip[j, t] * flow[j, 8 * t : 8 * t + 8, :]
            for t in inner:
                spread(s_planes, range(2), 8 * t, around(2))

    lane = iota((8, LANES), 1)
    block = lane // 8
    step = jnp.where(lane % 8 == 7, 1, jnp.where(lane % 8 == 0, -1, 0))
    per = LANES // 8
    for t in inner:
        main = flow[0, 8 * t : 8 * t + 8, :]
        apart = flow[1, 8 * t : 8 * t + 8, :]
        for j in range(chunks):
            here = block + per * j
            over = here + step
            up_ref[j, 8 * t : 8 * t + 8, :] = jnp.take_along_axis(main, here, axis=1, mode="promise_in_bounds")
            v = jnp.take_along_axis(main, over & (LANES - 1), axis=1, mode="promise_in_bounds")
            if j == 0:
                far = jnp.take_along_axis(apart, over & (LANES - 1), axis=1, mode="promise_in_bounds")
                v = jnp.where(lane == 0, far, v)
            if j == chunks - 1:
                far = jnp.take_along_axis(apart, over & (LANES - 1), axis=1, mode="promise_in_bounds")
                v = jnp.where(lane == LANES - 1, far, v)
            vv_ref[j, 8 * t : 8 * t + 8, :] = v

    sub = iota((8, LANES), 0)
    high = sub < 4
    writes = []
    for b in range(rows // 8):
        for j in range(chunks):
            lanes = slice(LANES * j, LANES * j + LANES)
            at = slice(8 * b, 8 * b + 8)
            row = k + b
            wide = [jnp.broadcast_to(up_ref[j, row + i : row + i + 1, :], (8, LANES)) for i in (-1, 0, 1)]
            apart = [jnp.broadcast_to(vv_ref[j, row + i : row + i + 1, :], (8, LANES)) for i in (-1, 0, 1)]
            if 2 <= j < chunks - 2:
                a = [middle[i, j - 2, at, :] for i in range(4)]
            else:
                a = [outer[i, j if j < 2 else j - chunks + 4, at, :] for i in range(4)]
            if b == 0:
                a = [jnp.where(sub < 2, pltpu.roll(border[j][i], 7, 0), a[i]) for i in range(4)]
            if b == rows // 8 - 1:
                a = [jnp.where(sub > 5, pltpu.roll(border[j][i], 1, 0), a[i]) for i in range(4)]
            out[at, lanes] = mk[at, lanes].astype(jnp.float32) + (
                (a[0] * wide[1] + a[1] * apart[1])
                + (a[2] * jnp.where(high, wide[0], wide[2]) + a[3] * jnp.where(high, apart[0], apart[2]))
            )
        size = rows // PARTS
        if (8 * b + 8) % size == 0:
            p = 8 * b // size
            lines = pl.ds(p * size, size)
            copy = pltpu.make_async_copy(out.at[lines, :], out_hbm.at[lines, :], out_sem.at[p])
            copy.start()
            writes.append(copy)
    for copy in writes:
        copy.wait()


def swap(x, axis, far):
    count = lax.axis_size(axis)
    if far:
        pairs = [(i, (i + 1) % count if i % 2 else (i - 1) % count) for i in range(count)]
    else:
        pairs = [(i, i ^ 1) for i in range(count)]
    return lax.ppermute(x, axis, pairs)


def f32(*shape):
    return jax.ShapeDtypeStruct(shape, jnp.float32)


def whole(count):
    return [pl.BlockSpec(memory_space=VMEM)] * count


def on_device(elevation, data_mask, tie_order):
    rows, cols = elevation.shape
    k, chunks = rows // 8, cols // LANES
    params = pltpu.CompilerParams(vmem_limit_bytes=LIMIT)
    dma = pltpu.SemaphoreType.DMA
    hbm = pl.BlockSpec(memory_space=pltpu.HBM)
    msg, el, mk, coefs = pl.pallas_call(
        overview_kernel,
        out_shape=[f32(2 * k + 8, LANES), f32(rows, cols), jax.ShapeDtypeStruct((rows, cols), jnp.int32), f32(8, LANES)],
        in_specs=[hbm] * 3,
        out_specs=whole(4),
        scratch_shapes=[pltpu.SMEM((8,), jnp.int32), dma, dma((PIECES,)), dma((PIECES,))],
        compiler_params=params,
        name="overview",
    )(tie_order, elevation, data_mask)
    from_b = swap(msg, "cols", True)
    from_a = swap(msg, "cols", False)
    plane = lambda count, height: VMEM((count, height, LANES), jnp.float32)
    cost = pl.CostEstimate(flops=10_000_000, bytes_accessed=3_000_000, transcendentals=0)
    middle, middle_recip = pl.pallas_call(
        middle_kernel,
        out_shape=[f32(4, chunks - 4, rows, LANES), f32(chunks - 2, rows, LANES)],
        in_specs=whole(2),
        out_specs=whole(2),
        scratch_shapes=[plane(chunks, rows + 16)] * 6,
        compiler_params=params,
        cost_estimate=cost,
        name="middle_fields",
    )(coefs, el)
    size = 4 * k + 24
    coarse, side, to_n, to_f = pl.pallas_call(
        row_message_kernel,
        out_shape=[f32(4 * k, LANES), f32(rows, LANES), f32(size, LANES), f32(size, LANES)],
        in_specs=whole(4),
        out_specs=whole(4),
        compiler_params=params,
        name="row_message",
    )(msg, from_a, from_b, el)
    from_n = swap(to_n, "rows", False)
    from_f = swap(to_f, "rows", True)
    outer, outer_recip = pl.pallas_call(
        outer_kernel,
        out_shape=[f32(4, 4, rows, LANES), f32(3, rows, LANES)],
        in_specs=whole(4),
        out_specs=whole(2),
        scratch_shapes=[plane(7, rows + 16)] * 6,
        compiler_params=params,
        cost_estimate=cost,
        name="outer_fields",
    )(coefs, el, side, middle_recip)
    return pl.pallas_call(
        inflow_kernel,
        out_shape=f32(rows, cols),
        in_specs=whole(11),
        out_specs=hbm,
        scratch_shapes=[plane(2, 3 * k + 16)] * 3
        + [plane(2, 3 * k)] * 4
        + [VMEM((8, 2, 3 * k, LANES), jnp.float32), plane(2, 3 * k)]
        + [plane(chunks + 1, 40)] * 3
        + [plane(chunks + 1, 24)] * 3
        + [plane(chunks, 3 * k)] * 2
        + [VMEM((rows, cols), jnp.float32), dma((PARTS,))],
        compiler_params=params,
        name="inflow",
    )(coefs, coarse, from_n, from_f, el, side, middle, outer, middle_recip, outer_recip, mk)


def solution(mesh):
    in_specs = (P("rows", "cols"), P("rows", "cols"), P())
    out_specs = P("rows", "cols")
    return jax.shard_map(
        on_device, mesh=mesh, in_specs=in_specs, out_specs=out_specs, check_vma=False
    )
```

time: 29 us -> 31.6 us (1.090)
  Pallas kernels: 8.23 us -> 11.9 us
  local copies, waits for them, and re-layouts: 3.79 us -> 2.74 us
    pallas_call x3 -> x4, Pallas kernels: 8.12 us -> 11.8 us  [the longest x1 3.72 us: on_device(): pl.pallas_call(middle_kernel, out_shape=[f32(4, chunks - 4, rows, LANES),...]
    unnamed x10 -> x6, local copies, waits for them, and re-layouts: 3.78 us -> 2.74 us
  transfers between devices with their start and end apart: 4 -> 4, of which waited for: 2 -> 2; matrix products, arithmetic and copies ran while one was open for 0% -> 0% of each run, Pallas kernels for 14% -> 23%
where the time goes in v2:
time: 31.6 us; the launch traced here: 31.4 us
  starting transfers between devices  13.8 us (44%)
  Pallas kernels  11.9 us (38%)
  waiting for transfers between devices  2.91 us (9%)
  local copies, waits for them, and re-layouts  2.74 us (9%)
    ppermute x4, starting transfers between devices, swap(): return lax.ppermute(x, axis, pairs)  13.8 us
    pallas_call x1, Pallas kernels, on_device(): pl.pallas_call(middle_kernel, out_shape=[f32(4, chunks - 4, rows, LANES),...  3.72 us
    pallas_call x1, Pallas kernels, on_device(): pl.pallas_call(outer_kernel, out_shape=[f32(4, 4, rows, LANES), f32(3, ro...  3.57 us
    ppermute x4, waiting for transfers between devices, swap(): return lax.ppermute(x, axis, pairs)  2.91 us
    unnamed x6, local copies, waits for them, and re-layouts  2.74 us
    pallas_call x1, Pallas kernels, on_device(): pl.pallas_call(overview_kernel, out_shape=[f32(2 * k + 8, LANES), f32(row...  2.36 us
    pallas_call x1, Pallas kernels, on_device(): pl.pallas_call(inflow_kernel, out_shape=f32(rows, cols), in_specs=whole(1...  2.14 us
  transfers between devices with their start and end apart: 4, of which 2 were waited for; matrix products, arithmetic and copies ran while one was open for 0% of the time, Pallas kernels for 23%

profile of v2, /device:TPU:1, one launch (start us, length us, event | category | flops | bytes accessed | tf_op | source)
XLA Modules:
  0.0 31.4 jit_solution(7342372396767289374)
XLA Ops:
  0.0 0.0 copy-start
  0.0 1.0 %copy-done = f32[128,1024]{1,0:T(8,128)S(1)} copy-done((f32[128,1024]{1,0:T(8,128)S(1)}, f32[128,1024]{1,0:T(8,128)}, u32[]{:S(2)}) %copy-start) | copy-done | bytes 524312
  1.0 0.0 copy-start.1
  1.0 1.0 %copy-done.1 = s32[128,1024]{1,0:T(8,128)S(1)} copy-done((s32[128,1024]{1,0:T(8,128)S(1)}, s32[128,1024]{1,0:T(8,128)}, u32[]{:S(2)}) %copy-start.1) | copy-done | bytes 524312
  2.1 0.0 copy-start.2
  2.1 0.7 %copy-done.2 = s32[8]{0:T(128)S(1)} copy-done((s32[8]{0:T(128)S(1)}, s32[8]{0:T(128)}, u32[]{:S(2)}) %copy-start.2) | copy-done | bytes 56
  2.7 2.4 %overview.1 = (f32[40,128]{1,0:T(8,128)S(1)}, f32[128,1024]{1,0:T(8,128)S(1)}, s32[128,1024]{1,0:T(8,128)S(1)}, f32[8,128]{1,0:T(8,128)S(1)}) custom-call(s32[8]{0:T(128)S(1)} %copy-done.2, f32[128,1024]{1,0:T(8,128)S(1)} %copy-done, s32[128,1024]{1,0:T(8,128)S(1)} %copy-done.1), custom_call_target="tpu_custom_call" | custom-call | tf_op jit(solution)/shard_map/overview/pallas_call | solution.py:464
  5.1 7.7 %collective-permute-start.1 = (f32[40,128]{1,0:T(8,128)S(1)}, f32[40,128]{1,0:T(8,128)S(1)}, u32[]{:S(2)}, u32[]{:S(2)}) collective-permute-start(f32[40,128]{1,0:T(8,128)S(1)} %get-tuple-element.18.own), channel_id=1, source_target_pairs={{0,15},{1,2},{2,1},{3,4},{4,3},{5,6},{6,5},{7,8},{8,7},{9,10},{10,... | collective-permute-start | bytes 61448 | tf_op jit(solution)/shard_map/ppermute | solution.py:447
  12.8 0.0 collective-permute-start
  12.8 1.2 %collective-permute-done.1.from_b = f32[40,128]{1,0:T(8,128)S(1)} collective-permute-done((f32[40,128]{1,0:T(8,128)S(1)}, f32[40,128]{1,0:T(8,128)S(1)}, u32[]{:S(2)}, u32[]{:S(2)}) %collective-permute-start.1) | collective-permute-done | bytes 20512 | tf_op jit(solution)/shard_map/ppermute | solution.py:447
  14.0 1.7 %collective-permute-done.from_a = f32[40,128]{1,0:T(8,128)S(1)} collective-permute-done((f32[40,128]{1,0:T(8,128)S(1)}, f32[40,128]{1,0:T(8,128)S(1)}, u32[]{:S(2)}, u32[]{:S(2)}) %collective-permute-start) | collective-permute-done | bytes 20512 | tf_op jit(solution)/shard_map/ppermute | solution.py:447
  15.7 0.1 row_message.1
  15.8 1.9 %collective-permute-start.2 = (f32[88,128]{1,0:T(8,128)S(1)}, f32[88,128]{1,0:T(8,128)S(1)}, u32[]{:S(2)}, u32[]{:S(2)}) collective-permute-start(f32[88,128]{1,0:T(8,128)S(1)} %get-tuple-element.21), channel_id=1, source_target_pairs={{0,16},{16,0},{32,48},{48,32},{64,80},{80,64},{96,112},{112,96},{1... | collective-permute-start | bytes 135176 | tf_op jit(solution)/shard_map/ppermute | solution.py:447
  17.8 4.2 %collective-permute-start.3 = (f32[88,128]{1,0:T(8,128)S(1)}, f32[88,128]{1,0:T(8,128)S(1)}, u32[]{:S(2)}, u32[]{:S(2)}) collective-permute-start(f32[88,128]{1,0:T(8,128)S(1)} %get-tuple-element.22), channel_id=1, source_target_pairs={{0,240},{16,32},{32,16},{48,64},{64,48},{80,96},{96,80},{112,128},... | collective-permute-start | bytes 135176 | tf_op jit(solution)/shard_map/ppermute | solution.py:447
  22.0 3.7 %middle_fields.1 = (f32[4,4,128,128]{3,2,1,0:T(8,128)S(1)}, f32[6,128,128]{2,1,0:T(8,128)S(1)}) custom-call(f32[8,128]{1,0:T(8,128)S(1)} %get-tuple-element.17.coefs, f32[128,1024]{1,0:T(8,128)S(1)} %get-tuple-element.19.el), custom_call_target="tpu_custom_call" | custom-call | flops 10000000 | bytes 3000000 | tf_op jit(solution)/shard_map/middle_fields/pallas_call | solution.py:477
  25.7 3.6 %outer_fields.1 = (f32[4,4,128,128]{3,2,1,0:T(8,128)S(1)}, f32[3,128,128]{2,1,0:T(8,128)S(1)}) custom-call(f32[8,128]{1,0:T(8,128)S(1)} %get-tuple-element.17.coefs, f32[128,1024]{1,0:T(8,128)S(1)} %get-tuple-element.19.el, f32[128,128]{1,0:T(8,128)S(1)} %get-tuple-element.23.side, f32[6,128,128]{2,1,0:T(8,128)S(1)} %get-tuple-element.25.known.middle_recip), custom_call_target="tpu_custom_call" | custom-call | flops 10000000 | bytes 3000000 | tf_op jit(solution)/shard_map/outer_fields/pallas_call | solution.py:498
  29.3 0.0 collective-permute-done.2.from_n
  29.3 0.0 collective-permute-done.3.from_f
  29.3 2.1 %inflow.1 = f32[128,1024]{1,0:T(8,128)} custom-call(f32[8,128]{1,0:T(8,128)S(1)} %get-tuple-element.17.coefs, f32[64,128]{1,0:T(8,128)S(1)} %get-tuple-element.20.coarse, f32[88,128]{1,0:T(8,128)S(1)} %collective-permute-done.2.from_n, f32[88,128]{1,0:T(8,128)S(1)} %collective-permute-done.3.from_f, f32[128,1024]{1,0:T(8,128)S(1)} %get-tuple-element.19.el, ...), custom_call_target="tpu_custom_call" | custom-call | tf_op jit(solution)/shard_map/inflow/pallas_call | solution.py:508
Async XLA Ops:
  0.0 1.0 %copy-start = (f32[128,1024]{1,0:T(8,128)S(1)}, f32[128,1024]{1,0:T(8,128)}, u32[]{:S(2)}) copy-start(f32[128,1024]{1,0:T(8,128)} %el_hbm.1) | copy-start | bytes 1572868
  1.0 1.0 %copy-start.1 = (s32[128,1024]{1,0:T(8,128)S(1)}, s32[128,1024]{1,0:T(8,128)}, u32[]{:S(2)}) copy-start(s32[128,1024]{1,0:T(8,128)} %mk_hbm.1) | copy-start | bytes 1572868
  2.1 0.7 %copy-start.2 = (s32[8]{0:T(128)S(1)}, s32[8]{0:T(128)}, u32[]{:S(2)}) copy-start(s32[8]{0:T(128)} %tie_hbm.1) | copy-start | bytes 100
  5.1 8.9 %collective-permute-start.1 = (f32[40,128]{1,0:T(8,128)S(1)}, f32[40,128]{1,0:T(8,128)S(1)}, u32[]{:S(2)}, u32[]{:S(2)}) collective-permute-start(f32[40,128]{1,0:T(8,128)S(1)} %get-tuple-element.18.own), channel_id=1, source_target_pairs={{0,15},{1,2},{2,1},{3,4},{4,3},{5,6},{6,5},{7,8},{8,7},{9,10},{10,... | collective-permute-start | bytes 61448 | tf_op jit(solution)/shard_map/ppermute | solution.py:447
  12.8 2.9 %collective-permute-start = (f32[40,128]{1,0:T(8,128)S(1)}, f32[40,128]{1,0:T(8,128)S(1)}, u32[]{:S(2)}, u32[]{:S(2)}) collective-permute-start(f32[40,128]{1,0:T(8,128)S(1)} %get-tuple-element.18.own), channel_id=1, source_target_pairs={{0,1},{1,0},{2,3},{3,2},{4,5},{5,4},{6,7},{7,6},{8,9},{9,8},{10,11... | collective-permute-start | bytes 61448 | tf_op jit(solution)/shard_map/ppermute | solution.py:447
  15.8 13.4 %collective-permute-start.2 = (f32[88,128]{1,0:T(8,128)S(1)}, f32[88,128]{1,0:T(8,128)S(1)}, u32[]{:S(2)}, u32[]{:S(2)}) collective-permute-start(f32[88,128]{1,0:T(8,128)S(1)} %get-tuple-element.21), channel_id=1, source_target_pairs={{0,16},{16,0},{32,48},{48,32},{64,80},{80,64},{96,112},{112,96},{1... | collective-permute-start | bytes 135176 | tf_op jit(solution)/shard_map/ppermute | solution.py:447
  17.8 11.5 %collective-permute-start.3 = (f32[88,128]{1,0:T(8,128)S(1)}, f32[88,128]{1,0:T(8,128)S(1)}, u32[]{:S(2)}, u32[]{:S(2)}) collective-permute-start(f32[88,128]{1,0:T(8,128)S(1)} %get-tuple-element.22), channel_id=1, source_target_pairs={{0,240},{16,32},{32,16},{48,64},{64,48},{80,96},{96,80},{112,128},... | collective-permute-start | bytes 135176 | tf_op jit(solution)/shard_map/ppermute | solution.py:447

commit v3 on v2

--- a/solution.py
+++ b/solution.py
@@ -102,7 +102,7 @@
     return level[0]
 
 
-PIECES = 4
+PIECES = 8
 PARTS = 4
 
 
@@ -166,7 +166,7 @@
     msg[2 * k + 4 : 2 * k + 8, :] = last[LANES - 4 : LANES]
 
 
-def row_message_kernel(own, from_a, from_b, el, coarse, side, to_n, to_f):
+def row_message_kernel(own, from_a, from_b, el, after, coarse, side, to_n, to_f):
     k = (own.shape[0] - 8) // 2
     rows, cols = el.shape
     chunks = cols // LANES
@@ -216,34 +216,25 @@
             for ref in z_planes + r_planes:
                 ref[j, at : at + 8, :] = blank
 
-    def lift(t, carry):
-        row = pl.multiple_of(8 + 8 * t, 8)
+    for t in range(rows // 8):
+        row = 8 + 8 * t
         for j in range(chunks):
-            zc[j, pl.ds(row, 8), :] = el[pl.ds(pl.multiple_of(8 * t, 8), 8), LANES * j : LANES * j + LANES]
+            zc[j, pl.ds(row, 8), :] = el[pl.ds(8 * t, 8), LANES * j : LANES * j + LANES]
         spread(z_planes, inner, row)
-        return carry
-
-    lax.fori_loop(0, rows // 8, lift, 0)
-
-    def totals(t, carry):
-        row = pl.multiple_of(8 + 8 * t, 8)
+
+    for t in range(rows // 8):
+        row = 8 + 8 * t
         for j in inner:
             total = reciprocal_total(z_planes, j, row, coef)
             rc[j, pl.ds(row, 8), :] = total
-            recip[j - 1, pl.ds(pl.multiple_of(8 * t, 8), 8), :] = total
+            recip[j - 1, pl.ds(8 * t, 8), :] = total
         spread(r_planes, core, row)
-        return carry
-
-    lax.fori_loop(0, rows // 8, totals, 0)
-
-    def combine(t, carry):
-        row = pl.multiple_of(8 + 8 * t, 8)
+
+    for t in range(rows // 8):
+        row = 8 + 8 * t
         for j in core:
             for i, field in enumerate(fields(z_planes, r_planes, j, row, coef)):
-                out[i, j - 2, pl.ds(pl.multiple_of(8 * t, 8), 8), :] = field
-        return carry
-
-    lax.fori_loop(0, rows // 8, combine, 0)
+                out[i, j - 2, pl.ds(8 * t, 8), :] = field
 
 
 def outer_kernel(coefs, el, side, known, out, recip, zc, zw, ze, rc, rw, re):
@@ -258,19 +249,16 @@
             for ref in z_planes + r_planes:
                 ref[i, at : at + 8, :] = blank
 
-    def lift(t, carry):
-        row = pl.multiple_of(8 + 8 * t, 8)
-        at = pl.ds(pl.multiple_of(8 * t, 8), 8)
+    for t in range(rows // 8):
+        row = 8 + 8 * t
+        at = pl.ds(8 * t, 8)
         for i, j in enumerate(order):
             zc[i, pl.ds(row, 8), :] = el[at, LANES * j : LANES * j + LANES] if j < chunks else side[at, :]
         spread(z_planes, range(1, 6), row)
-        return carry
-
-    lax.fori_loop(0, rows // 8, lift, 0)
-
-    def totals(t, carry):
-        row = pl.multiple_of(8 + 8 * t, 8)
-        at = pl.ds(pl.multiple_of(8 * t, 8), 8)
+
+    for t in range(rows // 8):
+        row = 8 + 8 * t
+        at = pl.ds(8 * t, 8)
         for i, j in enumerate(order):
             if i in (2, 3, 4):
                 total = reciprocal_total(z_planes, i, row, coef)
@@ -279,18 +267,12 @@
                 total = known[j - 1, at, :]
             rc[i, pl.ds(row, 8), :] = total
         spread(r_planes, (1, 2, 4, 5), row)
-        return carry
-
-    lax.fori_loop(0, rows // 8, totals, 0)
-
-    def combine(t, carry):
-        row = pl.multiple_of(8 + 8 * t, 8)
+
+    for t in range(rows // 8):
+        row = 8 + 8 * t
         for n, i in enumerate((4, 5, 1, 2)):
             for which, field in enumerate(fields(z_planes, r_planes, i, row, coef)):
-                out[which, n, pl.ds(pl.multiple_of(8 * t, 8), 8), :] = field
-        return carry
-
-    lax.fori_loop(0, rows // 8, combine, 0)
+                out[which, n, pl.ds(8 * t, 8), :] = field
 
 
 def inflow_kernel(
@@ -469,7 +451,7 @@
         scratch_shapes=[pltpu.SMEM((8,), jnp.int32), dma, dma((PIECES,)), dma((PIECES,))],
         compiler_params=params,
         name="overview",
-    )(tie_order, elevation, data_mask)
+    )(*(pltpu.with_memory_space_constraint(x, pltpu.HBM) for x in (tie_order, elevation, data_mask)))
     from_b = swap(msg, "cols", True)
     from_a = swap(msg, "cols", False)
     plane = lambda count, height: VMEM((count, height, LANES), jnp.float32)
@@ -488,11 +470,11 @@
     coarse, side, to_n, to_f = pl.pallas_call(
         row_message_kernel,
         out_shape=[f32(4 * k, LANES), f32(rows, LANES), f32(size, LANES), f32(size, LANES)],
-        in_specs=whole(4),
+        in_specs=whole(5),
         out_specs=whole(4),
         compiler_params=params,
         name="row_message",
-    )(msg, from_a, from_b, el)
+    )(msg, from_a, from_b, el, middle_recip)
     from_n = swap(to_n, "rows", False)
     from_f = swap(to_f, "rows", True)
     outer, outer_recip = pl.pallas_call(

time: 31.6 us -> 24.9 us (0.79)
  Pallas kernels: 11.9 us -> 6.24 us
  local copies, waits for them, and re-layouts: 2.74 us -> 0 us
  waiting for transfers between devices: 2.91 us -> 4.68 us
    unnamed x6 -> x0, local copies, waits for them, and re-layouts: 2.74 us -> none
    pallas_call x1, Pallas kernels: 3.57 us -> 1.02 us  [on_device(): pl.pallas_call(outer_kernel, out_shape=[f32(4, 4, rows, LANES), f32(3, ro...]
    pallas_call x1, Pallas kernels: 3.72 us -> 1.32 us  [on_device(): pl.pallas_call(middle_kernel, out_shape=[f32(4, chunks - 4, rows, LANES),...]
    ppermute x4, waiting for transfers between devices: 2.91 us -> 4.68 us  [swap(): return lax.ppermute(x, axis, pairs)]
    pallas_call x1, Pallas kernels: 2.36 us -> 1.66 us  [on_device(): pl.pallas_call(overview_kernel, out_shape=[f32(2 * k + 8, LANES), f32(row...]
  transfers between devices with their start and end apart: 4 -> 4, of which waited for: 2 -> 2; matrix products, arithmetic and copies ran while one was open for 0% -> 0% of each run, Pallas kernels for 23% -> 9%
where the time goes in v3:
time: 24.9 us; the launch traced here: 24.8 us
  starting transfers between devices  13.8 us (55%)
  Pallas kernels  6.24 us (25%)
  waiting for transfers between devices  4.68 us (19%)
    ppermute x4, starting transfers between devices, swap(): return lax.ppermute(x, axis, pairs)  13.8 us
    ppermute x4, waiting for transfers between devices, swap(): return lax.ppermute(x, axis, pairs)  4.68 us
    pallas_call x1, Pallas kernels, on_device(): pl.pallas_call(inflow_kernel, out_shape=f32(rows, cols), in_specs=whole(1...  2.13 us
    pallas_call x1, Pallas kernels, on_device(): pl.pallas_call(overview_kernel, out_shape=[f32(2 * k + 8, LANES), f32(row...  1.66 us
    pallas_call x1, Pallas kernels, on_device(): pl.pallas_call(middle_kernel, out_shape=[f32(4, chunks - 4, rows, LANES),...  1.32 us
    pallas_call x1, Pallas kernels, on_device(): pl.pallas_call(outer_kernel, out_shape=[f32(4, 4, rows, LANES), f32(3, ro...  1.02 us
  transfers between devices with their start and end apart: 4, of which 2 were waited for; matrix products, arithmetic and copies ran while one was open for 0% of the time, Pallas kernels for 9%

profile of v3, /device:TPU:1, one launch (start us, length us, event | category | flops | bytes accessed | tf_op | source)
XLA Modules:
  0.0 24.8 jit_solution(3915764622639639946)
XLA Ops:
  0.0 1.7 %overview.1 = (f32[40,128]{1,0:T(8,128)S(1)}, f32[128,1024]{1,0:T(8,128)S(1)}, s32[128,1024]{1,0:T(8,128)S(1)}, f32[8,128]{1,0:T(8,128)S(1)}) custom-call(s32[8]{0:T(128)} %tie_hbm.1, f32[128,1024]{1,0:T(8,128)} %el_hbm.1, s32[128,1024]{1,0:T(8,128)} %mk_hbm.1), custom_call_target="tpu_custom_call" | custom-call | tf_op jit(solution)/shard_map/overview/pallas_call | solution.py:446
  1.7 7.7 %collective-permute-start.1 = (f32[40,128]{1,0:T(8,128)S(1)}, f32[40,128]{1,0:T(8,128)S(1)}, u32[]{:S(2)}, u32[]{:S(2)}) collective-permute-start(f32[40,128]{1,0:T(8,128)S(1)} %get-tuple-element.18.own), channel_id=1, source_target_pairs={{0,15},{1,2},{2,1},{3,4},{4,3},{5,6},{6,5},{7,8},{8,7},{9,10},{10,... | collective-permute-start | bytes 61448 | tf_op jit(solution)/shard_map/ppermute | solution.py:429
  9.4 0.0 collective-permute-start
  9.4 1.3 %middle_fields.1 = (f32[4,4,128,128]{3,2,1,0:T(8,128)S(1)}, f32[6,128,128]{2,1,0:T(8,128)S(1)}) custom-call(f32[8,128]{1,0:T(8,128)S(1)} %get-tuple-element.17.coefs, f32[128,1024]{1,0:T(8,128)S(1)} %get-tuple-element.19.el), custom_call_target="tpu_custom_call" | custom-call | flops 10000000 | bytes 3000000 | tf_op jit(solution)/shard_map/middle_fields/pallas_call | solution.py:459
  10.7 0.0 collective-permute-done.1.from_b
  10.7 1.6 %collective-permute-done.from_a = f32[40,128]{1,0:T(8,128)S(1)} collective-permute-done((f32[40,128]{1,0:T(8,128)S(1)}, f32[40,128]{1,0:T(8,128)S(1)}, u32[]{:S(2)}, u32[]{:S(2)}) %collective-permute-start) | collective-permute-done | bytes 20512 | tf_op jit(solution)/shard_map/ppermute | solution.py:429
  12.3 0.1 row_message.1
  12.4 1.9 %collective-permute-start.2 = (f32[88,128]{1,0:T(8,128)S(1)}, f32[88,128]{1,0:T(8,128)S(1)}, u32[]{:S(2)}, u32[]{:S(2)}) collective-permute-start(f32[88,128]{1,0:T(8,128)S(1)} %get-tuple-element.22), channel_id=1, source_target_pairs={{0,16},{16,0},{32,48},{48,32},{64,80},{80,64},{96,112},{112,96},{1... | collective-permute-start | bytes 135176 | tf_op jit(solution)/shard_map/ppermute | solution.py:429
  14.3 4.2 %collective-permute-start.3 = (f32[88,128]{1,0:T(8,128)S(1)}, f32[88,128]{1,0:T(8,128)S(1)}, u32[]{:S(2)}, u32[]{:S(2)}) collective-permute-start(f32[88,128]{1,0:T(8,128)S(1)} %get-tuple-element.23), channel_id=1, source_target_pairs={{0,240},{16,32},{32,16},{48,64},{64,48},{80,96},{96,80},{112,128},... | collective-permute-start | bytes 135176 | tf_op jit(solution)/shard_map/ppermute | solution.py:429
  18.5 1.0 %outer_fields.1 = (f32[4,4,128,128]{3,2,1,0:T(8,128)S(1)}, f32[3,128,128]{2,1,0:T(8,128)S(1)}) custom-call(f32[8,128]{1,0:T(8,128)S(1)} %get-tuple-element.17.coefs, f32[128,1024]{1,0:T(8,128)S(1)} %get-tuple-element.19.el, f32[128,128]{1,0:T(8,128)S(1)} %get-tuple-element.24.side, f32[6,128,128]{2,1,0:T(8,128)S(1)} %get-tuple-element.20.after.known.middle_recip), custom_call_target="tpu_custom_call" | custom-call | flops 10000000 | bytes 3000000 | tf_op jit(solution)/shard_map/outer_fields/pallas_call | solution.py:480
  19.5 0.0 collective-permute-done.2.from_n
  19.6 3.1 %collective-permute-done.3.from_f = f32[88,128]{1,0:T(8,128)S(1)} collective-permute-done((f32[88,128]{1,0:T(8,128)S(1)}, f32[88,128]{1,0:T(8,128)S(1)}, u32[]{:S(2)}, u32[]{:S(2)}) %collective-permute-start.3) | collective-permute-done | bytes 45088 | tf_op jit(solution)/shard_map/ppermute | solution.py:429
  22.7 2.1 %inflow.1 = f32[128,1024]{1,0:T(8,128)} custom-call(f32[8,128]{1,0:T(8,128)S(1)} %get-tuple-element.17.coefs, f32[64,128]{1,0:T(8,128)S(1)} %get-tuple-element.21.coarse, f32[88,128]{1,0:T(8,128)S(1)} %collective-permute-done.2.from_n, f32[88,128]{1,0:T(8,128)S(1)} %collective-permute-done.3.from_f, f32[128,1024]{1,0:T(8,128)S(1)} %get-tuple-element.19.el, ...), custom_call_target="tpu_custom_call" | custom-call | tf_op jit(solution)/shard_map/inflow/pallas_call | solution.py:490
Async XLA Ops:
  1.7 9.0 %collective-permute-start.1 = (f32[40,128]{1,0:T(8,128)S(1)}, f32[40,128]{1,0:T(8,128)S(1)}, u32[]{:S(2)}, u32[]{:S(2)}) collective-permute-start(f32[40,128]{1,0:T(8,128)S(1)} %get-tuple-element.18.own), channel_id=1, source_target_pairs={{0,15},{1,2},{2,1},{3,4},{4,3},{5,6},{6,5},{7,8},{8,7},{9,10},{10,... | collective-permute-start | bytes 61448 | tf_op jit(solution)/shard_map/ppermute | solution.py:429
  9.4 2.9 %collective-permute-start = (f32[40,128]{1,0:T(8,128)S(1)}, f32[40,128]{1,0:T(8,128)S(1)}, u32[]{:S(2)}, u32[]{:S(2)}) collective-permute-start(f32[40,128]{1,0:T(8,128)S(1)} %get-tuple-element.18.own), channel_id=1, source_target_pairs={{0,1},{1,0},{2,3},{3,2},{4,5},{5,4},{6,7},{7,6},{8,9},{9,8},{10,11... | collective-permute-start | bytes 61448 | tf_op jit(solution)/shard_map/ppermute | solution.py:429
  12.4 7.1 %collective-permute-start.2 = (f32[88,128]{1,0:T(8,128)S(1)}, f32[88,128]{1,0:T(8,128)S(1)}, u32[]{:S(2)}, u32[]{:S(2)}) collective-permute-start(f32[88,128]{1,0:T(8,128)S(1)} %get-tuple-element.22), channel_id=1, source_target_pairs={{0,16},{16,0},{32,48},{48,32},{64,80},{80,64},{96,112},{112,96},{1... | collective-permute-start | bytes 135176 | tf_op jit(solution)/shard_map/ppermute | solution.py:429
  14.3 8.3 %collective-permute-start.3 = (f32[88,128]{1,0:T(8,128)S(1)}, f32[88,128]{1,0:T(8,128)S(1)}, u32[]{:S(2)}, u32[]{:S(2)}) collective-permute-start(f32[88,128]{1,0:T(8,128)S(1)} %get-tuple-element.23), channel_id=1, source_target_pairs={{0,240},{16,32},{32,16},{48,64},{64,48},{80,96},{96,80},{112,128},... | collective-permute-start | bytes 135176 | tf_op jit(solution)/shard_map/ppermute | solution.py:429

commit v4 on v3

--- a/solution.py
+++ b/solution.py
@@ -421,12 +421,20 @@
 
 
 def swap(x, axis, far):
-    count = lax.axis_size(axis)
-    if far:
-        pairs = [(i, (i + 1) % count if i % 2 else (i - 1) % count) for i in range(count)]
-    else:
-        pairs = [(i, i ^ 1) for i in range(count)]
-    return lax.ppermute(x, axis, pairs)
+    sizes = {name: lax.axis_size(name) for name in ("rows", "cols")}
+    pairs = []
+    for r in range(sizes["rows"]):
+        for c in range(sizes["cols"]):
+            to = {"rows": r, "cols": c}
+            i = to[axis]
+            partner = i ^ 1 if not far else i + 1 if i % 2 else i - 1
+            if 0 <= partner < sizes[axis]:
+                to[axis] = partner
+            else:
+                other = "cols" if axis == "rows" else "rows"
+                to[other] ^= 1
+            pairs.append((r * sizes["cols"] + c, to["rows"] * sizes["cols"] + to["cols"]))
+    return lax.ppermute(x, ("rows", "cols"), pairs)
 
 
 def f32(*shape):

time: 24.9 us -> 21.6 us (0.87)
  the two profiles are of different devices: /device:TPU:1 before, /device:TPU:30 now
where the time goes in v4:
time: 21.6 us; the launch traced here: 21.5 us
  starting transfers between devices  10.4 us (48%)
  Pallas kernels  6.24 us (29%)
  waiting for transfers between devices  4.77 us (22%)
    ppermute x4, starting transfers between devices, swap(): return lax.ppermute(x, ('rows', 'cols'), pairs)  10.4 us
    ppermute x4, waiting for transfers between devices, swap(): return lax.ppermute(x, ('rows', 'cols'), pairs)  4.77 us
    pallas_call x1, Pallas kernels, on_device(): pl.pallas_call(inflow_kernel, out_shape=f32(rows, cols), in_specs=whole(1...  2.13 us
    pallas_call x1, Pallas kernels, on_device(): pl.pallas_call(overview_kernel, out_shape=[f32(2 * k + 8, LANES), f32(row...  1.66 us
    pallas_call x1, Pallas kernels, on_device(): pl.pallas_call(middle_kernel, out_shape=[f32(4, chunks - 4, rows, LANES),...  1.32 us
    pallas_call x1, Pallas kernels, on_device(): pl.pallas_call(outer_kernel, out_shape=[f32(4, 4, rows, LANES), f32(3, ro...  1.02 us
  transfers between devices with their start and end apart: 4, of which 3 were waited for; matrix products, arithmetic and copies ran while one was open for 0% of the time, Pallas kernels for 11%

profile of v4, /device:TPU:30, one launch (start us, length us, event | category | flops | bytes accessed | tf_op | source)
XLA Modules:
  0.0 21.5 jit_solution(9602191330711022217)
XLA Ops:
  0.0 1.7 %overview.1 = (f32[40,128]{1,0:T(8,128)S(1)}, f32[128,1024]{1,0:T(8,128)S(1)}, s32[128,1024]{1,0:T(8,128)S(1)}, f32[8,128]{1,0:T(8,128)S(1)}) custom-call(s32[8]{0:T(128)} %tie_hbm.1, f32[128,1024]{1,0:T(8,128)} %el_hbm.1, s32[128,1024]{1,0:T(8,128)} %mk_hbm.1), custom_call_target="tpu_custom_call" | custom-call | tf_op jit(solution)/shard_map/overview/pallas_call | solution.py:454
  1.7 4.9 %collective-permute-start.1 = (f32[40,128]{1,0:T(8,128)S(1)}, f32[40,128]{1,0:T(8,128)S(1)}, u32[]{:S(2)}, u32[]{:S(2)}) collective-permute-start(f32[40,128]{1,0:T(8,128)S(1)} %get-tuple-element.18.own), channel_id=1, source_target_pairs={{0,16},{1,2},{2,1},{3,4},{4,3},{5,6},{6,5},{7,8},{8,7},{9,10},{10,... | collective-permute-start | bytes 61448 | tf_op jit(solution)/shard_map/ppermute | solution.py:437
  6.6 0.0 collective-permute-start
  6.6 1.3 %middle_fields.1 = (f32[4,4,128,128]{3,2,1,0:T(8,128)S(1)}, f32[6,128,128]{2,1,0:T(8,128)S(1)}) custom-call(f32[8,128]{1,0:T(8,128)S(1)} %get-tuple-element.17.coefs, f32[128,1024]{1,0:T(8,128)S(1)} %get-tuple-element.19.el), custom_call_target="tpu_custom_call" | custom-call | flops 10000000 | bytes 3000000 | tf_op jit(solution)/shard_map/middle_fields/pallas_call | solution.py:467
  7.9 0.4 %collective-permute-done.1.from_b = f32[40,128]{1,0:T(8,128)S(1)} collective-permute-done((f32[40,128]{1,0:T(8,128)S(1)}, f32[40,128]{1,0:T(8,128)S(1)}, u32[]{:S(2)}, u32[]{:S(2)}) %collective-permute-start.1) | collective-permute-done | bytes 20512 | tf_op jit(solution)/shard_map/ppermute | solution.py:437
  8.3 2.0 %collective-permute-done.from_a = f32[40,128]{1,0:T(8,128)S(1)} collective-permute-done((f32[40,128]{1,0:T(8,128)S(1)}, f32[40,128]{1,0:T(8,128)S(1)}, u32[]{:S(2)}, u32[]{:S(2)}) %collective-permute-start) | collective-permute-done | bytes 20512 | tf_op jit(solution)/shard_map/ppermute | solution.py:437
  10.3 0.1 row_message.1
  10.5 0.1 collective-permute-start.2
  10.6 5.5 %collective-permute-start.3 = (f32[88,128]{1,0:T(8,128)S(1)}, f32[88,128]{1,0:T(8,128)S(1)}, u32[]{:S(2)}, u32[]{:S(2)}) collective-permute-start(f32[88,128]{1,0:T(8,128)S(1)} %get-tuple-element.23), channel_id=1, source_target_pairs={{0,1},{1,0},{2,3},{3,2},{4,5},{5,4},{6,7},{7,6},{8,9},{9,8},{10,11... | collective-permute-start | bytes 135176 | tf_op jit(solution)/shard_map/ppermute | solution.py:437
  16.0 1.0 %outer_fields.1 = (f32[4,4,128,128]{3,2,1,0:T(8,128)S(1)}, f32[3,128,128]{2,1,0:T(8,128)S(1)}) custom-call(f32[8,128]{1,0:T(8,128)S(1)} %get-tuple-element.17.coefs, f32[128,1024]{1,0:T(8,128)S(1)} %get-tuple-element.19.el, f32[128,128]{1,0:T(8,128)S(1)} %get-tuple-element.24.side, f32[6,128,128]{2,1,0:T(8,128)S(1)} %get-tuple-element.20.after.known.middle_recip), custom_call_target="tpu_custom_call" | custom-call | flops 10000000 | bytes 3000000 | tf_op jit(solution)/shard_map/outer_fields/pallas_call | solution.py:488
  17.0 0.0 collective-permute-done.2.from_n
  17.1 2.3 %collective-permute-done.3.from_f = f32[88,128]{1,0:T(8,128)S(1)} collective-permute-done((f32[88,128]{1,0:T(8,128)S(1)}, f32[88,128]{1,0:T(8,128)S(1)}, u32[]{:S(2)}, u32[]{:S(2)}) %collective-permute-start.3) | collective-permute-done | bytes 45088 | tf_op jit(solution)/shard_map/ppermute | solution.py:437
  19.4 2.1 %inflow.1 = f32[128,1024]{1,0:T(8,128)} custom-call(f32[8,128]{1,0:T(8,128)S(1)} %get-tuple-element.17.coefs, f32[64,128]{1,0:T(8,128)S(1)} %get-tuple-element.21.coarse, f32[88,128]{1,0:T(8,128)S(1)} %collective-permute-done.2.from_n, f32[88,128]{1,0:T(8,128)S(1)} %collective-permute-done.3.from_f, f32[128,1024]{1,0:T(8,128)S(1)} %get-tuple-element.19.el, ...), custom_call_target="tpu_custom_call" | custom-call | tf_op jit(solution)/shard_map/inflow/pallas_call | solution.py:498
Async XLA Ops:
  1.7 6.7 %collective-permute-start.1 = (f32[40,128]{1,0:T(8,128)S(1)}, f32[40,128]{1,0:T(8,128)S(1)}, u32[]{:S(2)}, u32[]{:S(2)}) collective-permute-start(f32[40,128]{1,0:T(8,128)S(1)} %get-tuple-element.18.own), channel_id=1, source_target_pairs={{0,16},{1,2},{2,1},{3,4},{4,3},{5,6},{6,5},{7,8},{8,7},{9,10},{10,... | collective-permute-start | bytes 61448 | tf_op jit(solution)/shard_map/ppermute | solution.py:437
  6.6 3.8 %collective-permute-start = (f32[40,128]{1,0:T(8,128)S(1)}, f32[40,128]{1,0:T(8,128)S(1)}, u32[]{:S(2)}, u32[]{:S(2)}) collective-permute-start(f32[40,128]{1,0:T(8,128)S(1)} %get-tuple-element.18.own), channel_id=1, source_target_pairs={{0,1},{1,0},{2,3},{3,2},{4,5},{5,4},{6,7},{7,6},{8,9},{9,8},{10,11... | collective-permute-start | bytes 61448 | tf_op jit(solution)/shard_map/ppermute | solution.py:437
  10.5 6.6 %collective-permute-start.2 = (f32[88,128]{1,0:T(8,128)S(1)}, f32[88,128]{1,0:T(8,128)S(1)}, u32[]{:S(2)}, u32[]{:S(2)}) collective-permute-start(f32[88,128]{1,0:T(8,128)S(1)} %get-tuple-element.22), channel_id=1, source_target_pairs={{0,16},{1,17},{2,18},{3,19},{4,20},{5,21},{6,22},{7,23},{8,24},{9,... | collective-permute-start | bytes 135176 | tf_op jit(solution)/shard_map/ppermute | solution.py:437
  10.6 8.8 %collective-permute-start.3 = (f32[88,128]{1,0:T(8,128)S(1)}, f32[88,128]{1,0:T(8,128)S(1)}, u32[]{:S(2)}, u32[]{:S(2)}) collective-permute-start(f32[88,128]{1,0:T(8,128)S(1)} %get-tuple-element.23), channel_id=1, source_target_pairs={{0,1},{1,0},{2,3},{3,2},{4,5},{5,4},{6,7},{7,6},{8,9},{9,8},{10,11... | collective-permute-start | bytes 135176 | tf_op jit(solution)/shard_map/ppermute | solution.py:437

commit v5 on v4

--- a/solution.py
+++ b/solution.py
@@ -102,106 +102,124 @@
     return level[0]
 
 
-PIECES = 8
+DEPTH = ITERS + 2
+PIECES = 4
 PARTS = 4
 
 
-def overview_kernel(tie_hbm, el_hbm, mk_hbm, msg, el, mk, coef, tie, tie_sem, el_sem, mk_sem):
+def edges(overview, runoff):
+    lane = iota(overview.shape, 1)
+    outer = (lane < DEPTH) | (lane >= LANES - DEPTH)
+    return jnp.where(outer, overview, pltpu.roll(runoff, LANES // 2, 1))
+
+
+def overview_kernel(tie_hbm, el_hbm, mk_hbm, msg, own, el, mk, coef, tie, tie_sem, el_sem, mk_sem):
     rows, cols = el.shape
     chunks = cols // LANES
-    size = rows // PIECES
+    k = rows // 8
+    per = chunks // PIECES
+    pieces = [0, PIECES - 1, *range(1, PIECES - 1)]
     fetch = []
-    for p in range(PIECES):
-        at = pl.ds(p * size, size)
-        fetch.append(
-            (
-                pltpu.make_async_copy(el_hbm.at[at, :], el.at[at, :], el_sem.at[p]),
-                pltpu.make_async_copy(mk_hbm.at[at, :], mk.at[at, :], mk_sem.at[p]),
-            )
+    for p in pieces:
+        at = pl.ds(p * per * LANES, per * LANES)
+        pair = (
+            pltpu.make_async_copy(el_hbm.at[:, at], el.at[:, at], el_sem.at[p]),
+            pltpu.make_async_copy(mk_hbm.at[:, at], mk.at[:, at], mk_sem.at[p]),
         )
-    for pair in fetch:
         for copy in pair:
             copy.start()
+        fetch.append(pair)
     tie_copy = pltpu.make_async_copy(tie_hbm, tie, tie_sem)
     tie_copy.start()
     col = iota((cols, LANES), 0) // 8
     pick = jnp.where(col == iota((cols, LANES), 1), 1.0, 0.0).astype(jnp.bfloat16)
     tie_copy.wait()
     coefficients(tie, coef)
-    sums, counts = [], []
-    waited = 0
-    for g in range(rows // 64):
-        while waited * size < 64 * (g + 1):
-            for copy in fetch[waited]:
-                copy.wait()
-            waited += 1
-        s_parts, n_parts = [], []
-        for j in range(chunks):
-            s_tiles, n_tiles = [], []
-            for t in range(8):
-                at = (slice(64 * g + 8 * t, 64 * g + 8 * t + 8), slice(LANES * j, LANES * j + LANES))
-                m = mk[at].astype(jnp.float32)
-                n_tiles.append(m)
-                s_tiles.append(m * el[at])
-            s_parts.append(block_rows(s_tiles))
-            n_parts.append(block_rows(n_tiles))
-        sums.append(jnp.concatenate(s_parts, axis=1))
-        counts.append(jnp.concatenate(n_parts, axis=1))
-    s = jnp.concatenate(sums, axis=0)
-    n = jnp.concatenate(counts, axis=0)
+    sums, counts = {}, {}
+    for p, pair in zip(pieces, fetch):
+        for copy in pair:
+            copy.wait()
+        for j in range(p * per, (p + 1) * per):
+            lanes = slice(LANES * j, LANES * j + LANES)
+            s_groups, n_groups = [], []
+            for g in range(rows // 64):
+                at = [(slice(64 * g + 8 * t, 64 * g + 8 * t + 8), lanes) for t in range(8)]
+                flags = [mk[i].astype(jnp.float32) for i in at]
+                n_groups.append(block_rows(flags))
+                s_groups.append(block_rows([m * el[i] for m, i in zip(flags, at)]))
+            sums[j] = jnp.concatenate(s_groups, axis=0)
+            counts[j] = jnp.concatenate(n_groups, axis=0)
+            if j == 0:
+                msg[k : k + 4, :] = jnp.transpose(el[:, lanes])[0:4]
+            if j == chunks - 1:
+                msg[k + 4 : k + 8, :] = jnp.transpose(el[:, lanes])[LANES - 4 : LANES]
+    s = jnp.concatenate([sums[j] for j in range(chunks)], axis=1)
+    n = jnp.concatenate([counts[j] for j in range(chunks)], axis=1)
     hi = s.astype(jnp.bfloat16)
     rest = s - hi.astype(jnp.float32)
     mid = rest.astype(jnp.bfloat16)
     low = (rest - mid.astype(jnp.float32)).astype(jnp.bfloat16)
     left = jnp.concatenate([hi, mid, low, n.astype(jnp.bfloat16)], axis=0)
     out = lax.dot_general(left, pick, (((1,), (0,)), ((), ())), preferred_element_type=jnp.float32)
-    k = rows // 8
     summed = out[0:k] + (out[k : 2 * k] + out[2 * k : 3 * k])
     count = out[3 * k : 4 * k]
-    msg[0:k, :] = summed / (count + 1.0)
-    msg[k : 2 * k, :] = count * (1.0 / 64.0)
-    first = jnp.transpose(el[:, 0:LANES])
-    last = jnp.transpose(el[:, cols - LANES : cols])
-    msg[2 * k : 2 * k + 4, :] = first[0:4]
-    msg[2 * k + 4 : 2 * k + 8, :] = last[LANES - 4 : LANES]
+    overview, runoff = summed / (count + 1.0), count * (1.0 / 64.0)
+    msg[0:k, :] = edges(overview, runoff)
+    own[0:k, :] = overview
+    own[k : 2 * k, :] = runoff
 
 
 def row_message_kernel(own, from_a, from_b, el, after, coarse, side, to_n, to_f):
-    k = (own.shape[0] - 8) // 2
+    k = own.shape[0] // 2
     rows, cols = el.shape
     chunks = cols // LANES
     r, c = lax.axis_index("rows"), lax.axis_index("cols")
     count = lax.axis_size("cols")
-    even = c % 2 == 0
-    shape = own.shape
+    even = jnp.full((k + 8, LANES), c % 2 == 0)
     a, b = from_a[...], from_b[...]
-    line = iota(shape, 0)
-    missing = jnp.where((line >= k) & (line < 2 * k), 0.0, OUTSIDE)
-    right = jnp.where(jnp.full(shape, c == count - 1), missing, jnp.where(jnp.full(shape, even), a, b))
-    left = jnp.where(jnp.full(shape, c == 0), missing, jnp.where(jnp.full(shape, even), b, a))
-    lane = iota((2 * k, LANES), 1)
-    near = jnp.where(lane < LANES // 2, right[0 : 2 * k], left[0 : 2 * k])
-    mine = own[...]
-    c4 = (mine[0:k], near[0:k], mine[k : 2 * k], near[k : 2 * k])
-    for i, part in enumerate(c4):
+    right, left = jnp.where(even, a, b), jnp.where(even, b, a)
+    lane = iota((k, LANES), 1)
+    east = lane < LANES // 2
+    gone_east, gone_west = jnp.full((k, LANES), c == count - 1), jnp.full((k, LANES), c == 0)
+    gone = (east & gone_east) | (~east & gone_west)
+    near = jnp.where(gone, OUTSIDE, jnp.where(east, right[0:k], left[0:k]))
+    near_run = pltpu.roll(jnp.where(east, left[0:k], right[0:k]), LANES // 2, 1)
+    near_run = jnp.where(gone, 0.0, near_run)
+    over, run = own[0:k, :], own[k : 2 * k, :]
+    for i, part in enumerate((over, near, run, near_run)):
         coarse[i * k : (i + 1) * k, :] = part
-        to_n[i * k : (i + 1) * k, :] = part
-        to_f[i * k : (i + 1) * k, :] = part
-    cols_t = jnp.concatenate(
-        [right[2 * k : 2 * k + 4], jnp.zeros((LANES - 8, LANES), jnp.float32), left[2 * k + 4 : 2 * k + 8]], axis=0
+    columns = jnp.concatenate(
+        [
+            jnp.where(jnp.full((4, LANES), c == count - 1), OUTSIDE, right[k : k + 4]),
+            jnp.zeros((LANES - 8, LANES), jnp.float32),
+            jnp.where(jnp.full((4, LANES), c == 0), OUTSIDE, left[k + 4 : k + 8]),
+        ],
+        axis=0,
     )
-    beyond = jnp.transpose(cols_t)
+    beyond = jnp.transpose(columns)
     side[...] = beyond
     upper = r % 2 == 0
-    for j in range(chunks + 1):
-        if j < chunks:
-            lanes = slice(LANES * j, LANES * j + LANES)
-            top, bottom = el[0:2, lanes], el[rows - 2 : rows, lanes]
-        else:
-            top, bottom = beyond[0:2], beyond[rows - 2 : rows]
-        cond = jnp.full((2, LANES), upper)
-        to_n[4 * k + 2 * j : 4 * k + 2 * j + 2, :] = jnp.where(cond, bottom, top)
-        to_f[4 * k + 2 * j : 4 * k + 2 * j + 2, :] = jnp.where(cond, top, bottom)
+    packed = edges(near, near_run)
+    turned = pltpu.roll(jnp.concatenate([beyond[0:8], beyond[rows - 8 : rows]], axis=0), LANES // 4, 1)
+    ends = (turned[0:2], turned[14:16])
+    lane2 = iota((2, LANES), 1)
+    quarter = (lane2 >= LANES // 4 - 2) & (lane2 < LANES // 4 + 2)
+
+    def put(at, top, bottom):
+        cond = jnp.full(top.shape, upper)
+        to_n[at : at + top.shape[0], :] = jnp.where(cond, bottom, top)
+        to_f[at : at + top.shape[0], :] = jnp.where(cond, top, bottom)
+
+    for i, part in enumerate((over, run, packed)):
+        put(i * DEPTH, part[0:DEPTH], part[k - DEPTH : k])
+    for j in range(chunks):
+        lanes = slice(LANES * j, LANES * j + LANES)
+        put(3 * DEPTH + 2 * j, el[0:2, lanes], el[rows - 2 : rows, lanes])
+    put(
+        2 * DEPTH,
+        jnp.where(quarter, ends[0], packed[0:2]),
+        jnp.where(quarter, ends[1], packed[k - DEPTH : k - DEPTH + 2]),
+    )
 
 
 def middle_kernel(coefs, el, out, recip, zc, zw, ze, rc, rw, re):
@@ -286,23 +304,33 @@
     upper = r % 2 == 0
     coef = coefficient_tiles(coefs)
     n, f = from_n[...], from_f[...]
-    shape = n.shape
-    line = iota(shape, 0)
-    missing = jnp.where((line >= 2 * k) & (line < 4 * k), 0.0, OUTSIDE)
-    cond = jnp.full(shape, upper)
-    above = jnp.where(jnp.full(shape, r == 0), missing, jnp.where(cond, f, n))
-    below = jnp.where(jnp.full(shape, r == count - 1), missing, jnp.where(cond, n, f))
+    cond = jnp.full(n.shape, upper)
+
+    def unpack(x, gone):
+        rest = lambda part, value: jnp.where(jnp.full(part.shape, gone), value, part)
+        packed = x[2 * DEPTH : 3 * DEPTH]
+        parts = (
+            rest(x[0:DEPTH], OUTSIDE),
+            rest(packed, OUTSIDE),
+            rest(x[DEPTH : 2 * DEPTH], 0.0),
+            rest(pltpu.roll(jnp.concatenate([packed, x[0:6]], axis=0), LANES // 2, 1)[0:DEPTH], 0.0),
+        )
+        lines = rest(x[3 * DEPTH : 3 * DEPTH + 2 * chunks], OUTSIDE)
+        turned = pltpu.roll(x[2 * DEPTH : 2 * DEPTH + 8], LANES - LANES // 4, 1)[0:2]
+        return parts, [lines[2 * j : 2 * j + 2] for j in range(chunks)] + [rest(turned, OUTSIDE)]
+
+    above, above_lines = unpack(jnp.where(cond, f, n), r == 0)
+    below, below_lines = unpack(jnp.where(cond, n, f), r == count - 1)
 
     k_planes, s_planes = (kc, kw, ke), (sc, sw, se)
     around = lambda size: (lambda j: j % size)
     for j in range(2):
-        kc[j, 0:8, :] = jnp.zeros((8, LANES), jnp.float32)
-        kc[j, 8 + 3 * k : 16 + 3 * k, :] = jnp.zeros((8, LANES), jnp.float32)
-        for ref, base, first in ((kc, 0, 8), (run, 2 * k, 0)):
-            lo = base + j * k
-            ref[j, first : first + k, :] = above[lo : lo + k]
-            ref[j, first + k : first + 2 * k, :] = coarse[lo : lo + k, :]
-            ref[j, first + 2 * k : first + 3 * k, :] = below[lo : lo + k]
+        for ref, base, first, total in ((kc, 0, 8, 3 * k + 16), (run, 2, 0, 3 * k)):
+            ref[j, 0 : first + k, :] = jnp.zeros((first + k, LANES), jnp.float32)
+            ref[j, first + 2 * k : total, :] = jnp.zeros((total - first - 2 * k, LANES), jnp.float32)
+            ref[j, first + k - DEPTH : first + k, :] = above[base + j]
+            ref[j, first + k : first + 2 * k, :] = coarse[(base + j) * k : (base + j + 1) * k, :]
+            ref[j, first + 2 * k : first + 2 * k + DEPTH, :] = below[base + j]
     for t in range(3 * k // 8 + 2):
         spread(k_planes, range(2), 8 * t, around(2))
     recip = {}
@@ -319,7 +347,7 @@
     ring = around(chunks + 1)
     every = range(chunks + 1)
     for j in every:
-        up2, down2 = above[4 * k + 2 * j : 4 * k + 2 * j + 2], below[4 * k + 2 * j : 4 * k + 2 * j + 2]
+        up2, down2 = above_lines[j], below_lines[j]
         if j < chunks:
             first, last = el[0:8, LANES * j : LANES * j + LANES], el[rows - 8 : rows, LANES * j : LANES * j + LANES]
         else:
@@ -451,11 +479,17 @@
     params = pltpu.CompilerParams(vmem_limit_bytes=LIMIT)
     dma = pltpu.SemaphoreType.DMA
     hbm = pl.BlockSpec(memory_space=pltpu.HBM)
-    msg, el, mk, coefs = pl.pallas_call(
+    msg, own, el, mk, coefs = pl.pallas_call(
         overview_kernel,
-        out_shape=[f32(2 * k + 8, LANES), f32(rows, cols), jax.ShapeDtypeStruct((rows, cols), jnp.int32), f32(8, LANES)],
+        out_shape=[
+            f32(k + 8, LANES),
+            f32(2 * k, LANES),
+            f32(rows, cols),
+            jax.ShapeDtypeStruct((rows, cols), jnp.int32),
+            f32(8, LANES),
+        ],
         in_specs=[hbm] * 3,
-        out_specs=whole(4),
+        out_specs=whole(5),
         scratch_shapes=[pltpu.SMEM((8,), jnp.int32), dma, dma((PIECES,)), dma((PIECES,))],
         compiler_params=params,
         name="overview",
@@ -474,7 +508,7 @@
         cost_estimate=cost,
         name="middle_fields",
     )(coefs, el)
-    size = 4 * k + 24
+    size = (3 * DEPTH + 2 * chunks + 7) // 8 * 8
     coarse, side, to_n, to_f = pl.pallas_call(
         row_message_kernel,
         out_shape=[f32(4 * k, LANES), f32(rows, LANES), f32(size, LANES), f32(size, LANES)],
@@ -482,7 +516,7 @@
         out_specs=whole(4),
         compiler_params=params,
         name="row_message",
-    )(msg, from_a, from_b, el, middle_recip)
+    )(own, from_a, from_b, el, middle_recip)
     from_n = swap(to_n, "rows", False)
     from_f = swap(to_f, "rows", True)
     outer, outer_recip = pl.pallas_call(

time: 21.6 us -> 21.1 us (0.977)
  waiting for transfers between devices: 4.77 us -> 4.25 us
    ppermute x4, waiting for transfers between devices: 4.77 us -> 4.25 us  [swap(): return lax.ppermute(x, ('rows', 'cols'), pairs)]
where the time goes in v5:
time: 21.1 us; the launch traced here: 21 us
  starting transfers between devices  10.4 us (49%)
  Pallas kernels  6.28 us (30%)
  waiting for transfers between devices  4.25 us (20%)
    ppermute x4, starting transfers between devices, swap(): return lax.ppermute(x, ('rows', 'cols'), pairs)  10.4 us
    ppermute x4, waiting for transfers between devices, swap(): return lax.ppermute(x, ('rows', 'cols'), pairs)  4.25 us
    pallas_call x1, Pallas kernels, on_device(): pl.pallas_call(inflow_kernel, out_shape=f32(rows, cols), in_specs=whole(1...  2.14 us
    pallas_call x1, Pallas kernels, on_device(): pl.pallas_call(overview_kernel, out_shape=[f32(k + 8, LANES), f32(2 * k,...  1.64 us
    pallas_call x1, Pallas kernels, on_device(): pl.pallas_call(middle_kernel, out_shape=[f32(4, chunks - 4, rows, LANES),...  1.31 us
    pallas_call x1, Pallas kernels, on_device(): pl.pallas_call(outer_kernel, out_shape=[f32(4, 4, rows, LANES), f32(3, ro...  1.01 us
  transfers between devices with their start and end apart: 4, of which 3 were waited for; matrix products, arithmetic and copies ran while one was open for 0% of the time, Pallas kernels for 11%

profile of v5, /device:TPU:30, one launch (start us, length us, event | category | flops | bytes accessed | tf_op | source)
XLA Modules:
  0.0 21.0 jit_solution(8710639454593088864)
XLA Ops:
  0.0 1.6 %overview.1 = (f32[24,128]{1,0:T(8,128)S(1)}, f32[32,128]{1,0:T(8,128)S(1)}, f32[128,1024]{1,0:T(8,128)S(1)}, s32[128,1024]{1,0:T(8,128)S(1)}, f32[8,128]{1,0:T(8,128)S(1)}) custom-call(s32[8]{0:T(128)} %tie_hbm.1, f32[128,1024]{1,0:T(8,128)} %el_hbm.1, s32[128,1024]{1,0:T(8,128)} %mk_hbm.1), custom_call_target="tpu_custom_call" | custom-call | tf_op jit(solution)/shard_map/overview/pallas_call | solution.py:482
  1.7 4.9 %collective-permute-start.1 = (f32[24,128]{1,0:T(8,128)S(1)}, f32[24,128]{1,0:T(8,128)S(1)}, u32[]{:S(2)}, u32[]{:S(2)}) collective-permute-start(f32[24,128]{1,0:T(8,128)S(1)} %get-tuple-element.20), channel_id=1, source_target_pairs={{0,16},{1,2},{2,1},{3,4},{4,3},{5,6},{6,5},{7,8},{8,7},{9,10},{10,... | collective-permute-start | bytes 36872 | tf_op jit(solution)/shard_map/ppermute | solution.py:465
  6.5 0.0 collective-permute-start
  6.5 1.3 %middle_fields.1 = (f32[4,4,128,128]{3,2,1,0:T(8,128)S(1)}, f32[6,128,128]{2,1,0:T(8,128)S(1)}) custom-call(f32[8,128]{1,0:T(8,128)S(1)} %get-tuple-element.18.coefs, f32[128,1024]{1,0:T(8,128)S(1)} %get-tuple-element.21.el), custom_call_target="tpu_custom_call" | custom-call | flops 10000000 | bytes 3000000 | tf_op jit(solution)/shard_map/middle_fields/pallas_call | solution.py:501
  7.9 0.4 %collective-permute-done.1.from_b = f32[24,128]{1,0:T(8,128)S(1)} collective-permute-done((f32[24,128]{1,0:T(8,128)S(1)}, f32[24,128]{1,0:T(8,128)S(1)}, u32[]{:S(2)}, u32[]{:S(2)}) %collective-permute-start.1) | collective-permute-done | bytes 12320 | tf_op jit(solution)/shard_map/ppermute | solution.py:465
  8.2 2.0 %collective-permute-done.from_a = f32[24,128]{1,0:T(8,128)S(1)} collective-permute-done((f32[24,128]{1,0:T(8,128)S(1)}, f32[24,128]{1,0:T(8,128)S(1)}, u32[]{:S(2)}, u32[]{:S(2)}) %collective-permute-start) | collective-permute-done | bytes 12320 | tf_op jit(solution)/shard_map/ppermute | solution.py:465
  10.2 0.2 row_message.1
  10.4 0.0 collective-permute-start.2
  10.5 5.5 %collective-permute-start.3 = (f32[48,128]{1,0:T(8,128)S(1)}, f32[48,128]{1,0:T(8,128)S(1)}, u32[]{:S(2)}, u32[]{:S(2)}) collective-permute-start(f32[48,128]{1,0:T(8,128)S(1)} %get-tuple-element.25), channel_id=1, source_target_pairs={{0,1},{1,0},{2,3},{3,2},{4,5},{5,4},{6,7},{7,6},{8,9},{9,8},{10,11... | collective-permute-start | bytes 73736 | tf_op jit(solution)/shard_map/ppermute | solution.py:465
  15.9 1.0 %outer_fields.1 = (f32[4,4,128,128]{3,2,1,0:T(8,128)S(1)}, f32[3,128,128]{2,1,0:T(8,128)S(1)}) custom-call(f32[8,128]{1,0:T(8,128)S(1)} %get-tuple-element.18.coefs, f32[128,1024]{1,0:T(8,128)S(1)} %get-tuple-element.21.el, f32[128,128]{1,0:T(8,128)S(1)} %get-tuple-element.26.side, f32[6,128,128]{2,1,0:T(8,128)S(1)} %get-tuple-element.22.after.known.middle_recip), custom_call_target="tpu_custom_call" | custom-call | flops 10000000 | bytes 3000000 | tf_op jit(solution)/shard_map/outer_fields/pallas_call | solution.py:522
  16.9 0.0 collective-permute-done.2.from_n
  17.0 1.9 %collective-permute-done.3.from_f = f32[48,128]{1,0:T(8,128)S(1)} collective-permute-done((f32[48,128]{1,0:T(8,128)S(1)}, f32[48,128]{1,0:T(8,128)S(1)}, u32[]{:S(2)}, u32[]{:S(2)}) %collective-permute-start.3) | collective-permute-done | bytes 24608 | tf_op jit(solution)/shard_map/ppermute | solution.py:465
  18.8 2.1 %inflow.1 = f32[128,1024]{1,0:T(8,128)} custom-call(f32[8,128]{1,0:T(8,128)S(1)} %get-tuple-element.18.coefs, f32[64,128]{1,0:T(8,128)S(1)} %get-tuple-element.23.coarse, f32[48,128]{1,0:T(8,128)S(1)} %collective-permute-done.2.from_n, f32[48,128]{1,0:T(8,128)S(1)} %collective-permute-done.3.from_f, f32[128,1024]{1,0:T(8,128)S(1)} %get-tuple-element.21.el, ...), custom_call_target="tpu_custom_call" | custom-call | tf_op jit(solution)/shard_map/inflow/pallas_call | solution.py:532
Async XLA Ops:
  1.7 6.6 %collective-permute-start.1 = (f32[24,128]{1,0:T(8,128)S(1)}, f32[24,128]{1,0:T(8,128)S(1)}, u32[]{:S(2)}, u32[]{:S(2)}) collective-permute-start(f32[24,128]{1,0:T(8,128)S(1)} %get-tuple-element.20), channel_id=1, source_target_pairs={{0,16},{1,2},{2,1},{3,4},{4,3},{5,6},{6,5},{7,8},{8,7},{9,10},{10,... | collective-permute-start | bytes 36872 | tf_op jit(solution)/shard_map/ppermute | solution.py:465
  6.5 3.7 %collective-permute-start = (f32[24,128]{1,0:T(8,128)S(1)}, f32[24,128]{1,0:T(8,128)S(1)}, u32[]{:S(2)}, u32[]{:S(2)}) collective-permute-start(f32[24,128]{1,0:T(8,128)S(1)} %get-tuple-element.20), channel_id=1, source_target_pairs={{0,1},{1,0},{2,3},{3,2},{4,5},{5,4},{6,7},{7,6},{8,9},{9,8},{10,11... | collective-permute-start | bytes 36872 | tf_op jit(solution)/shard_map/ppermute | solution.py:465
  10.4 6.5 %collective-permute-start.2 = (f32[48,128]{1,0:T(8,128)S(1)}, f32[48,128]{1,0:T(8,128)S(1)}, u32[]{:S(2)}, u32[]{:S(2)}) collective-permute-start(f32[48,128]{1,0:T(8,128)S(1)} %get-tuple-element.24), channel_id=1, source_target_pairs={{0,16},{1,17},{2,18},{3,19},{4,20},{5,21},{6,22},{7,23},{8,24},{9,... | collective-permute-start | bytes 73736 | tf_op jit(solution)/shard_map/ppermute | solution.py:465
  10.5 8.4 %collective-permute-start.3 = (f32[48,128]{1,0:T(8,128)S(1)}, f32[48,128]{1,0:T(8,128)S(1)}, u32[]{:S(2)}, u32[]{:S(2)}) collective-permute-start(f32[48,128]{1,0:T(8,128)S(1)} %get-tuple-element.25), channel_id=1, source_target_pairs={{0,1},{1,0},{2,3},{3,2},{4,5},{5,4},{6,7},{7,6},{8,9},{9,8},{10,11... | collective-permute-start | bytes 73736 | tf_op jit(solution)/shard_map/ppermute | solution.py:465

commit v6 on v5

--- a/solution.py
+++ b/solution.py
@@ -169,10 +169,8 @@
     own[k : 2 * k, :] = runoff
 
 
-def row_message_kernel(own, from_a, from_b, el, after, coarse, side, to_n, to_f):
+def row_message_kernel(own, from_a, from_b, el, after, coarse, side, to_f):
     k = own.shape[0] // 2
-    rows, cols = el.shape
-    chunks = cols // LANES
     r, c = lax.axis_index("rows"), lax.axis_index("cols")
     count = lax.axis_size("cols")
     even = jnp.full((k + 8, LANES), c % 2 == 0)
@@ -198,28 +196,36 @@
     )
     beyond = jnp.transpose(columns)
     side[...] = beyond
-    upper = r % 2 == 0
-    packed = edges(near, near_run)
+    message((over, run, edges(near, near_run)), beyond, el, r % 2 == 1, to_f)
+
+
+def message(parts, beyond, el, lower, out):
+    rows, cols = el.shape
+    k = parts[0].shape[0]
     turned = pltpu.roll(jnp.concatenate([beyond[0:8], beyond[rows - 8 : rows]], axis=0), LANES // 4, 1)
-    ends = (turned[0:2], turned[14:16])
     lane2 = iota((2, LANES), 1)
     quarter = (lane2 >= LANES // 4 - 2) & (lane2 < LANES // 4 + 2)
 
     def put(at, top, bottom):
-        cond = jnp.full(top.shape, upper)
-        to_n[at : at + top.shape[0], :] = jnp.where(cond, bottom, top)
-        to_f[at : at + top.shape[0], :] = jnp.where(cond, top, bottom)
-
-    for i, part in enumerate((over, run, packed)):
+        out[at : at + top.shape[0], :] = jnp.where(jnp.full(top.shape, lower), bottom, top)
+
+    for i, part in enumerate(parts):
         put(i * DEPTH, part[0:DEPTH], part[k - DEPTH : k])
-    for j in range(chunks):
+    for j in range(cols // LANES):
         lanes = slice(LANES * j, LANES * j + LANES)
         put(3 * DEPTH + 2 * j, el[0:2, lanes], el[rows - 2 : rows, lanes])
+    packed = parts[2]
     put(
         2 * DEPTH,
-        jnp.where(quarter, ends[0], packed[0:2]),
-        jnp.where(quarter, ends[1], packed[k - DEPTH : k - DEPTH + 2]),
+        jnp.where(quarter, turned[0:2], packed[0:2]),
+        jnp.where(quarter, turned[14:16], packed[k - DEPTH : k - DEPTH + 2]),
     )
+
+
+def near_message_kernel(coarse, side, el, after, to_n):
+    k = coarse.shape[0] // 4
+    over, near, run, near_run = (coarse[i * k : (i + 1) * k, :] for i in range(4))
+    message((over, run, edges(near, near_run)), side[...], el, lax.axis_index("rows") % 2 == 0, to_n)
 
 
 def middle_kernel(coefs, el, out, recip, zc, zw, ze, rc, rw, re):
@@ -509,15 +515,14 @@
         name="middle_fields",
     )(coefs, el)
     size = (3 * DEPTH + 2 * chunks + 7) // 8 * 8
-    coarse, side, to_n, to_f = pl.pallas_call(
+    coarse, side, to_f = pl.pallas_call(
         row_message_kernel,
-        out_shape=[f32(4 * k, LANES), f32(rows, LANES), f32(size, LANES), f32(size, LANES)],
+        out_shape=[f32(4 * k, LANES), f32(rows, LANES), f32(size, LANES)],
         in_specs=whole(5),
-        out_specs=whole(4),
+        out_specs=whole(3),
         compiler_params=params,
-        name="row_message",
+        name="far_message",
     )(own, from_a, from_b, el, middle_recip)
-    from_n = swap(to_n, "rows", False)
     from_f = swap(to_f, "rows", True)
     outer, outer_recip = pl.pallas_call(
         outer_kernel,
@@ -529,6 +534,15 @@
         cost_estimate=cost,
         name="outer_fields",
     )(coefs, el, side, middle_recip)
+    to_n = pl.pallas_call(
+        near_message_kernel,
+        out_shape=f32(size, LANES),
+        in_specs=whole(4),
+        out_specs=whole(1)[0],
+        compiler_params=params,
+        name="near_message",
+    )(coarse, side, el, outer_recip)
+    from_n = swap(to_n, "rows", False)
     return pl.pallas_call(
         inflow_kernel,
         out_shape=f32(rows, cols),

time: 21.1 us -> 20.9 us (level)
    ppermute x4, starting transfers between devices: 10.4 us -> 10.2 us  [swap(): return lax.ppermute(x, ('rows', 'cols'), pairs)]
where the time goes in v6:
time: 20.9 us; the launch traced here: 20.8 us
  starting transfers between devices  10.2 us (49%)
  Pallas kernels  6.32 us (30%)
  waiting for transfers between devices  4.24 us (20%)
    ppermute x4, starting transfers between devices, swap(): return lax.ppermute(x, ('rows', 'cols'), pairs)  10.2 us
    ppermute x4, waiting for transfers between devices, swap(): return lax.ppermute(x, ('rows', 'cols'), pairs)  4.24 us
    pallas_call x1, Pallas kernels, on_device(): pl.pallas_call(inflow_kernel, out_shape=f32(rows, cols), in_specs=whole(1...  2.12 us
    pallas_call x1, Pallas kernels, on_device(): pl.pallas_call(overview_kernel, out_shape=[f32(k + 8, LANES), f32(2 * k,...  1.64 us
    pallas_call x1, Pallas kernels, on_device(): pl.pallas_call(middle_kernel, out_shape=[f32(4, chunks - 4, rows, LANES),...  1.3 us
    pallas_call x1, Pallas kernels, on_device(): pl.pallas_call(outer_kernel, out_shape=[f32(4, 4, rows, LANES), f32(3, ro...  1.01 us
  transfers between devices with their start and end apart: 4, of which 3 were waited for; matrix products, arithmetic and copies ran while one was open for 0% of the time, Pallas kernels for 11%

profile of v6, /device:TPU:30, one launch (start us, length us, event | category | flops | bytes accessed | tf_op | source)
XLA Modules:
  0.0 20.8 jit_solution(18195435618561293267)
XLA Ops:
  0.0 1.6 %overview.1 = (f32[24,128]{1,0:T(8,128)S(1)}, f32[32,128]{1,0:T(8,128)S(1)}, f32[128,1024]{1,0:T(8,128)S(1)}, s32[128,1024]{1,0:T(8,128)S(1)}, f32[8,128]{1,0:T(8,128)S(1)}) custom-call(s32[8]{0:T(128)} %tie_hbm.1, f32[128,1024]{1,0:T(8,128)} %el_hbm.1, s32[128,1024]{1,0:T(8,128)} %mk_hbm.1), custom_call_target="tpu_custom_call" | custom-call | tf_op jit(solution)/shard_map/overview/pallas_call | solution.py:488
  1.7 4.9 %collective-permute-start.1 = (f32[24,128]{1,0:T(8,128)S(1)}, f32[24,128]{1,0:T(8,128)S(1)}, u32[]{:S(2)}, u32[]{:S(2)}) collective-permute-start(f32[24,128]{1,0:T(8,128)S(1)} %get-tuple-element.19), channel_id=1, source_target_pairs={{0,16},{1,2},{2,1},{3,4},{4,3},{5,6},{6,5},{7,8},{8,7},{9,10},{10,... | collective-permute-start | bytes 36872 | tf_op jit(solution)/shard_map/ppermute | solution.py:471
  6.5 0.0 collective-permute-start
  6.5 1.3 %middle_fields.1 = (f32[4,4,128,128]{3,2,1,0:T(8,128)S(1)}, f32[6,128,128]{2,1,0:T(8,128)S(1)}) custom-call(f32[8,128]{1,0:T(8,128)S(1)} %get-tuple-element.17.coefs, f32[128,1024]{1,0:T(8,128)S(1)} %get-tuple-element.20.el), custom_call_target="tpu_custom_call" | custom-call | flops 10000000 | bytes 3000000 | tf_op jit(solution)/shard_map/middle_fields/pallas_call | solution.py:507
  7.9 0.4 %collective-permute-done.1.from_b = f32[24,128]{1,0:T(8,128)S(1)} collective-permute-done((f32[24,128]{1,0:T(8,128)S(1)}, f32[24,128]{1,0:T(8,128)S(1)}, u32[]{:S(2)}, u32[]{:S(2)}) %collective-permute-start.1) | collective-permute-done | bytes 12320 | tf_op jit(solution)/shard_map/ppermute | solution.py:471
  8.2 2.0 %collective-permute-done.from_a = f32[24,128]{1,0:T(8,128)S(1)} collective-permute-done((f32[24,128]{1,0:T(8,128)S(1)}, f32[24,128]{1,0:T(8,128)S(1)}, u32[]{:S(2)}, u32[]{:S(2)}) %collective-permute-start) | collective-permute-done | bytes 12320 | tf_op jit(solution)/shard_map/ppermute | solution.py:471
  10.2 0.2 far_message.1
  10.4 3.7 %collective-permute-start.3 = (f32[48,128]{1,0:T(8,128)S(1)}, f32[48,128]{1,0:T(8,128)S(1)}, u32[]{:S(2)}, u32[]{:S(2)}) collective-permute-start(f32[48,128]{1,0:T(8,128)S(1)} %get-tuple-element.25), channel_id=1, source_target_pairs={{0,1},{1,0},{2,3},{3,2},{4,5},{5,4},{6,7},{7,6},{8,9},{9,8},{10,11... | collective-permute-start | bytes 73736 | tf_op jit(solution)/shard_map/ppermute | solution.py:471
  14.1 1.0 %outer_fields.1 = (f32[4,4,128,128]{3,2,1,0:T(8,128)S(1)}, f32[3,128,128]{2,1,0:T(8,128)S(1)}) custom-call(f32[8,128]{1,0:T(8,128)S(1)} %get-tuple-element.17.coefs, f32[128,1024]{1,0:T(8,128)S(1)} %get-tuple-element.20.el, f32[128,128]{1,0:T(8,128)S(1)} %get-tuple-element.23.side, f32[6,128,128]{2,1,0:T(8,128)S(1)} %get-tuple-element.21.after.known.middle_recip), custom_call_target="tpu_custom_call" | custom-call | flops 10000000 | bytes 3000000 | tf_op jit(solution)/shard_map/outer_fields/pallas_call | solution.py:527
  15.1 0.1 near_message.1
  15.2 1.6 %collective-permute-start.2 = (f32[48,128]{1,0:T(8,128)S(1)}, f32[48,128]{1,0:T(8,128)S(1)}, u32[]{:S(2)}, u32[]{:S(2)}) collective-permute-start(f32[48,128]{1,0:T(8,128)S(1)} %near_message.1), channel_id=1, source_target_pairs={{0,16},{1,17},{2,18},{3,19},{4,20},{5,21},{6,22},{7,23},{8,24},{9,... | collective-permute-start | bytes 73736 | tf_op jit(solution)/shard_map/ppermute | solution.py:471
  16.8 1.8 %collective-permute-done.3.from_f = f32[48,128]{1,0:T(8,128)S(1)} collective-permute-done((f32[48,128]{1,0:T(8,128)S(1)}, f32[48,128]{1,0:T(8,128)S(1)}, u32[]{:S(2)}, u32[]{:S(2)}) %collective-permute-start.3) | collective-permute-done | bytes 24608 | tf_op jit(solution)/shard_map/ppermute | solution.py:471
  18.6 0.0 collective-permute-done.2.from_n
  18.6 2.1 %inflow.1 = f32[128,1024]{1,0:T(8,128)} custom-call(f32[8,128]{1,0:T(8,128)S(1)} %get-tuple-element.17.coefs, f32[64,128]{1,0:T(8,128)S(1)} %get-tuple-element.22.coarse, f32[48,128]{1,0:T(8,128)S(1)} %collective-permute-done.2.from_n, f32[48,128]{1,0:T(8,128)S(1)} %collective-permute-done.3.from_f, f32[128,1024]{1,0:T(8,128)S(1)} %get-tuple-element.20.el, ...), custom_call_target="tpu_custom_call" | custom-call | tf_op jit(solution)/shard_map/inflow/pallas_call | solution.py:546
Async XLA Ops:
  1.7 6.6 %collective-permute-start.1 = (f32[24,128]{1,0:T(8,128)S(1)}, f32[24,128]{1,0:T(8,128)S(1)}, u32[]{:S(2)}, u32[]{:S(2)}) collective-permute-start(f32[24,128]{1,0:T(8,128)S(1)} %get-tuple-element.19), channel_id=1, source_target_pairs={{0,16},{1,2},{2,1},{3,4},{4,3},{5,6},{6,5},{7,8},{8,7},{9,10},{10,... | collective-permute-start | bytes 36872 | tf_op jit(solution)/shard_map/ppermute | solution.py:471
  6.5 3.7 %collective-permute-start = (f32[24,128]{1,0:T(8,128)S(1)}, f32[24,128]{1,0:T(8,128)S(1)}, u32[]{:S(2)}, u32[]{:S(2)}) collective-permute-start(f32[24,128]{1,0:T(8,128)S(1)} %get-tuple-element.19), channel_id=1, source_target_pairs={{0,1},{1,0},{2,3},{3,2},{4,5},{5,4},{6,7},{7,6},{8,9},{9,8},{10,11... | collective-permute-start | bytes 36872 | tf_op jit(solution)/shard_map/ppermute | solution.py:471
  10.4 8.2 %collective-permute-start.3 = (f32[48,128]{1,0:T(8,128)S(1)}, f32[48,128]{1,0:T(8,128)S(1)}, u32[]{:S(2)}, u32[]{:S(2)}) collective-permute-start(f32[48,128]{1,0:T(8,128)S(1)} %get-tuple-element.25), channel_id=1, source_target_pairs={{0,1},{1,0},{2,3},{3,2},{4,5},{5,4},{6,7},{7,6},{8,9},{9,8},{10,11... | collective-permute-start | bytes 73736 | tf_op jit(solution)/shard_map/ppermute | solution.py:471
  15.2 3.5 %collective-permute-start.2 = (f32[48,128]{1,0:T(8,128)S(1)}, f32[48,128]{1,0:T(8,128)S(1)}, u32[]{:S(2)}, u32[]{:S(2)}) collective-permute-start(f32[48,128]{1,0:T(8,128)S(1)} %near_message.1), channel_id=1, source_target_pairs={{0,16},{1,17},{2,18},{3,19},{4,20},{5,21},{6,22},{7,23},{8,24},{9,... | collective-permute-start | bytes 73736 | tf_op jit(solution)/shard_map/ppermute | solution.py:471

commit v7 on v6

--- a/solution.py
+++ b/solution.py
@@ -103,7 +103,7 @@
 
 
 DEPTH = ITERS + 2
-PIECES = 4
+PIECES = 2
 PARTS = 4
 
 
@@ -113,14 +113,59 @@
     return jnp.where(outer, overview, pltpu.roll(runoff, LANES // 2, 1))
 
 
-def overview_kernel(tie_hbm, el_hbm, mk_hbm, msg, own, el, mk, coef, tie, tie_sem, el_sem, mk_sem):
+def chunk_sums(el, mk, lanes, rows):
+    s_groups, n_groups = [], []
+    for g in range(rows // 64):
+        at = [(slice(64 * g + 8 * t, 64 * g + 8 * t + 8), lanes) for t in range(8)]
+        flags = [mk[i].astype(jnp.float32) for i in at]
+        n_groups.append(block_rows(flags))
+        s_groups.append(block_rows([m * el[i] for m, i in zip(flags, at)]))
+    return jnp.concatenate(s_groups, axis=0), jnp.concatenate(n_groups, axis=0)
+
+
+def block_means(s, n, place):
+    k = s.shape[0]
+    pick = jnp.where(place == iota((s.shape[1], LANES), 1), 1.0, 0.0).astype(jnp.bfloat16)
+    hi = s.astype(jnp.bfloat16)
+    rest = s - hi.astype(jnp.float32)
+    mid = rest.astype(jnp.bfloat16)
+    low = (rest - mid.astype(jnp.float32)).astype(jnp.bfloat16)
+    left = jnp.concatenate([hi, mid, low, n.astype(jnp.bfloat16)], axis=0)
+    out = lax.dot_general(left, pick, (((1,), (0,)), ((), ())), preferred_element_type=jnp.float32)
+    summed = out[0:k] + (out[k : 2 * k] + out[2 * k : 3 * k])
+    count = out[3 * k : 4 * k]
+    return summed / (count + 1.0), count * (1.0 / 64.0)
+
+
+def column_message_kernel(el_hbm, mk_hbm, msg, el, mk, el_sem, mk_sem):
+    rows, cols = el_hbm.shape
+    k = rows // 8
+    fetch = []
+    for i, start in enumerate((0, cols - LANES)):
+        far, near = pl.ds(start, LANES), pl.ds(i * LANES, LANES)
+        fetch.append(pltpu.make_async_copy(el_hbm.at[:, far], el.at[:, near], el_sem.at[i]))
+        fetch.append(pltpu.make_async_copy(mk_hbm.at[:, far], mk.at[:, near], mk_sem.at[i]))
+    for copy in fetch:
+        copy.start()
+    for copy in fetch:
+        copy.wait()
+    first, last = slice(0, LANES), slice(LANES, 2 * LANES)
+    (s0, n0), (s1, n1) = chunk_sums(el, mk, first, rows), chunk_sums(el, mk, last, rows)
+    column = iota((2 * LANES, LANES), 0)
+    place = jnp.where(column < LANES, column // 8, LANES - 2 * LANES // 8 + column // 8)
+    overview, runoff = block_means(jnp.concatenate([s0, s1], axis=1), jnp.concatenate([n0, n1], axis=1), place)
+    msg[0:k, :] = edges(overview, runoff)
+    msg[k : k + 4, :] = jnp.transpose(el[:, first])[0:4]
+    msg[k + 4 : k + 8, :] = jnp.transpose(el[:, last])[LANES - 4 : LANES]
+
+
+def overview_kernel(tie_hbm, el_hbm, mk_hbm, after, own, el, mk, coef, tie, tie_sem, el_sem, mk_sem):
     rows, cols = el.shape
     chunks = cols // LANES
     k = rows // 8
     per = chunks // PIECES
-    pieces = [0, PIECES - 1, *range(1, PIECES - 1)]
     fetch = []
-    for p in pieces:
+    for p in range(PIECES):
         at = pl.ds(p * per * LANES, per * LANES)
         pair = (
             pltpu.make_async_copy(el_hbm.at[:, at], el.at[:, at], el_sem.at[p]),
@@ -131,40 +176,16 @@
         fetch.append(pair)
     tie_copy = pltpu.make_async_copy(tie_hbm, tie, tie_sem)
     tie_copy.start()
-    col = iota((cols, LANES), 0) // 8
-    pick = jnp.where(col == iota((cols, LANES), 1), 1.0, 0.0).astype(jnp.bfloat16)
     tie_copy.wait()
     coefficients(tie, coef)
-    sums, counts = {}, {}
-    for p, pair in zip(pieces, fetch):
+    parts = []
+    for p, pair in enumerate(fetch):
         for copy in pair:
             copy.wait()
         for j in range(p * per, (p + 1) * per):
-            lanes = slice(LANES * j, LANES * j + LANES)
-            s_groups, n_groups = [], []
-            for g in range(rows // 64):
-                at = [(slice(64 * g + 8 * t, 64 * g + 8 * t + 8), lanes) for t in range(8)]
-                flags = [mk[i].astype(jnp.float32) for i in at]
-                n_groups.append(block_rows(flags))
-                s_groups.append(block_rows([m * el[i] for m, i in zip(flags, at)]))
-            sums[j] = jnp.concatenate(s_groups, axis=0)
-            counts[j] = jnp.concatenate(n_groups, axis=0)
-            if j == 0:
-                msg[k : k + 4, :] = jnp.transpose(el[:, lanes])[0:4]
-            if j == chunks - 1:
-                msg[k + 4 : k + 8, :] = jnp.transpose(el[:, lanes])[LANES - 4 : LANES]
-    s = jnp.concatenate([sums[j] for j in range(chunks)], axis=1)
-    n = jnp.concatenate([counts[j] for j in range(chunks)], axis=1)
-    hi = s.astype(jnp.bfloat16)
-    rest = s - hi.astype(jnp.float32)
-    mid = rest.astype(jnp.bfloat16)
-    low = (rest - mid.astype(jnp.float32)).astype(jnp.bfloat16)
-    left = jnp.concatenate([hi, mid, low, n.astype(jnp.bfloat16)], axis=0)
-    out = lax.dot_general(left, pick, (((1,), (0,)), ((), ())), preferred_element_type=jnp.float32)
-    summed = out[0:k] + (out[k : 2 * k] + out[2 * k : 3 * k])
-    count = out[3 * k : 4 * k]
-    overview, runoff = summed / (count + 1.0), count * (1.0 / 64.0)
-    msg[0:k, :] = edges(overview, runoff)
+            parts.append(chunk_sums(el, mk, slice(LANES * j, LANES * j + LANES), rows))
+    s, n = (jnp.concatenate(x, axis=1) for x in zip(*parts))
+    overview, runoff = block_means(s, n, iota((cols, LANES), 0) // 8)
     own[0:k, :] = overview
     own[k : 2 * k, :] = runoff
 
@@ -485,25 +506,42 @@
     params = pltpu.CompilerParams(vmem_limit_bytes=LIMIT)
     dma = pltpu.SemaphoreType.DMA
     hbm = pl.BlockSpec(memory_space=pltpu.HBM)
-    msg, own, el, mk, coefs = pl.pallas_call(
+    tie_order, elevation, data_mask = (
+        pltpu.with_memory_space_constraint(x, pltpu.HBM) for x in (tie_order, elevation, data_mask)
+    )
+    msg = pl.pallas_call(
+        column_message_kernel,
+        out_shape=f32(k + 8, LANES),
+        in_specs=[hbm] * 2,
+        out_specs=whole(1)[0],
+        scratch_shapes=[
+            VMEM((rows, 2 * LANES), jnp.float32),
+            VMEM((rows, 2 * LANES), jnp.int32),
+            dma((2,)),
+            dma((2,)),
+        ],
+        compiler_params=params,
+        name="column_message",
+    )(elevation, data_mask)
+    from_b = swap(msg, "cols", True)
+    from_a = swap(msg, "cols", False)
+    cost = pl.CostEstimate(flops=10_000_000, bytes_accessed=3_000_000, transcendentals=0)
+    own, el, mk, coefs = pl.pallas_call(
         overview_kernel,
         out_shape=[
-            f32(k + 8, LANES),
             f32(2 * k, LANES),
             f32(rows, cols),
             jax.ShapeDtypeStruct((rows, cols), jnp.int32),
             f32(8, LANES),
         ],
-        in_specs=[hbm] * 3,
-        out_specs=whole(5),
+        in_specs=[hbm] * 3 + whole(1),
+        out_specs=whole(4),
         scratch_shapes=[pltpu.SMEM((8,), jnp.int32), dma, dma((PIECES,)), dma((PIECES,))],
         compiler_params=params,
+        cost_estimate=cost,
         name="overview",
-    )(*(pltpu.with_memory_space_constraint(x, pltpu.HBM) for x in (tie_order, elevation, data_mask)))
-    from_b = swap(msg, "cols", True)
-    from_a = swap(msg, "cols", False)
+    )(tie_order, elevation, data_mask, msg)
     plane = lambda count, height: VMEM((count, height, LANES), jnp.float32)
-    cost = pl.CostEstimate(flops=10_000_000, bytes_accessed=3_000_000, transcendentals=0)
     middle, middle_recip = pl.pallas_call(
         middle_kernel,
         out_shape=[f32(4, chunks - 4, rows, LANES), f32(chunks - 2, rows, LANES)],

time: 20.9 us -> 20.4 us (0.976)
  waiting for transfers between devices: 4.24 us -> 2.57 us
  Pallas kernels: 6.32 us -> 7.47 us
    ppermute x4, waiting for transfers between devices: 4.24 us -> 2.57 us  [swap(): return lax.ppermute(x, ('rows', 'cols'), pairs)]
    pallas_call x1 -> x2, Pallas kernels: 1.64 us -> 2.8 us  [the longest x1 1.53 us: on_device(): pl.pallas_call(overview_kernel, out_shape=[f32(2 * k, LANES), f32(rows, c...]
  transfers between devices with their start and end apart: 4 -> 4, of which waited for: 3 -> 2; matrix products, arithmetic and copies ran while one was open for 0% -> 0% of each run, Pallas kernels for 11% -> 19%
where the time goes in v7:
time: 20.4 us; the launch traced here: 20.3 us
  starting transfers between devices  10.2 us (50%)
  Pallas kernels  7.47 us (37%)
  waiting for transfers between devices  2.57 us (13%)
    ppermute x4, starting transfers between devices, swap(): return lax.ppermute(x, ('rows', 'cols'), pairs)  10.2 us
    ppermute x4, waiting for transfers between devices, swap(): return lax.ppermute(x, ('rows', 'cols'), pairs)  2.57 us
    pallas_call x1, Pallas kernels, on_device(): pl.pallas_call(inflow_kernel, out_shape=f32(rows, cols), in_specs=whole(1...  2.12 us
    pallas_call x1, Pallas kernels, on_device(): pl.pallas_call(overview_kernel, out_shape=[f32(2 * k, LANES), f32(rows, c...  1.53 us
    pallas_call x1, Pallas kernels, on_device(): pl.pallas_call(middle_kernel, out_shape=[f32(4, chunks - 4, rows, LANES),...  1.3 us
    pallas_call x1, Pallas kernels, on_device(): pl.pallas_call(column_message_kernel, out_shape=f32(k + 8, LANES), in_spe...  1.27 us
    pallas_call x1, Pallas kernels, on_device(): pl.pallas_call(outer_kernel, out_shape=[f32(4, 4, rows, LANES), f32(3, ro...  1.01 us
  transfers between devices with their start and end apart: 4, of which 2 were waited for; matrix products, arithmetic and copies ran while one was open for 0% of the time, Pallas kernels for 19%

profile of v7, /device:TPU:30, one launch (start us, length us, event | category | flops | bytes accessed | tf_op | source)
XLA Modules:
  0.0 20.3 jit_solution(9340731019450954187)
XLA Ops:
  0.0 1.3 %column_message.1.after = f32[24,128]{1,0:T(8,128)S(1)} custom-call(f32[128,1024]{1,0:T(8,128)} %el_hbm.3, s32[128,1024]{1,0:T(8,128)} %mk_hbm.3), custom_call_target="tpu_custom_call" | custom-call | tf_op jit(solution)/shard_map/column_message/pallas_call | solution.py:512
  1.3 4.9 %collective-permute-start.1 = (f32[24,128]{1,0:T(8,128)S(1)}, f32[24,128]{1,0:T(8,128)S(1)}, u32[]{:S(2)}, u32[]{:S(2)}) collective-permute-start(f32[24,128]{1,0:T(8,128)S(1)} %column_message.1.after), channel_id=1, source_target_pairs={{0,16},{1,2},{2,1},{3,4},{4,3},{5,6},{6,5},{7,8},{8,7},{9,10},{10,... | collective-permute-start | bytes 36872 | tf_op jit(solution)/shard_map/ppermute | solution.py:492
  6.2 0.0 collective-permute-start
  6.2 1.5 %overview.1 = (f32[32,128]{1,0:T(8,128)S(1)}, f32[128,1024]{1,0:T(8,128)S(1)}, s32[128,1024]{1,0:T(8,128)S(1)}, f32[8,128]{1,0:T(8,128)S(1)}) custom-call(s32[8]{0:T(128)} %tie_hbm.1, f32[128,1024]{1,0:T(8,128)} %el_hbm.3, s32[128,1024]{1,0:T(8,128)} %mk_hbm.3, f32[24,128]{1,0:T(8,128)S(1)} %column_message.1.after), custom_call_target="tpu_custom_call" | custom-call | flops 10000000 | bytes 3000000 | tf_op jit(solution)/shard_map/overview/pallas_call | solution.py:529
  7.7 1.3 %middle_fields.1 = (f32[4,4,128,128]{3,2,1,0:T(8,128)S(1)}, f32[6,128,128]{2,1,0:T(8,128)S(1)}) custom-call(f32[8,128]{1,0:T(8,128)S(1)} %get-tuple-element.16.coefs, f32[128,1024]{1,0:T(8,128)S(1)} %get-tuple-element.18.el), custom_call_target="tpu_custom_call" | custom-call | flops 10000000 | bytes 3000000 | tf_op jit(solution)/shard_map/middle_fields/pallas_call | solution.py:545
  9.0 0.0 collective-permute-done.1.from_b
  9.0 0.8 %collective-permute-done.from_a = f32[24,128]{1,0:T(8,128)S(1)} collective-permute-done((f32[24,128]{1,0:T(8,128)S(1)}, f32[24,128]{1,0:T(8,128)S(1)}, u32[]{:S(2)}, u32[]{:S(2)}) %collective-permute-start) | collective-permute-done | bytes 12320 | tf_op jit(solution)/shard_map/ppermute | solution.py:492
  9.9 0.2 far_message.1
  10.0 3.7 %collective-permute-start.3 = (f32[48,128]{1,0:T(8,128)S(1)}, f32[48,128]{1,0:T(8,128)S(1)}, u32[]{:S(2)}, u32[]{:S(2)}) collective-permute-start(f32[48,128]{1,0:T(8,128)S(1)} %get-tuple-element.23), channel_id=1, source_target_pairs={{0,1},{1,0},{2,3},{3,2},{4,5},{5,4},{6,7},{7,6},{8,9},{9,8},{10,11... | collective-permute-start | bytes 73736 | tf_op jit(solution)/shard_map/ppermute | solution.py:492
  13.7 1.0 %outer_fields.1 = (f32[4,4,128,128]{3,2,1,0:T(8,128)S(1)}, f32[3,128,128]{2,1,0:T(8,128)S(1)}) custom-call(f32[8,128]{1,0:T(8,128)S(1)} %get-tuple-element.16.coefs, f32[128,1024]{1,0:T(8,128)S(1)} %get-tuple-element.18.el, f32[128,128]{1,0:T(8,128)S(1)} %get-tuple-element.21.side, f32[6,128,128]{2,1,0:T(8,128)S(1)} %get-tuple-element.19.after.known.middle_recip), custom_call_target="tpu_custom_call" | custom-call | flops 10000000 | bytes 3000000 | tf_op jit(solution)/shard_map/outer_fields/pallas_call | solution.py:565
  14.7 0.1 near_message.1
  14.8 1.6 %collective-permute-start.2 = (f32[48,128]{1,0:T(8,128)S(1)}, f32[48,128]{1,0:T(8,128)S(1)}, u32[]{:S(2)}, u32[]{:S(2)}) collective-permute-start(f32[48,128]{1,0:T(8,128)S(1)} %near_message.1), channel_id=1, source_target_pairs={{0,16},{1,17},{2,18},{3,19},{4,20},{5,21},{6,22},{7,23},{8,24},{9,... | collective-permute-start | bytes 73736 | tf_op jit(solution)/shard_map/ppermute | solution.py:492
  16.4 1.7 %collective-permute-done.3.from_f = f32[48,128]{1,0:T(8,128)S(1)} collective-permute-done((f32[48,128]{1,0:T(8,128)S(1)}, f32[48,128]{1,0:T(8,128)S(1)}, u32[]{:S(2)}, u32[]{:S(2)}) %collective-permute-start.3) | collective-permute-done | bytes 24608 | tf_op jit(solution)/shard_map/ppermute | solution.py:492
  18.1 0.0 collective-permute-done.2.from_n
  18.1 2.1 %inflow.1 = f32[128,1024]{1,0:T(8,128)} custom-call(f32[8,128]{1,0:T(8,128)S(1)} %get-tuple-element.16.coefs, f32[64,128]{1,0:T(8,128)S(1)} %get-tuple-element.20.coarse, f32[48,128]{1,0:T(8,128)S(1)} %collective-permute-done.2.from_n, f32[48,128]{1,0:T(8,128)S(1)} %collective-permute-done.3.from_f, f32[128,1024]{1,0:T(8,128)S(1)} %get-tuple-element.18.el, ...), custom_call_target="tpu_custom_call" | custom-call | tf_op jit(solution)/shard_map/inflow/pallas_call | solution.py:584
Async XLA Ops:
  1.3 7.7 %collective-permute-start.1 = (f32[24,128]{1,0:T(8,128)S(1)}, f32[24,128]{1,0:T(8,128)S(1)}, u32[]{:S(2)}, u32[]{:S(2)}) collective-permute-start(f32[24,128]{1,0:T(8,128)S(1)} %column_message.1.after), channel_id=1, source_target_pairs={{0,16},{1,2},{2,1},{3,4},{4,3},{5,6},{6,5},{7,8},{8,7},{9,10},{10,... | collective-permute-start | bytes 36872 | tf_op jit(solution)/shard_map/ppermute | solution.py:492
  6.2 3.7 %collective-permute-start = (f32[24,128]{1,0:T(8,128)S(1)}, f32[24,128]{1,0:T(8,128)S(1)}, u32[]{:S(2)}, u32[]{:S(2)}) collective-permute-start(f32[24,128]{1,0:T(8,128)S(1)} %column_message.1.after), channel_id=1, source_target_pairs={{0,1},{1,0},{2,3},{3,2},{4,5},{5,4},{6,7},{7,6},{8,9},{9,8},{10,11... | collective-permute-start | bytes 36872 | tf_op jit(solution)/shard_map/ppermute | solution.py:492
  10.0 8.1 %collective-permute-start.3 = (f32[48,128]{1,0:T(8,128)S(1)}, f32[48,128]{1,0:T(8,128)S(1)}, u32[]{:S(2)}, u32[]{:S(2)}) collective-permute-start(f32[48,128]{1,0:T(8,128)S(1)} %get-tuple-element.23), channel_id=1, source_target_pairs={{0,1},{1,0},{2,3},{3,2},{4,5},{5,4},{6,7},{7,6},{8,9},{9,8},{10,11... | collective-permute-start | bytes 73736 | tf_op jit(solution)/shard_map/ppermute | solution.py:492
  14.8 3.3 %collective-permute-start.2 = (f32[48,128]{1,0:T(8,128)S(1)}, f32[48,128]{1,0:T(8,128)S(1)}, u32[]{:S(2)}, u32[]{:S(2)}) collective-permute-start(f32[48,128]{1,0:T(8,128)S(1)} %near_message.1), channel_id=1, source_target_pairs={{0,16},{1,17},{2,18},{3,19},{4,20},{5,21},{6,22},{7,23},{8,24},{9,... | collective-permute-start | bytes 73736 | tf_op jit(solution)/shard_map/ppermute | solution.py:492

commit v8 on v7

--- a/solution.py
+++ b/solution.py
@@ -190,7 +190,7 @@
     own[k : 2 * k, :] = runoff
 
 
-def row_message_kernel(own, from_a, from_b, el, after, coarse, side, to_f):
+def row_message_kernel(own, from_a, from_b, el, coarse, side, to_f):
     k = own.shape[0] // 2
     r, c = lax.axis_index("rows"), lax.axis_index("cols")
     count = lax.axis_size("cols")
@@ -249,7 +249,7 @@
     message((over, run, edges(near, near_run)), side[...], el, lax.axis_index("rows") % 2 == 0, to_n)
 
 
-def middle_kernel(coefs, el, out, recip, zc, zw, ze, rc, rw, re):
+def middle_kernel(coefs, el, after, out, recip, zc, zw, ze, rc, rw, re):
     rows, cols = el.shape
     chunks = cols // LANES
     coef = coefficient_tiles(coefs)
@@ -542,26 +542,35 @@
         name="overview",
     )(tie_order, elevation, data_mask, msg)
     plane = lambda count, height: VMEM((count, height, LANES), jnp.float32)
+    size = (3 * DEPTH + 2 * chunks + 7) // 8 * 8
+    coarse, side, to_f = pl.pallas_call(
+        row_message_kernel,
+        out_shape=[f32(4 * k, LANES), f32(rows, LANES), f32(size, LANES)],
+        in_specs=whole(4),
+        out_specs=whole(3),
+        compiler_params=params,
+        name="far_message",
+    )(own, from_a, from_b, el)
+    from_f = swap(to_f, "rows", True)
     middle, middle_recip = pl.pallas_call(
         middle_kernel,
         out_shape=[f32(4, chunks - 4, rows, LANES), f32(chunks - 2, rows, LANES)],
-        in_specs=whole(2),
+        in_specs=whole(3),
         out_specs=whole(2),
         scratch_shapes=[plane(chunks, rows + 16)] * 6,
         compiler_params=params,
         cost_estimate=cost,
         name="middle_fields",
-    )(coefs, el)
-    size = (3 * DEPTH + 2 * chunks + 7) // 8 * 8
-    coarse, side, to_f = pl.pallas_call(
-        row_message_kernel,
-        out_shape=[f32(4 * k, LANES), f32(rows, LANES), f32(size, LANES)],
-        in_specs=whole(5),
-        out_specs=whole(3),
+    )(coefs, el, to_f)
+    to_n = pl.pallas_call(
+        near_message_kernel,
+        out_shape=f32(size, LANES),
+        in_specs=whole(4),
+        out_specs=whole(1)[0],
         compiler_params=params,
-        name="far_message",
-    )(own, from_a, from_b, el, middle_recip)
-    from_f = swap(to_f, "rows", True)
+        name="near_message",
+    )(coarse, side, el, middle_recip)
+    from_n = swap(to_n, "rows", False)
     outer, outer_recip = pl.pallas_call(
         outer_kernel,
         out_shape=[f32(4, 4, rows, LANES), f32(3, rows, LANES)],
@@ -572,15 +581,6 @@
         cost_estimate=cost,
         name="outer_fields",
     )(coefs, el, side, middle_recip)
-    to_n = pl.pallas_call(
-        near_message_kernel,
-        out_shape=f32(size, LANES),
-        in_specs=whole(4),
-        out_specs=whole(1)[0],
-        compiler_params=params,
-        name="near_message",
-    )(coarse, side, el, outer_recip)
-    from_n = swap(to_n, "rows", False)
     return pl.pallas_call(
         inflow_kernel,
         out_shape=f32(rows, cols),

time: 20.4 us -> 20.5 us (level)
  transfers between devices with their start and end apart: 4 -> 4, of which waited for: 2 -> 3; matrix products, arithmetic and copies ran while one was open for 0% -> 0% of each run, Pallas kernels for 19% -> 19%
where the time goes in v8:
time: 20.5 us; the launch traced here: 20.4 us
  starting transfers between devices  10.2 us (50%)
  Pallas kernels  7.5 us (37%)
  waiting for transfers between devices  2.68 us (13%)
    ppermute x4, starting transfers between devices, swap(): return lax.ppermute(x, ('rows', 'cols'), pairs)  10.2 us
    ppermute x4, waiting for transfers between devices, swap(): return lax.ppermute(x, ('rows', 'cols'), pairs)  2.68 us
    pallas_call x1, Pallas kernels, on_device(): pl.pallas_call(inflow_kernel, out_shape=f32(rows, cols), in_specs=whole(1...  2.12 us
    pallas_call x1, Pallas kernels, on_device(): pl.pallas_call(overview_kernel, out_shape=[f32(2 * k, LANES), f32(rows, c...  1.53 us
    pallas_call x1, Pallas kernels, on_device(): pl.pallas_call(middle_kernel, out_shape=[f32(4, chunks - 4, rows, LANES),...  1.31 us
    pallas_call x1, Pallas kernels, on_device(): pl.pallas_call(column_message_kernel, out_shape=f32(k + 8, LANES), in_spe...  1.27 us
    pallas_call x1, Pallas kernels, on_device(): pl.pallas_call(outer_kernel, out_shape=[f32(4, 4, rows, LANES), f32(3, ro...  1.02 us
  transfers between devices with their start and end apart: 4, of which 3 were waited for; matrix products, arithmetic and copies ran while one was open for 0% of the time, Pallas kernels for 19%

profile of v8, /device:TPU:30, one launch (start us, length us, event | category | flops | bytes accessed | tf_op | source)
XLA Modules:
  0.0 20.4 jit_solution(13052081115447425136)
XLA Ops:
  0.0 1.3 %column_message.1.after = f32[24,128]{1,0:T(8,128)S(1)} custom-call(f32[128,1024]{1,0:T(8,128)} %el_hbm.3, s32[128,1024]{1,0:T(8,128)} %mk_hbm.3), custom_call_target="tpu_custom_call" | custom-call | tf_op jit(solution)/shard_map/column_message/pallas_call | solution.py:512
  1.3 4.9 %collective-permute-start.1 = (f32[24,128]{1,0:T(8,128)S(1)}, f32[24,128]{1,0:T(8,128)S(1)}, u32[]{:S(2)}, u32[]{:S(2)}) collective-permute-start(f32[24,128]{1,0:T(8,128)S(1)} %column_message.1.after), channel_id=1, source_target_pairs={{0,16},{1,2},{2,1},{3,4},{4,3},{5,6},{6,5},{7,8},{8,7},{9,10},{10,... | collective-permute-start | bytes 36872 | tf_op jit(solution)/shard_map/ppermute | solution.py:492
  6.2 0.0 collective-permute-start
  6.2 1.5 %overview.1 = (f32[32,128]{1,0:T(8,128)S(1)}, f32[128,1024]{1,0:T(8,128)S(1)}, s32[128,1024]{1,0:T(8,128)S(1)}, f32[8,128]{1,0:T(8,128)S(1)}) custom-call(s32[8]{0:T(128)} %tie_hbm.1, f32[128,1024]{1,0:T(8,128)} %el_hbm.3, s32[128,1024]{1,0:T(8,128)} %mk_hbm.3, f32[24,128]{1,0:T(8,128)S(1)} %column_message.1.after), custom_call_target="tpu_custom_call" | custom-call | flops 10000000 | bytes 3000000 | tf_op jit(solution)/shard_map/overview/pallas_call | solution.py:529
  7.7 0.1 collective-permute-done.1.from_b
  7.8 2.0 %collective-permute-done.from_a = f32[24,128]{1,0:T(8,128)S(1)} collective-permute-done((f32[24,128]{1,0:T(8,128)S(1)}, f32[24,128]{1,0:T(8,128)S(1)}, u32[]{:S(2)}, u32[]{:S(2)}) %collective-permute-start) | collective-permute-done | bytes 12320 | tf_op jit(solution)/shard_map/ppermute | solution.py:492
  9.9 0.2 far_message.1
  10.0 3.7 %collective-permute-start.3 = (f32[48,128]{1,0:T(8,128)S(1)}, f32[48,128]{1,0:T(8,128)S(1)}, u32[]{:S(2)}, u32[]{:S(2)}) collective-permute-start(f32[48,128]{1,0:T(8,128)S(1)} %get-tuple-element.21.after), channel_id=1, source_target_pairs={{0,1},{1,0},{2,3},{3,2},{4,5},{5,4},{6,7},{7,6},{8,9},{9,8},{10,11... | collective-permute-start | bytes 73736 | tf_op jit(solution)/shard_map/ppermute | solution.py:492
  13.7 1.3 %middle_fields.1 = (f32[4,4,128,128]{3,2,1,0:T(8,128)S(1)}, f32[6,128,128]{2,1,0:T(8,128)S(1)}) custom-call(f32[8,128]{1,0:T(8,128)S(1)} %get-tuple-element.16.coefs, f32[128,1024]{1,0:T(8,128)S(1)} %get-tuple-element.18.el, f32[48,128]{1,0:T(8,128)S(1)} %get-tuple-element.21.after), custom_call_target="tpu_custom_call" | custom-call | flops 10000000 | bytes 3000000 | tf_op jit(solution)/shard_map/middle_fields/pallas_call | solution.py:555
  15.0 0.1 near_message.1
  15.1 1.6 %collective-permute-start.2 = (f32[48,128]{1,0:T(8,128)S(1)}, f32[48,128]{1,0:T(8,128)S(1)}, u32[]{:S(2)}, u32[]{:S(2)}) collective-permute-start(f32[48,128]{1,0:T(8,128)S(1)} %near_message.1), channel_id=1, source_target_pairs={{0,16},{1,17},{2,18},{3,19},{4,20},{5,21},{6,22},{7,23},{8,24},{9,... | collective-permute-start | bytes 73736 | tf_op jit(solution)/shard_map/ppermute | solution.py:492
  16.7 1.0 %outer_fields.1 = (f32[4,4,128,128]{3,2,1,0:T(8,128)S(1)}, f32[3,128,128]{2,1,0:T(8,128)S(1)}) custom-call(f32[8,128]{1,0:T(8,128)S(1)} %get-tuple-element.16.coefs, f32[128,1024]{1,0:T(8,128)S(1)} %get-tuple-element.18.el, f32[128,128]{1,0:T(8,128)S(1)} %get-tuple-element.20.side, f32[6,128,128]{2,1,0:T(8,128)S(1)} %get-tuple-element.22.after.known.middle_recip), custom_call_target="tpu_custom_call" | custom-call | flops 10000000 | bytes 3000000 | tf_op jit(solution)/shard_map/outer_fields/pallas_call | solution.py:574
  17.7 0.5 %collective-permute-done.3.from_f = f32[48,128]{1,0:T(8,128)S(1)} collective-permute-done((f32[48,128]{1,0:T(8,128)S(1)}, f32[48,128]{1,0:T(8,128)S(1)}, u32[]{:S(2)}, u32[]{:S(2)}) %collective-permute-start.3) | collective-permute-done | bytes 24608 | tf_op jit(solution)/shard_map/ppermute | solution.py:492
  18.3 0.0 collective-permute-done.2.from_n
  18.3 2.1 %inflow.1 = f32[128,1024]{1,0:T(8,128)} custom-call(f32[8,128]{1,0:T(8,128)S(1)} %get-tuple-element.16.coefs, f32[64,128]{1,0:T(8,128)S(1)} %get-tuple-element.19.coarse, f32[48,128]{1,0:T(8,128)S(1)} %collective-permute-done.2.from_n, f32[48,128]{1,0:T(8,128)S(1)} %collective-permute-done.3.from_f, f32[128,1024]{1,0:T(8,128)S(1)} %get-tuple-element.18.el, ...), custom_call_target="tpu_custom_call" | custom-call | tf_op jit(solution)/shard_map/inflow/pallas_call | solution.py:584
Async XLA Ops:
  1.3 6.6 %collective-permute-start.1 = (f32[24,128]{1,0:T(8,128)S(1)}, f32[24,128]{1,0:T(8,128)S(1)}, u32[]{:S(2)}, u32[]{:S(2)}) collective-permute-start(f32[24,128]{1,0:T(8,128)S(1)} %column_message.1.after), channel_id=1, source_target_pairs={{0,16},{1,2},{2,1},{3,4},{4,3},{5,6},{6,5},{7,8},{8,7},{9,10},{10,... | collective-permute-start | bytes 36872 | tf_op jit(solution)/shard_map/ppermute | solution.py:492
  6.2 3.7 %collective-permute-start = (f32[24,128]{1,0:T(8,128)S(1)}, f32[24,128]{1,0:T(8,128)S(1)}, u32[]{:S(2)}, u32[]{:S(2)}) collective-permute-start(f32[24,128]{1,0:T(8,128)S(1)} %column_message.1.after), channel_id=1, source_target_pairs={{0,1},{1,0},{2,3},{3,2},{4,5},{5,4},{6,7},{7,6},{8,9},{9,8},{10,11... | collective-permute-start | bytes 36872 | tf_op jit(solution)/shard_map/ppermute | solution.py:492
  10.0 8.2 %collective-permute-start.3 = (f32[48,128]{1,0:T(8,128)S(1)}, f32[48,128]{1,0:T(8,128)S(1)}, u32[]{:S(2)}, u32[]{:S(2)}) collective-permute-start(f32[48,128]{1,0:T(8,128)S(1)} %get-tuple-element.21.after), channel_id=1, source_target_pairs={{0,1},{1,0},{2,3},{3,2},{4,5},{5,4},{6,7},{7,6},{8,9},{9,8},{10,11... | collective-permute-start | bytes 73736 | tf_op jit(solution)/shard_map/ppermute | solution.py:492
  15.1 3.1 %collective-permute-start.2 = (f32[48,128]{1,0:T(8,128)S(1)}, f32[48,128]{1,0:T(8,128)S(1)}, u32[]{:S(2)}, u32[]{:S(2)}) collective-permute-start(f32[48,128]{1,0:T(8,128)S(1)} %near_message.1), channel_id=1, source_target_pairs={{0,16},{1,17},{2,18},{3,19},{4,20},{5,21},{6,22},{7,23},{8,24},{9,... | collective-permute-start | bytes 73736 | tf_op jit(solution)/shard_map/ppermute | solution.py:492

commit v9 on v7

--- a/solution.py
+++ b/solution.py
@@ -399,8 +399,7 @@
     for row in (0, 8, 16):
         spread(r_planes, every, row, ring)
     border = {}
-    for j in range(chunks):
-        border[j] = fields((zc.at[:, 16:40, :], zw.at[:, 16:40, :], ze.at[:, 16:40, :]), r_planes, j, 8, coef, 1, 6)
+    lifted = (zc.at[:, 16:40, :], zw.at[:, 16:40, :], ze.at[:, 16:40, :])
 
     for j in range(2):
         for t in range(3 * k // 8):
@@ -415,6 +414,8 @@
                     (parts[4] + parts[5]) + (parts[6] + parts[7])
                 )
                 flow[j, 8 * t : 8 * t + 8, :] = run[j, 8 * t : 8 * t + 8, :] + total
+        for j in range(sweep, chunks, ITERS):
+            border[j] = fields(lifted, r_planes, j, 8, coef, 1, 6)
         if sweep < ITERS - 1:
             for j in range(2):
                 for t in inner:

time: 20.4 us -> 20.4 us (level)
  no operation moved by 1% of the time
where the time goes in v9:
time: 20.4 us; the launch traced here: 20.3 us
  starting transfers between devices  10.2 us (50%)
  Pallas kernels  7.47 us (37%)
  waiting for transfers between devices  2.57 us (13%)
    ppermute x4, starting transfers between devices, swap(): return lax.ppermute(x, ('rows', 'cols'), pairs)  10.2 us
    ppermute x4, waiting for transfers between devices, swap(): return lax.ppermute(x, ('rows', 'cols'), pairs)  2.57 us
    pallas_call x1, Pallas kernels, on_device(): pl.pallas_call(inflow_kernel, out_shape=f32(rows, cols), in_specs=whole(1...  2.12 us
    pallas_call x1, Pallas kernels, on_device(): pl.pallas_call(overview_kernel, out_shape=[f32(2 * k, LANES), f32(rows, c...  1.53 us
    pallas_call x1, Pallas kernels, on_device(): pl.pallas_call(middle_kernel, out_shape=[f32(4, chunks - 4, rows, LANES),...  1.3 us
    pallas_call x1, Pallas kernels, on_device(): pl.pallas_call(column_message_kernel, out_shape=f32(k + 8, LANES), in_spe...  1.27 us
    pallas_call x1, Pallas kernels, on_device(): pl.pallas_call(outer_kernel, out_shape=[f32(4, 4, rows, LANES), f32(3, ro...  1.01 us
  transfers between devices with their start and end apart: 4, of which 2 were waited for; matrix products, arithmetic and copies ran while one was open for 0% of the time, Pallas kernels for 19%

profile of v9, /device:TPU:30, one launch (start us, length us, event | category | flops | bytes accessed | tf_op | source)
XLA Modules:
  0.0 20.3 jit_solution(9340731019450954187)
XLA Ops:
  0.0 1.3 %column_message.1.after = f32[24,128]{1,0:T(8,128)S(1)} custom-call(f32[128,1024]{1,0:T(8,128)} %el_hbm.3, s32[128,1024]{1,0:T(8,128)} %mk_hbm.3), custom_call_target="tpu_custom_call" | custom-call | tf_op jit(solution)/shard_map/column_message/pallas_call | solution.py:513
  1.3 4.9 %collective-permute-start.1 = (f32[24,128]{1,0:T(8,128)S(1)}, f32[24,128]{1,0:T(8,128)S(1)}, u32[]{:S(2)}, u32[]{:S(2)}) collective-permute-start(f32[24,128]{1,0:T(8,128)S(1)} %column_message.1.after), channel_id=1, source_target_pairs={{0,16},{1,2},{2,1},{3,4},{4,3},{5,6},{6,5},{7,8},{8,7},{9,10},{10,... | collective-permute-start | bytes 36872 | tf_op jit(solution)/shard_map/ppermute | solution.py:493
  6.2 0.0 collective-permute-start
  6.2 1.5 %overview.1 = (f32[32,128]{1,0:T(8,128)S(1)}, f32[128,1024]{1,0:T(8,128)S(1)}, s32[128,1024]{1,0:T(8,128)S(1)}, f32[8,128]{1,0:T(8,128)S(1)}) custom-call(s32[8]{0:T(128)} %tie_hbm.1, f32[128,1024]{1,0:T(8,128)} %el_hbm.3, s32[128,1024]{1,0:T(8,128)} %mk_hbm.3, f32[24,128]{1,0:T(8,128)S(1)} %column_message.1.after), custom_call_target="tpu_custom_call" | custom-call | flops 10000000 | bytes 3000000 | tf_op jit(solution)/shard_map/overview/pallas_call | solution.py:530
  7.7 1.3 %middle_fields.1 = (f32[4,4,128,128]{3,2,1,0:T(8,128)S(1)}, f32[6,128,128]{2,1,0:T(8,128)S(1)}) custom-call(f32[8,128]{1,0:T(8,128)S(1)} %get-tuple-element.16.coefs, f32[128,1024]{1,0:T(8,128)S(1)} %get-tuple-element.18.el), custom_call_target="tpu_custom_call" | custom-call | flops 10000000 | bytes 3000000 | tf_op jit(solution)/shard_map/middle_fields/pallas_call | solution.py:546
  9.0 0.0 collective-permute-done.1.from_b
  9.0 0.8 %collective-permute-done.from_a = f32[24,128]{1,0:T(8,128)S(1)} collective-permute-done((f32[24,128]{1,0:T(8,128)S(1)}, f32[24,128]{1,0:T(8,128)S(1)}, u32[]{:S(2)}, u32[]{:S(2)}) %collective-permute-start) | collective-permute-done | bytes 12320 | tf_op jit(solution)/shard_map/ppermute | solution.py:493
  9.9 0.2 far_message.1
  10.0 3.7 %collective-permute-start.3 = (f32[48,128]{1,0:T(8,128)S(1)}, f32[48,128]{1,0:T(8,128)S(1)}, u32[]{:S(2)}, u32[]{:S(2)}) collective-permute-start(f32[48,128]{1,0:T(8,128)S(1)} %get-tuple-element.23), channel_id=1, source_target_pairs={{0,1},{1,0},{2,3},{3,2},{4,5},{5,4},{6,7},{7,6},{8,9},{9,8},{10,11... | collective-permute-start | bytes 73736 | tf_op jit(solution)/shard_map/ppermute | solution.py:493
  13.7 1.0 %outer_fields.1 = (f32[4,4,128,128]{3,2,1,0:T(8,128)S(1)}, f32[3,128,128]{2,1,0:T(8,128)S(1)}) custom-call(f32[8,128]{1,0:T(8,128)S(1)} %get-tuple-element.16.coefs, f32[128,1024]{1,0:T(8,128)S(1)} %get-tuple-element.18.el, f32[128,128]{1,0:T(8,128)S(1)} %get-tuple-element.21.side, f32[6,128,128]{2,1,0:T(8,128)S(1)} %get-tuple-element.19.after.known.middle_recip), custom_call_target="tpu_custom_call" | custom-call | flops 10000000 | bytes 3000000 | tf_op jit(solution)/shard_map/outer_fields/pallas_call | solution.py:566
  14.7 0.1 near_message.1
  14.8 1.6 %collective-permute-start.2 = (f32[48,128]{1,0:T(8,128)S(1)}, f32[48,128]{1,0:T(8,128)S(1)}, u32[]{:S(2)}, u32[]{:S(2)}) collective-permute-start(f32[48,128]{1,0:T(8,128)S(1)} %near_message.1), channel_id=1, source_target_pairs={{0,16},{1,17},{2,18},{3,19},{4,20},{5,21},{6,22},{7,23},{8,24},{9,... | collective-permute-start | bytes 73736 | tf_op jit(solution)/shard_map/ppermute | solution.py:493
  16.4 1.7 %collective-permute-done.3.from_f = f32[48,128]{1,0:T(8,128)S(1)} collective-permute-done((f32[48,128]{1,0:T(8,128)S(1)}, f32[48,128]{1,0:T(8,128)S(1)}, u32[]{:S(2)}, u32[]{:S(2)}) %collective-permute-start.3) | collective-permute-done | bytes 24608 | tf_op jit(solution)/shard_map/ppermute | solution.py:493
  18.1 0.0 collective-permute-done.2.from_n
  18.1 2.1 %inflow.1 = f32[128,1024]{1,0:T(8,128)} custom-call(f32[8,128]{1,0:T(8,128)S(1)} %get-tuple-element.16.coefs, f32[64,128]{1,0:T(8,128)S(1)} %get-tuple-element.20.coarse, f32[48,128]{1,0:T(8,128)S(1)} %collective-permute-done.2.from_n, f32[48,128]{1,0:T(8,128)S(1)} %collective-permute-done.3.from_f, f32[128,1024]{1,0:T(8,128)S(1)} %get-tuple-element.18.el, ...), custom_call_target="tpu_custom_call" | custom-call | tf_op jit(solution)/shard_map/inflow/pallas_call | solution.py:585
Async XLA Ops:
  1.3 7.7 %collective-permute-start.1 = (f32[24,128]{1,0:T(8,128)S(1)}, f32[24,128]{1,0:T(8,128)S(1)}, u32[]{:S(2)}, u32[]{:S(2)}) collective-permute-start(f32[24,128]{1,0:T(8,128)S(1)} %column_message.1.after), channel_id=1, source_target_pairs={{0,16},{1,2},{2,1},{3,4},{4,3},{5,6},{6,5},{7,8},{8,7},{9,10},{10,... | collective-permute-start | bytes 36872 | tf_op jit(solution)/shard_map/ppermute | solution.py:493
  6.2 3.7 %collective-permute-start = (f32[24,128]{1,0:T(8,128)S(1)}, f32[24,128]{1,0:T(8,128)S(1)}, u32[]{:S(2)}, u32[]{:S(2)}) collective-permute-start(f32[24,128]{1,0:T(8,128)S(1)} %column_message.1.after), channel_id=1, source_target_pairs={{0,1},{1,0},{2,3},{3,2},{4,5},{5,4},{6,7},{7,6},{8,9},{9,8},{10,11... | collective-permute-start | bytes 36872 | tf_op jit(solution)/shard_map/ppermute | solution.py:493
  10.0 8.1 %collective-permute-start.3 = (f32[48,128]{1,0:T(8,128)S(1)}, f32[48,128]{1,0:T(8,128)S(1)}, u32[]{:S(2)}, u32[]{:S(2)}) collective-permute-start(f32[48,128]{1,0:T(8,128)S(1)} %get-tuple-element.23), channel_id=1, source_target_pairs={{0,1},{1,0},{2,3},{3,2},{4,5},{5,4},{6,7},{7,6},{8,9},{9,8},{10,11... | collective-permute-start | bytes 73736 | tf_op jit(solution)/shard_map/ppermute | solution.py:493
  14.8 3.3 %collective-permute-start.2 = (f32[48,128]{1,0:T(8,128)S(1)}, f32[48,128]{1,0:T(8,128)S(1)}, u32[]{:S(2)}, u32[]{:S(2)}) collective-permute-start(f32[48,128]{1,0:T(8,128)S(1)} %near_message.1), channel_id=1, source_target_pairs={{0,16},{1,17},{2,18},{3,19},{4,20},{5,21},{6,22},{7,23},{8,24},{9,... | collective-permute-start | bytes 73736 | tf_op jit(solution)/shard_map/ppermute | solution.py:493
